TPU v7x, 32 devices: a whole 2x2x4 slice. The times are simulated.
32 devices in a mesh: ctx: 8 (over z, y), wsh: 4 (over x, core).
Axes of the slice: x: 2, y: 2, z: 4, core: 2. Of those that a mesh axis runs over, the one named last changes fastest.
Arguments:
- inputs: bfloat16 [8, 2, 1024, 960], P('wsh', None, 'ctx'), may hold values from -6 to 6
- norm1_gain: bfloat16 [960], P('wsh'), may hold values from 0.25 to 1.75
- q_weight: bfloat16 [960, 960], P('wsh'), may hold values from -0.1875 to 0.1875
- k_weight: bfloat16 [960, 320], P('wsh'), may hold values from -0.1875 to 0.1875
- v_weight: bfloat16 [960, 320], P('wsh'), may hold values from -0.1875 to 0.1875
- o_weight: bfloat16 [960, 960], P('wsh'), may hold values from -1 to 1
- norm2_gain: bfloat16 [960], P('wsh'), may hold values from 0.25 to 1.75
- gate_weight: bfloat16 [960, 2560], P('wsh'), may hold values from -0.1875 to 0.1875
- up_weight: bfloat16 [960, 2560], P('wsh'), may hold values from -0.1875 to 0.1875
- down_weight: bfloat16 [2560, 960], P('wsh'), may hold values from -0.125 to 0.125
- cotangent: bfloat16 [8, 2, 1024, 960], P('wsh', None, 'ctx'), may hold values from -6 to 6
Outputs:
- output: bfloat16 [8, 2, 1024, 960], P('wsh', None, 'ctx')
- input_grad: float32 [8, 2, 1024, 960], P('wsh', None, 'ctx')
- norm1_gain_grad: float32 [960], P('wsh')
- q_weight_grad: float32 [960, 960], P('wsh')
- k_weight_grad: float32 [960, 320], P('wsh')
- v_weight_grad: float32 [960, 320], P('wsh')
- o_weight_grad: float32 [960, 960], P('wsh')
- norm2_gain_grad: float32 [960], P('wsh')
- gate_weight_grad: float32 [960, 2560], P('wsh')
- up_weight_grad: float32 [960, 2560], P('wsh')
- down_weight_grad: float32 [2560, 960], P('wsh')
All inputs are finite; a program needn't handle non-finite values.
Results may differ from a plain program's by a relative error of at most 0.022.
Values may be sent and summed in bfloat16 or wider, within the bound.
No kernel may reach another device: no remote copies, remote signals or barrier semaphores. Data moves between devices by JAX's collectives and lax.ppermute only.
A program may use at most 256 MiB of HBM per device.

v0:
```python
import math

import jax
import jax.numpy as jnp
from jax import lax
from jax.sharding import PartitionSpec as P

HEADS = 15
KV_HEADS = 5
HEAD = 64


EPSILON = 1e-05
MASKED = -1e30


def rotary(values, places, direction):
    half_size = values.shape[-1] // 2
    frequency = jnp.exp(
        jnp.arange(half_size).astype(jnp.float32) * (-math.log(10000.0) / half_size)
    )
    angles = places[:, None] * frequency[None, :]
    cosine = jnp.cos(angles)[:, None, :]
    sine = direction * jnp.sin(angles)[:, None, :]
    first_half = values[..., :half_size]
    second_half = values[..., half_size:]
    return jnp.concatenate(
        [first_half * cosine - second_half * sine, second_half * cosine + first_half * sine], -1
    )


def rms_scale(stream):
    return lax.rsqrt(jnp.mean(stream * stream, -1, keepdims=True) + EPSILON)


def take_half(stacked, my_half):
    return lax.dynamic_index_in_dim(stacked, my_half, 0, keepdims=False)


def store_half(stacked, my_half, update):
    return lax.dynamic_update_index_in_dim(stacked, update, my_half, 0)


def per_device(
    inputs,
    norm1_gain,
    q_weight,
    k_weight,
    v_weight,
    o_weight,
    norm2_gain,
    gate_weight,
    up_weight,
    down_weight,
    cotangent,
):
    seq_count = inputs.shape[0]
    block_len = inputs.shape[2]
    model_width = inputs.shape[3]
    ctx_count = lax.axis_size("ctx")
    ctx_rank = lax.axis_index("ctx")
    groups = HEADS // KV_HEADS
    kv_width = KV_HEADS * HEAD
    score_scale = HEAD ** (-0.5)
    row_count = 2 * block_len * seq_count
    stream = jnp.transpose(inputs, (1, 2, 0, 3)).reshape(row_count, model_width).astype(jnp.float32)
    cot_rows = jnp.transpose(cotangent, (1, 2, 0, 3)).reshape(row_count, model_width)
    offsets = jnp.arange(block_len, dtype=jnp.int32)
    front_start = ctx_rank * block_len
    back_start = (2 * ctx_count - 1 - ctx_rank) * block_len
    own_places = jnp.concatenate([front_start + offsets, back_start + offsets])
    places = jnp.repeat(own_places.astype(jnp.float32), seq_count)
    causal = offsets[:, None] >= offsets[None, :]
    everywhere = jnp.ones((block_len, block_len), jnp.bool_)
    gain_one, weight_q, weight_k, weight_v, weight_o = (
        lax.all_gather(norm1_gain, "wsh", axis=0, tiled=True),
        lax.all_gather(q_weight, "wsh", axis=0, tiled=True),
        lax.all_gather(k_weight, "wsh", axis=0, tiled=True),
        lax.all_gather(v_weight, "wsh", axis=0, tiled=True),
        lax.all_gather(o_weight, "wsh", axis=0, tiled=True),
    )
    scale_one = rms_scale(stream)
    normed = (stream * scale_one * gain_one.astype(jnp.float32)).astype(jnp.bfloat16)
    queries = (
        rotary(
            jnp.dot(normed, weight_q, preferred_element_type=jnp.float32).reshape(
                row_count, HEADS, HEAD
            ),
            places,
            1.0,
        )
        .reshape(row_count, HEADS * HEAD)
        .astype(jnp.bfloat16)
    )
    key_rows = (
        rotary(
            jnp.dot(normed, weight_k, preferred_element_type=jnp.float32).reshape(
                row_count, KV_HEADS, HEAD
            ),
            places,
            1.0,
        )
        .reshape(row_count, kv_width)
        .astype(jnp.bfloat16)
    )
    value_rows = jnp.dot(normed, weight_v, preferred_element_type=jnp.float32).astype(jnp.bfloat16)
    own_pairs = jnp.concatenate([key_rows, value_rows], 1).reshape(
        2 * block_len, seq_count, 2 * kv_width
    )
    gathered = lax.all_gather(own_pairs, "ctx", axis=0, tiled=True)
    query_tiles = queries.reshape(2, block_len, seq_count, KV_HEADS, groups, HEAD)

    def split_pairs(pair_rows):
        shaped = pair_rows.reshape(2, block_len, seq_count, 2 * kv_width)
        key_part = shaped[..., :kv_width].reshape(2, block_len, seq_count, KV_HEADS, HEAD)
        value_part = shaped[..., kv_width:].reshape(2, block_len, seq_count, KV_HEADS, HEAD)
        return (key_part, value_part)

    def device_tiles(source, device):
        return split_pairs(
            lax.dynamic_slice_in_dim(source, device * 2 * block_len, 2 * block_len, 0)
        )

    own_keys, own_values = split_pairs(own_pairs)

    def visit_device(running, source, device, tile_fn):
        key_stack, value_stack = device_tiles(source, device)
        upper_half = (device > ctx_rank).astype(jnp.int32)
        running = tile_fn(running, 1, key_stack[0], value_stack[0], everywhere)
        allowed = jnp.logical_or(device != ctx_rank, causal)
        return tile_fn(
            running,
            upper_half,
            take_half(key_stack, upper_half),
            take_half(value_stack, upper_half),
            allowed,
        )

    def over_devices(running, source, tile_fn, with_own):
        if with_own:
            running = tile_fn(running, 1, own_keys[1], own_values[1], causal)
        half_count = ctx_count // 2

        def loop_step(turn_index, running_in):
            running_in = visit_device(running_in, source, turn_index, tile_fn)
            return visit_device(running_in, source, turn_index + half_count, tile_fn)

        return lax.fori_loop(0, half_count, loop_step, running)

    def scores_of(my_half, key_tile, allowed):
        raw_scores = jnp.einsum(
            "qbhgd,kbhd->bhgqk",
            take_half(query_tiles, my_half),
            key_tile,
            preferred_element_type=jnp.float32,
        )
        return jnp.where(allowed, raw_scores * score_scale, MASKED)

    def stat_tile(running, my_half, key_tile, value_tile, allowed):
        scores = scores_of(my_half, key_tile, allowed)
        top_old = take_half(running[0], my_half)
        sum_old = take_half(running[1], my_half)
        top_new = jnp.maximum(top_old, jnp.max(scores, -1))
        sum_new = sum_old * jnp.exp(top_old - top_new) + jnp.sum(
            jnp.exp(scores - top_new[..., None]), -1
        )
        return (store_half(running[0], my_half, top_new), store_half(running[1], my_half, sum_new))

    stat_shape = (2, seq_count, KV_HEADS, groups, block_len)
    row_tops, totals = over_devices(
        (jnp.full(stat_shape, MASKED, jnp.float32), jnp.zeros(stat_shape, jnp.float32)),
        gathered,
        stat_tile,
        True,
    )
    log_total = row_tops + jnp.log(totals)

    def probs_of(my_half, key_tile, allowed):
        return jnp.exp(
            scores_of(my_half, key_tile, allowed) - take_half(log_total, my_half)[..., None]
        )

    def out_tile(running, my_half, key_tile, value_tile, allowed):
        weights_low = probs_of(my_half, key_tile, allowed).astype(jnp.bfloat16)
        update = jnp.einsum(
            "bhgqk,kbhd->qbhgd", weights_low, value_tile, preferred_element_type=jnp.float32
        )
        return store_half(running, my_half, take_half(running, my_half) + update)

    attended = over_devices(
        jnp.zeros((2, block_len, seq_count, KV_HEADS, groups, HEAD), jnp.float32),
        gathered,
        out_tile,
        True,
    )
    attn_rows = attended.reshape(row_count, HEADS * HEAD).astype(jnp.bfloat16)
    middle = stream + jnp.dot(attn_rows, weight_o, preferred_element_type=jnp.float32)
    gain_two, weight_gate, weight_up, weight_down = (
        lax.all_gather(norm2_gain, "wsh", axis=0, tiled=True),
        lax.all_gather(gate_weight, "wsh", axis=0, tiled=True),
        lax.all_gather(up_weight, "wsh", axis=0, tiled=True),
        lax.all_gather(down_weight, "wsh", axis=0, tiled=True),
    )
    scale_two = rms_scale(middle)
    normed_two = (middle * scale_two * gain_two.astype(jnp.float32)).astype(jnp.bfloat16)
    gate_pre = jnp.dot(normed_two, weight_gate, preferred_element_type=jnp.float32)
    up_pre = jnp.dot(normed_two, weight_up, preferred_element_type=jnp.float32)
    gate_sig = jax.nn.sigmoid(gate_pre)
    gate_act = jax.nn.silu(gate_pre)
    hidden = (gate_act * up_pre).astype(jnp.bfloat16)
    result = middle + jnp.dot(hidden, weight_down, preferred_element_type=jnp.float32)
    output = jnp.transpose(
        result.astype(jnp.bfloat16).reshape(2, block_len, seq_count, model_width), (2, 0, 1, 3)
    )
    gain_two, weight_gate, weight_up, weight_down = (
        lax.all_gather(norm2_gain, "wsh", axis=0, tiled=True),
        lax.all_gather(gate_weight, "wsh", axis=0, tiled=True),
        lax.all_gather(up_weight, "wsh", axis=0, tiled=True),
        lax.all_gather(down_weight, "wsh", axis=0, tiled=True),
    )
    cot_float = cot_rows.astype(jnp.float32)
    grad_down = jnp.einsum("rf,rd->fd", hidden, cot_rows, preferred_element_type=jnp.float32)
    grad_hidden = jnp.einsum("rd,fd->rf", cot_rows, weight_down, preferred_element_type=jnp.float32)
    grad_gate = (grad_hidden * up_pre * gate_sig * (1.0 + gate_pre * (1.0 - gate_sig))).astype(
        jnp.bfloat16
    )
    grad_up = (grad_hidden * gate_act).astype(jnp.bfloat16)
    grad_wgate = jnp.einsum("rd,rf->df", normed_two, grad_gate, preferred_element_type=jnp.float32)
    grad_wup = jnp.einsum("rd,rf->df", normed_two, grad_up, preferred_element_type=jnp.float32)
    grad_normed_two = jnp.einsum(
        "rf,df->rd", grad_gate, weight_gate, preferred_element_type=jnp.float32
    ) + jnp.einsum("rf,df->rd", grad_up, weight_up, preferred_element_type=jnp.float32)
    grad_gain_two = jnp.sum(grad_normed_two * middle * scale_two, 0)
    scaled_two = grad_normed_two * gain_two.astype(jnp.float32)
    grad_middle = cot_float + scale_two * (
        scaled_two
        - middle * scale_two * scale_two * jnp.mean(scaled_two * middle, -1, keepdims=True)
    )
    mlp_sums = (
        lax.psum_scatter(
            grad_gain_two.astype(jnp.bfloat16), "wsh", scatter_dimension=0, tiled=True
        ).astype(jnp.float32),
        lax.psum_scatter(
            grad_wgate.astype(jnp.bfloat16), "wsh", scatter_dimension=0, tiled=True
        ).astype(jnp.float32),
        lax.psum_scatter(
            grad_wup.astype(jnp.bfloat16), "wsh", scatter_dimension=0, tiled=True
        ).astype(jnp.float32),
        lax.psum_scatter(
            grad_down.astype(jnp.bfloat16), "wsh", scatter_dimension=0, tiled=True
        ).astype(jnp.float32),
    )
    gain_one, weight_q, weight_k, weight_v, weight_o = (
        lax.all_gather(norm1_gain, "wsh", axis=0, tiled=True),
        lax.all_gather(q_weight, "wsh", axis=0, tiled=True),
        lax.all_gather(k_weight, "wsh", axis=0, tiled=True),
        lax.all_gather(v_weight, "wsh", axis=0, tiled=True),
        lax.all_gather(o_weight, "wsh", axis=0, tiled=True),
    )
    grad_branch = grad_middle.astype(jnp.bfloat16)
    grad_wo = jnp.einsum("rc,rd->cd", attn_rows, grad_branch, preferred_element_type=jnp.float32)
    grad_attn = jnp.einsum(
        "rd,cd->rc", grad_branch, weight_o, preferred_element_type=jnp.float32
    ).astype(jnp.bfloat16)
    grad_tiles = grad_attn.reshape(2, block_len, seq_count, KV_HEADS, groups, HEAD)
    inner_sum = jnp.transpose(
        jnp.sum(grad_tiles.astype(jnp.float32) * attended, -1), (0, 2, 3, 4, 1)
    )
    source = gathered

    def tile_grads(my_half, key_tile, value_tile, allowed):
        weights_f = probs_of(my_half, key_tile, allowed)
        grad_weights = jnp.einsum(
            "qbhgd,kbhd->bhgqk",
            take_half(grad_tiles, my_half),
            value_tile,
            preferred_element_type=jnp.float32,
        )
        grad_scores = (
            weights_f * (grad_weights - take_half(inner_sum, my_half)[..., None]) * score_scale
        ).astype(jnp.bfloat16)
        return (weights_f.astype(jnp.bfloat16), grad_scores)

    def query_tile(running, my_half, key_tile, value_tile, allowed):
        grad_scores = tile_grads(my_half, key_tile, value_tile, allowed)[1]
        update = jnp.einsum(
            "bhgqk,kbhd->qbhgd", grad_scores, key_tile, preferred_element_type=jnp.float32
        )
        return store_half(running, my_half, take_half(running, my_half) + update)

    query_zero = jnp.zeros((2, block_len, seq_count, KV_HEADS, groups, HEAD), jnp.float32)
    grad_queries = over_devices(query_zero, source, query_tile, False)

    def key_contrib(my_half, key_tile, value_tile, allowed):
        weights_low, grad_scores = tile_grads(my_half, key_tile, value_tile, allowed)
        grad_key = jnp.einsum(
            "bhgqk,qbhgd->kbhd",
            grad_scores,
            take_half(query_tiles, my_half),
            preferred_element_type=jnp.float32,
        )
        grad_value = jnp.einsum(
            "bhgqk,qbhgd->kbhd",
            weights_low,
            take_half(grad_tiles, my_half),
            preferred_element_type=jnp.float32,
        )
        return (grad_key, grad_value, grad_scores)

    def device_term(device):
        key_stack, value_stack = device_tiles(source, device)
        upper_half = (device > ctx_rank).astype(jnp.int32)
        key_front, value_front, unused_front = key_contrib(
            1, key_stack[0], value_stack[0], everywhere
        )
        allowed = jnp.logical_or(device != ctx_rank, causal)
        key_pick, value_pick, unused_pick = key_contrib(
            upper_half,
            take_half(key_stack, upper_half),
            take_half(value_stack, upper_half),
            allowed,
        )
        key_sum = jnp.stack([key_front, jnp.zeros_like(key_front)])
        key_sum = store_half(key_sum, upper_half, take_half(key_sum, upper_half) + key_pick)
        value_sum = jnp.stack([value_front, jnp.zeros_like(value_front)])
        value_sum = store_half(value_sum, upper_half, take_half(value_sum, upper_half) + value_pick)
        return jnp.concatenate(
            [
                key_sum.reshape(2 * block_len, seq_count, kv_width),
                value_sum.reshape(2 * block_len, seq_count, kv_width),
            ],
            -1,
        )

    def device_couple(device_pair):
        return jnp.stack([device_term(device_pair[0]), device_term(device_pair[1])])

    device_count = lax.axis_size("ctx") * (2 * block_len) // (2 * block_len)
    devices = jnp.arange(device_count, dtype=jnp.int32)
    term_rows = lax.map(device_couple, devices.reshape(device_count // 2, 2))
    kv_sums = lax.psum_scatter(
        term_rows.reshape(lax.axis_size("ctx") * (2 * block_len), seq_count, 2 * kv_width).astype(
            jnp.bfloat16
        ),
        "ctx",
        scatter_dimension=0,
        tiled=True,
    ).astype(jnp.float32)
    key_own, value_own, scores_own = key_contrib(1, own_keys[1], own_values[1], causal)
    grad_queries = grad_queries.at[1].add(
        jnp.einsum("bhgqk,kbhd->qbhgd", scores_own, own_keys[1], preferred_element_type=jnp.float32)
    )
    kv_shaped = kv_sums.reshape(2, block_len, seq_count, 2 * kv_width)
    grad_key_post = (
        kv_shaped[..., :kv_width]
        .reshape(2, block_len, seq_count, KV_HEADS, HEAD)
        .at[1]
        .add(key_own)
    )
    grad_value_post = (
        kv_shaped[..., kv_width:]
        .reshape(2, block_len, seq_count, KV_HEADS, HEAD)
        .at[1]
        .add(value_own)
    )
    grad_query_rows = (
        rotary(grad_queries.reshape(row_count, HEADS, HEAD), places, -1.0)
        .reshape(row_count, HEADS * HEAD)
        .astype(jnp.bfloat16)
    )
    grad_key_rows = (
        rotary(grad_key_post.reshape(row_count, KV_HEADS, HEAD), places, -1.0)
        .reshape(row_count, kv_width)
        .astype(jnp.bfloat16)
    )
    grad_value_rows = grad_value_post.reshape(row_count, kv_width).astype(jnp.bfloat16)
    grad_wq = jnp.einsum("rd,rc->dc", normed, grad_query_rows, preferred_element_type=jnp.float32)
    grad_wk = jnp.einsum("rd,rc->dc", normed, grad_key_rows, preferred_element_type=jnp.float32)
    grad_wv = jnp.einsum("rd,rc->dc", normed, grad_value_rows, preferred_element_type=jnp.float32)
    grad_normed = jnp.einsum(
        "rc,dc->rd", grad_query_rows, weight_q, preferred_element_type=jnp.float32
    )
    grad_normed = grad_normed + jnp.einsum(
        "rc,dc->rd", grad_key_rows, weight_k, preferred_element_type=jnp.float32
    )
    grad_normed = grad_normed + jnp.einsum(
        "rc,dc->rd", grad_value_rows, weight_v, preferred_element_type=jnp.float32
    )
    grad_gain_one = jnp.sum(grad_normed * stream * scale_one, 0)
    scaled_one = grad_normed * gain_one.astype(jnp.float32)
    grad_stream = grad_middle + scale_one * (
        scaled_one
        - stream * scale_one * scale_one * jnp.mean(scaled_one * stream, -1, keepdims=True)
    )
    attn_sums = (
        lax.psum_scatter(
            grad_gain_one.astype(jnp.bfloat16), "wsh", scatter_dimension=0, tiled=True
        ).astype(jnp.float32),
        lax.psum_scatter(
            grad_wq.astype(jnp.bfloat16), "wsh", scatter_dimension=0, tiled=True
        ).astype(jnp.float32),
        lax.psum_scatter(
            grad_wk.astype(jnp.bfloat16), "wsh", scatter_dimension=0, tiled=True
        ).astype(jnp.float32),
        lax.psum_scatter(
            grad_wv.astype(jnp.bfloat16), "wsh", scatter_dimension=0, tiled=True
        ).astype(jnp.float32),
        lax.psum_scatter(
            grad_wo.astype(jnp.bfloat16), "wsh", scatter_dimension=0, tiled=True
        ).astype(jnp.float32),
    )
    summed = (
        lax.psum(attn_sums[0].astype(jnp.bfloat16), "ctx").astype(jnp.float32),
        lax.psum(attn_sums[1].astype(jnp.bfloat16), "ctx").astype(jnp.float32),
        lax.psum(attn_sums[2].astype(jnp.bfloat16), "ctx").astype(jnp.float32),
        lax.psum(attn_sums[3].astype(jnp.bfloat16), "ctx").astype(jnp.float32),
        lax.psum(attn_sums[4].astype(jnp.bfloat16), "ctx").astype(jnp.float32),
        lax.psum(mlp_sums[0].astype(jnp.bfloat16), "ctx").astype(jnp.float32),
        lax.psum(mlp_sums[1].astype(jnp.bfloat16), "ctx").astype(jnp.float32),
        lax.psum(mlp_sums[2].astype(jnp.bfloat16), "ctx").astype(jnp.float32),
        lax.psum(mlp_sums[3].astype(jnp.bfloat16), "ctx").astype(jnp.float32),
    )
    input_grad = jnp.transpose(
        grad_stream.reshape(2, block_len, seq_count, model_width), (2, 0, 1, 3)
    )
    return (
        output,
        input_grad,
        summed[0],
        summed[1],
        summed[2],
        summed[3],
        summed[4],
        summed[5],
        summed[6],
        summed[7],
        summed[8],
    )


def solution(mesh):
    return jax.shard_map(
        per_device,
        mesh=mesh,
        in_specs=(
            P("wsh", None, "ctx", None),
            P("wsh"),
            P("wsh", None),
            P("wsh", None),
            P("wsh", None),
            P("wsh", None),
            P("wsh"),
            P("wsh", None),
            P("wsh", None),
            P("wsh", None),
            P("wsh", None, "ctx", None),
        ),
        out_specs=(
            P("wsh", None, "ctx", None),
            P("wsh", None, "ctx", None),
            P("wsh"),
            P("wsh", None),
            P("wsh", None),
            P("wsh", None),
            P("wsh", None),
            P("wsh"),
            P("wsh", None),
            P("wsh", None),
            P("wsh", None),
        ),
        check_vma=False,
    )
```

profile of v0, /device:TPU:0, one launch (start us, length us, event | category | flops | bytes accessed | tf_op | source)
XLA Modules:
  0.0 1336.8 jit_solution(14760902774438962299)
XLA Ops:
  12.0 8.3 all-reduce.14
  26.4 10.6 all-gather
  50.2 8.0 all-gather.1
  93.7 59.8 %all-gather.11.cloned.1.call-done = bf16[2048,2,640]{2,1,0:T(2,128)(2,1)} async-done(((bf16[256,2,640]{2,1,0:T(2,128)(2,1)}), bf16[2048,2,640]{2,1,0:T(2,128)(2,1)}) %all-gather.11.cloned.1.call-update) | async-done | bytes 5242896 | tf_op jit(solution)/shard_map/all_gather | solution.py:110
  153.5 5.5 copy.311
  159.0 25.4 %while.74 = (s32[]{:T(128)}, f32[2,2,5,3,128]{4,3,2,1,0:T(4,128)S(1)}, f32[2,2,5,3,128]{4,3,2,1,0:T(4,128)S(1)}, bf16[2048,2,640]{2,0,1:T(8,128)(2,1)}, bf16[2,1...) while((s32[]{:T(128)}, ...), condition=%wide.region_12.13_spmd.clone.clone, body=%wide.region_3.12_spmd.clone.clone.sunk | while | flops 263566336 | bytes 25864548 | solution.py:148
  186.9 107.7 %while.75 = (s32[]{:T(128)}, f32[2,128,2,5,3,64]{1,5,4,3,2,0:T(8,128)S(1)}, bf16[2048,2,640]{2,0,1:T(8,128)(2,1)}, bf16[2,128,2,5,3,64]{1,5,4,3,2,0:T(8,128)(2,1...) while((s32[]{:T(128)}, ...), condition=%wide.region_14.15_spmd.clone.clone, body=%wide.region_13.14_spmd.clone.clone.sunk | while | flops 511246336 | bytes 41531920 | solution.py:148
  303.6 5.5 convert_element_type.454
  313.8 7.4 fusion.412
  321.2 7.2 fusion.413
  328.4 9.5 multiply_convert_fusion
  338.0 6.6 fusion.414
  354.2 5.7 reshape.895
  362.9 7.5 multiply_reduce_fusion
  372.6 244.3 %while.77 = (s32[]{:T(128)}, bf16[4,2,256,2,640]{2,4,3,1,0:T(8,128)(2,1)}, s32[4,2]{0,1:T(2,128)S(1)}, bf16[2048,2,640]{2,0,1:T(8,128)(2,1)}, bf16[2,128,2,5,3,6...) while((s32[]{:T(128)}, ...), condition=%wide.region_21.22_spmd.clone.clone, body=%wide.region_20.21_spmd.clone.clone.sunk | while | flops 1028980736 | bytes 80653464 | solution.py:340
  616.9 7.9 copy.338
  626.0 6.7 convolution_convert_fusion
  632.7 7.9 copy.424
  653.3 72.6 %reduce-scatter.15.cloned.1.call-done = bf16[256,2,640]{2,0,1:T(8,128)(2,1)} async-done(((bf16[2048,2,640]{2,0,1:T(8,128)(2,1)}), bf16[256,2,640]{2,0,1:T(8,128)(2,1)}) %reduce-scatter.15.cloned.1.call-update) | async-done | bytes 655376 | tf_op jit(solution)/shard_map/reduce_scatter | solution.py:341
  750.8 175.0 %while.76 = (s32[]{:T(128)}, f32[2,128,2,5,3,64]{1,5,4,3,2,0:T(8,128)}, bf16[2048,2,640]{2,0,1:T(8,128)(2,1)}, bf16[2,128,2,5,3,64]{1,5,4,3,2,0:T(8,128)(2,1)S(1...) while((s32[]{:T(128)}, ...), condition=%wide.region_19.20_spmd.clone.clone, body=%wide.region_18.19_spmd.clone.clone.sunk | while | flops 768802816 | bytes 53811768 | solution.py:148
  928.7 5.7 copy.331
  940.1 7.6 fusion.406
  962.7 6.1 convolution_convert_fusion.2
  968.8 6.1 convolution_convert_fusion.1
  981.1 15.5 %reduce-scatter.17.cloned.1.call-done = bf16[240,960]{1,0:T(8,128)(2,1)} async-done(((bf16[960,960]{1,0:T(8,128)(2,1)}), bf16[240,960]{1,0:T(8,128)(2,1)}) %reduce-scatter.17.cloned.1.call-update) | async-done | bytes 460816 | tf_op jit(solution)/shard_map/reduce_scatter | solution.py:399
  996.6 33.6 %reduce-scatter.19.cloned.1.call-done = bf16[240,960]{1,0:T(8,128)(2,1)} async-done(((bf16[960,960]{1,0:T(8,128)(2,1)}), bf16[240,960]{1,0:T(8,128)(2,1)}) %reduce-scatter.19.cloned.1.call-update) | async-done | bytes 460816 | tf_op jit(solution)/shard_map/reduce_scatter | solution.py:408
  1030.2 52.0 %reduce-scatter.21.cloned.1.call-done = bf16[240,2560]{1,0:T(8,128)(2,1)} async-done(((bf16[960,2560]{1,0:T(8,128)(2,1)}), bf16[240,2560]{1,0:T(8,128)(2,1)}) %reduce-scatter.21.cloned.1.call-update) | async-done | bytes 1228816 | tf_op jit(solution)/shard_map/reduce_scatter | solution.py:243
  1082.2 51.7 %reduce-scatter.23.cloned.1.call-done = bf16[240,2560]{1,0:T(8,128)(2,1)} async-done(((bf16[960,2560]{1,0:T(8,128)(2,1)}), bf16[240,2560]{1,0:T(8,128)(2,1)}) %reduce-scatter.23.cloned.1.call-update) | async-done | bytes 1228816 | tf_op jit(solution)/shard_map/reduce_scatter | solution.py:246
  1135.5 5.9 add_convert_fusion
  1152.0 6.0 all-reduce.13
  1158.2 22.6 %all-reduce.11 = (bf16[240]{0:T(256)(128)(2,1)S(1)}, bf16[240]{0:T(256)(128)(2,1)S(1)}) all-reduce(bf16[240]{0:T(256)(128)(2,1)S(1)} %dynamic-slice.31, bf16[240]{0:T(256)(128)(2,1)S(1)} %dynamic-slice.33), channel_id=1, replica_groups=mesh['ctx'=8,'wsh'=4] {'ctx'}, use_global_device_ids=true, to_apply=%region_26.27 | all-reduce | flops 480 | bytes 1920 | tf_op jit(solution)/shard_map/psum | solution.py:413
  1194.2 125.5 %all-reduce.17.cloned.1.call-done = (bf16[240,960]{1,0:T(8,128)(2,1)}, bf16[240,320]{0,1:T(8,128)(2,1)}, bf16[240,320]{0,1:T(8,128)(2,1)}, bf16[240,960]{1,0:T(8...) async-done(((bf16[240,960]{1,0:T(8,128)(2,1)}, bf16[240,320]{0,1:T(8,128)(2,1)}, bf16[240,320]{0,1:T(8,128)(2,1)}, ...) | async-done | bytes 4915216 | tf_op jit(solution)/shard_map/psum | solution.py:414
  (972 shorter events, 726.6 us)
Async XLA Ops:
  7.2 14.7 %copy-start.24 = (bf16[2,2,128,960]{2,3,1,0:T(8,128)(2,1)S(1)}, bf16[2,2,128,960]{2,3,1,0:T(8,128)(2,1)}, u32[]{:S(2)}) copy-start(bf16[2,2,128,960]{2,3,1,0:T(8,128)(2,1)} %param.25) | copy-start | bytes 2949124
  7.2 71.6 %all-gather.9.cloned.1.call-start = ((), (), s32[]{:S(2)}) async-start(), calls=%async_computation.8 | async-start | bytes 2457600 | tf_op jit(solution)/shard_map/all_gather | solution.py:77
  7.9 145.6 %all-gather.11.cloned.1.call-start = ((), (), s32[]{:S(2)}) async-start(), calls=%async_computation.9 | async-start | bytes 5898240 | tf_op jit(solution)/shard_map/all_gather | solution.py:110
  20.3 44.7 %copy-start.75 = (f32[960]{0:T(1024)}, f32[960]{0:T(1024)S(1)}, u32[]{:S(2)}) copy-start(f32[960]{0:T(1024)S(1)} %convert_element_type.443) | copy-start | bytes 11524
  26.4 56.2 %copy-start.20 = (bf16[512,960]{1,0:T(8,128)(2,1)}, bf16[512,960]{1,0:T(8,128)(2,1)S(1)}, u32[]{:S(2)}) copy-start(bf16[512,960]{1,0:T(8,128)(2,1)S(1)} %convert_element_type.445) | copy-start | bytes 2949124
  50.1 14.9 %copy-start.13 = (f32[512,960]{0,1:T(8,128)}, f32[512,960]{0,1:T(8,128)S(1)}, u32[]{:S(2)}) copy-start(f32[512,960]{0,1:T(8,128)S(1)} %copy.317) | copy-start | bytes 5898244
  50.2 14.7 %copy-start.77 = (f32[512]{0:T(512)}, f32[512]{0:T(512)S(1)}, u32[]{:S(2)}) copy-start(f32[512]{0:T(512)S(1)} %rsqrt.21) | copy-start | bytes 6148
  63.1 22.3 %copy-start.52 = (f32[512,32]{0,1:T(8,128)}, f32[512,32]{0,1:T(8,128)S(1)}, u32[]{:S(2)}) copy-start(f32[512,32]{0,1:T(8,128)S(1)} %get-tuple-element.1318) | copy-start | bytes 196612
  67.0 242.1 %all-gather.13.cloned.1.call-start = ((), (), s32[]{:S(2)}) async-start(), calls=%async_computation.10 | async-start | bytes 2457600 | tf_op jit(solution)/shard_map/all_gather | solution.py:80
  67.8 246.1 %all-gather.15.cloned.1.call-start = ((), (), s32[]{:S(2)}) async-start(), calls=%async_computation.11 | async-start | bytes 6144000 | tf_op jit(solution)/shard_map/all_gather | solution.py:200
  68.4 252.9 %all-gather.17.cloned.1.call-start = ((), (), s32[]{:S(2)}) async-start(), calls=%async_computation.12 | async-start | bytes 6144000 | tf_op jit(solution)/shard_map/all_gather | solution.py:201
  68.9 259.5 %all-gather.19.cloned.1.call-start = ((), (), s32[]{:S(2)}) async-start(), calls=%async_computation.13 | async-start | bytes 6144000 | tf_op jit(solution)/shard_map/all_gather | solution.py:202
  69.5 656.3 %reduce-scatter.15.cloned.1.call-start = ((), (), s32[]{:S(2)}) async-start(), calls=%async_computation.14 | async-start | bytes 5898240 | tf_op jit(solution)/shard_map/reduce_scatter | solution.py:341
  71.5 16.5 %copy-start.57 = (bf16[1,128,2,320]{1,3,2,0:T(8,128)(2,1)}, bf16[1,128,2,320]{1,3,2,0:T(8,128)(2,1)S(1)}, u32[]{:S(2)}) copy-start(bf16[1,128,2,320]{1,3,2,0:T(8,128)(2,1)S(1)} %copy.304) | copy-start | bytes 491524
  71.8 112.7 %copy-start.55 = (bf16[1,128,2,320]{1,3,2,0:T(8,128)(2,1)}, bf16[1,128,2,320]{1,3,2,0:T(8,128)(2,1)S(1)}, u32[]{:S(2)}) copy-start(bf16[1,128,2,320]{1,3,2,0:T(8,128)(2,1)S(1)} %copy.303) | copy-start | bytes 491524
  313.8 7.4 copy-start.18
  321.2 7.2 copy-start.39
  338.0 6.6 copy-start.83
  338.0 6.6 copy-start.82
  338.0 6.6 copy-start.28
  338.0 6.6 copy-start.33
  389.2 6.4 copy-start.51
  624.8 350.4 %reduce-scatter.29.cloned.1.call-start = ((), (), s32[]{:S(2)}) async-start(), calls=%async_computation.21 | async-start | bytes 6553600
  640.6 337.1 %reduce-scatter.25.cloned.1.call-start = ((), (), s32[]{:S(2)}) async-start(), calls=%async_computation.19 | async-start | bytes 921600
  653.3 80.7 %copy-start.23 = (bf16[2,5,3,128,128]{3,4,2,1,0:T(8,128)(2,1)}, bf16[2,5,3,128,128]{3,4,2,1,0:T(8,128)(2,1)S(1)}, u32[]{:S(2)}) copy-start(bf16[2,5,3,128,128]{3,4,2,1,0:T(8,128)(2,1)S(1)} %fusion.371) | copy-start | bytes 2949124
  749.0 230.4 %reduce-scatter.27.cloned.1.call-start = ((), (), s32[]{:S(2)}) async-start(), calls=%async_computation.20 | async-start | bytes 921600
  928.6 7.4 copy-start.35
  939.8 56.8 %reduce-scatter.17.cloned.1.call-start = ((), (), s32[]{:S(2)}) async-start(), calls=%async_computation.15 | async-start | bytes 2457600 | tf_op jit(solution)/shard_map/reduce_scatter | solution.py:399
  957.3 72.9 %reduce-scatter.19.cloned.1.call-start = ((), (), s32[]{:S(2)}) async-start(), calls=%async_computation.16 | async-start | bytes 2457600 | tf_op jit(solution)/shard_map/reduce_scatter | solution.py:408
  961.5 120.7 %reduce-scatter.21.cloned.1.call-start = ((), (), s32[]{:S(2)}) async-start(), calls=%async_computation.17 | async-start | bytes 6144000 | tf_op jit(solution)/shard_map/reduce_scatter | solution.py:243
  968.8 165.1 %reduce-scatter.23.cloned.1.call-start = ((), (), s32[]{:S(2)}) async-start(), calls=%async_computation.18 | async-start | bytes 6144000 | tf_op jit(solution)/shard_map/reduce_scatter | solution.py:246
  974.9 344.8 %all-reduce.17.cloned.1.call-start = ((), (), s32[]{:S(2)}) async-start(), calls=%async_computation.22 | async-start | bytes 9994240 | tf_op jit(solution)/shard_map/psum | solution.py:414
  (133 other events, 441.5 us)
Sparse Core Ops, SparseCore 0:
  9.6 27.7 all-gather.8
  67.2 86.2 all-gather.10
  155.1 20.0 all-gather.12
  176.5 38.5 all-gather.14
  216.6 38.5 all-gather.16
  256.6 38.5 all-gather.18
  625.0 100.8 reduce-scatter.14
  728.4 51.1 reduce-scatter.28
  782.3 22.9 reduce-scatter.24
  940.0 22.5 reduce-scatter.26
  965.9 30.6 reduce-scatter.16
  999.6 30.5 reduce-scatter.18
  1033.0 49.1 reduce-scatter.20
  1084.6 49.2 reduce-scatter.22
  1139.7 180.0 all-reduce.16
where the time goes:
time: 1350 us; the launch traced here: 1340 us
  local copies, waits for them, and re-layouts  441 us (33%)
  waiting for transfers between devices  414 us (31%)
  matrix products  335 us (25%)
  blocking collectives  55.6 us (4%)
  other arithmetic  54.2 us (4%)
  loops' own time  18.3 us (1%)
  between operations  16.9 us (1%)
    psum x1, waiting for transfers between devices, per_device(): lax.psum(attn_sums[1].astype(jnp.bfloat16), 'ctx').astype(jnp.float32)  125 us
    reduce_scatter x1, waiting for transfers between devices, per_device(): lax.psum_scatter(term_rows.reshape(lax.axis_size('ctx') * (2 * block_len)...  72.6 us
    unnamed x149, local copies, waits for them, and re-layouts  63.4 us
    all_gather x1, waiting for transfers between devices, per_device(): gathered = lax.all_gather(own_pairs, 'ctx', axis=0, tiled=True)  59.8 us
    dot_general x16, matrix products, query_tile(): jnp.einsum('bhgqk,kbhd->qbhgd', grad_scores, key_tile, preferred_element_...  59.1 us
    reduce_scatter x1, waiting for transfers between devices, per_device(): lax.psum_scatter(grad_wgate.astype(jnp.bfloat16), 'wsh', scatter_dimensio...  52 us
    reduce_scatter x1, waiting for transfers between devices, per_device(): lax.psum_scatter(grad_wup.astype(jnp.bfloat16), 'wsh', scatter_dimension=...  51.7 us
    dot_general x17, matrix products, key_contrib(): jnp.einsum('bhgqk,qbhgd->kbhd', grad_scores, take_half(query_tiles, my_ha...  51.6 us
  transfers between devices with their start and end apart: 15, of which 7 were waited for; matrix products, arithmetic and copies ran while one was open for 39% of the time, Pallas kernels for 0%

commit v1 on v0

v1 whole, which is shorter than its diff:
```python
import functools
import math

import jax
import jax.numpy as jnp
from jax import lax
from jax.experimental import pallas as pl
from jax.experimental.pallas import tpu as pltpu
from jax.sharding import PartitionSpec as P

HEADS = 15
KV_HEADS = 5
HEAD = 64
GROUPS = HEADS // KV_HEADS
KV_WIDTH = KV_HEADS * HEAD
LANES = 128
EPSILON = 1e-05
MASKED = -1e30
SCALE = HEAD ** (-0.5)
VMEM_BYTES = 56 * 1024 * 1024

NT = (((1,), (1,)), ((), ()))
TN = (((0,), (0,)), ((), ()))


def dot(a, b, dims=None):
    if dims is None:
        return jnp.dot(a, b, preferred_element_type=jnp.float32)
    return lax.dot_general(a, b, dims, preferred_element_type=jnp.float32)


def lane_ids(shape):
    return lax.broadcasted_iota(jnp.int32, shape, 1)


def turn(u, cosine, sine):
    first = (lane_ids(u.shape) & 32) == 0
    partner = jnp.where(first, pltpu.roll(u, 96, 1), pltpu.roll(u, 32, 1))
    return u * cosine + partner * sine


def rope_tables(ctx_rank, ctx_count, block_len):
    offsets = jnp.arange(block_len, dtype=jnp.int32)
    front = ctx_rank * block_len + offsets
    back = (2 * ctx_count - 1 - ctx_rank) * block_len + offsets
    places = jnp.concatenate([front, back]).astype(jnp.float32)
    half = HEAD // 2
    frequency = jnp.exp(jnp.arange(half).astype(jnp.float32) * (-math.log(10000.0) / half))
    angles = places[:, None] * frequency[None, :]
    cosine = jnp.cos(angles)
    sine = jnp.sin(angles)
    return (
        jnp.concatenate([cosine] * 4, 1),
        jnp.concatenate([-sine, sine, -sine, sine], 1),
    )


def load_tile(ref, lead, tile, width):
    lo = tile * LANES
    hi = min(lo + LANES, width)
    value = ref[lead + (slice(None), slice(lo, hi))].astype(jnp.float32)
    if hi - lo < LANES:
        value = jnp.concatenate(
            [value, jnp.zeros((value.shape[0], LANES - (hi - lo)), jnp.float32)], 1
        )
    return value


def place_head(value, parity_from, parity_to):
    if parity_from != parity_to:
        value = pltpu.roll(value, HEAD, 1)
    keep = (lane_ids(value.shape) // HEAD) == parity_to
    return jnp.where(keep, value, 0.0)


def head_rows(ref, half, head, parity, width):
    parts = []
    for g in range(GROUPS):
        j = head * GROUPS + g
        parts.append(place_head(load_tile(ref, (0, half), j // 2, width), j % 2, parity))
    return jnp.concatenate(parts, 0)


def attend_kernel(n, block, rank_ref, q_ref, kv_ref, o_ref, lse_ref, qs, wide, narrow, top, total, acc):
    c = rank_ref[0]
    rows = GROUPS * block
    pair = 2 * block
    q_at = lax.broadcasted_iota(jnp.int32, (rows, block), 0) % block
    k_at = lax.broadcasted_iota(jnp.int32, (rows, block), 1)
    causal = k_at <= q_at
    unroll = n if n <= 8 else 4
    for h in range(KV_HEADS):
        kt, kp = h // 2, h % 2
        vt, vp = (KV_HEADS + h) // 2, (KV_HEADS + h) % 2
        kl, vl = pl.ds(kt * LANES, LANES), pl.ds(vt * LANES, LANES)
        for half in range(2):
            qs[half] = head_rows(q_ref, half, h, kp, q_ref.shape[-1]).astype(jnp.bfloat16)
        top[...] = jnp.full_like(top, MASKED)

        def wide_scores(i, carry):
            s = dot(qs[1], kv_ref[0, 0, pl.ds(i * pair, pair), kl], NT)
            wide[i] = s
            top[1] = jnp.maximum(top[1], jnp.maximum(s[:, :block], s[:, block:]))
            return carry

        lax.fori_loop(0, n // 2, wide_scores, 0, unroll=2)

        def narrow_scores(d, carry):
            sel = (d > c).astype(jnp.int32)
            s = dot(qs[sel], kv_ref[0, sel, pl.ds(d * block, block), kl], NT)
            s = jnp.where(jnp.logical_or(causal, d != c), s, MASKED)
            narrow[d] = s
            top[sel] = jnp.maximum(top[sel], s)
            return carry

        lax.fori_loop(0, n, narrow_scores, 0, unroll=unroll)
        s = dot(qs[1], kv_ref[0, 1, pl.ds(c * block, block), kl], NT)
        s = jnp.where(causal, s, MASKED)
        narrow[n] = s
        top[1] = jnp.maximum(top[1], s)
        for half in range(2):
            top[half] = jnp.broadcast_to(
                jnp.max(top[half], axis=1, keepdims=True), (rows, LANES)
            )
        total[...] = jnp.zeros_like(total)
        acc[...] = jnp.zeros_like(acc)

        def wide_sums(i, carry):
            t = top[1]
            s = wide[i]
            pa = jnp.exp(s[:, :block] - t)
            pb = jnp.exp(s[:, block:] - t)
            total[1] += pa + pb
            p = jnp.concatenate([pa, pb], 1).astype(jnp.bfloat16)
            acc[1] += dot(p, kv_ref[0, 0, pl.ds(i * pair, pair), vl])
            return carry

        lax.fori_loop(0, n // 2, wide_sums, 0, unroll=2)

        def narrow_sums(d, carry):
            sel = (d > c).astype(jnp.int32)
            p = jnp.exp(narrow[d] - top[sel])
            total[sel] += p
            acc[sel] += dot(p.astype(jnp.bfloat16), kv_ref[0, sel, pl.ds(d * block, block), vl])
            return carry

        lax.fori_loop(0, n, narrow_sums, 0, unroll=unroll)
        p = jnp.exp(narrow[n] - top[1])
        total[1] += p
        acc[1] += dot(p.astype(jnp.bfloat16), kv_ref[0, 1, pl.ds(c * block, block), vl])
        for half in range(2):
            whole = jnp.broadcast_to(jnp.sum(total[half], axis=1, keepdims=True), (rows, LANES))
            out = acc[half] / whole
            lse = top[half] + jnp.log(whole)
            lse_ref[0, 2 * h + half : 2 * h + half + 1, :] = lse.T[0:1, :]
            for g in range(GROUPS):
                j = h * GROUPS + g
                value = out[g * block : (g + 1) * block]
                if vp != j % 2:
                    value = pltpu.roll(value, HEAD, 1)
                lo = j * HEAD
                o_ref[0, half, :, lo : lo + HEAD] = value[:, (j % 2) * HEAD : (j % 2 + 1) * HEAD]


def attend(rank, queries, pairs, width):
    seqs, _, block, q_width = queries.shape
    n = pairs.shape[2] // block
    rows = GROUPS * block
    return pl.pallas_call(
        functools.partial(attend_kernel, n, block),
        grid=(seqs,),
        in_specs=[
            pl.BlockSpec(memory_space=pltpu.SMEM),
            pl.BlockSpec((1, 2, block, q_width), lambda b: (b, 0, 0, 0)),
            pl.BlockSpec((1, 2, n * block, 2 * KV_WIDTH), lambda b: (b, 0, 0, 0)),
        ],
        out_specs=[
            pl.BlockSpec((1, 2, block, width), lambda b: (b, 0, 0, 0)),
            pl.BlockSpec((1, 2 * KV_HEADS, rows), lambda b: (b, 0, 0)),
        ],
        out_shape=[
            jax.ShapeDtypeStruct((seqs, 2, block, width), jnp.float32),
            jax.ShapeDtypeStruct((seqs, 2 * KV_HEADS, rows), jnp.float32),
        ],
        scratch_shapes=[
            pltpu.VMEM((2, rows, LANES), jnp.bfloat16),
            pltpu.VMEM((n // 2, rows, 2 * block), jnp.float32),
            pltpu.VMEM((n + 1, rows, block), jnp.float32),
            pltpu.VMEM((2, rows, LANES), jnp.float32),
            pltpu.VMEM((2, rows, LANES), jnp.float32),
            pltpu.VMEM((2, rows, LANES), jnp.float32),
        ],
        compiler_params=pltpu.CompilerParams(vmem_limit_bytes=VMEM_BYTES),
        cost_estimate=pl.CostEstimate(
            flops=4 * seqs * HEADS * block * block * HEAD * (2 * n + 1),
            bytes_accessed=8 * 1024 * 1024,
            transcendentals=seqs * HEADS * block * block * (2 * n + 1),
        ),
        name="attend",
    )(rank, queries, pairs)


def attend_back_kernel(
    n, block, rank_ref, q_ref, kv_ref, do_ref, o_ref, lse_ref, cos_ref, sin_ref,
    dq_ref, dkv_ref, qs, dos, inner, dqt, dkv, dq_full,
):
    c = rank_ref[0]
    rows = GROUPS * block
    pair = 2 * block
    width = do_ref.shape[-1]
    k_at = lax.broadcasted_iota(jnp.int32, (block, rows), 0)
    q_at = lax.broadcasted_iota(jnp.int32, (block, rows), 1) % block
    causal = k_at <= q_at
    unroll = n if n <= 8 else 4
    dkv[...] = jnp.zeros_like(dkv)
    dq_full[...] = jnp.zeros_like(dq_full)
    for h in range(KV_HEADS):
        kt, kp = h // 2, h % 2
        vt, vp = (KV_HEADS + h) // 2, (KV_HEADS + h) % 2
        kl, vl = pl.ds(kt * LANES, LANES), pl.ds(vt * LANES, LANES)
        for half in range(2):
            qs[half] = head_rows(q_ref, half, h, kp, q_ref.shape[-1]).astype(jnp.bfloat16)
            inner_parts = []
            do_parts = []
            for g in range(GROUPS):
                j = h * GROUPS + g
                d_o = load_tile(do_ref, (0, half), j // 2, width)
                o = load_tile(o_ref, (0, half), j // 2, width)
                product = place_head(d_o * o, j % 2, j % 2)
                inner_parts.append(jnp.sum(product.T, axis=0, keepdims=True))
                do_parts.append(place_head(d_o, j % 2, vp))
            dos[half] = jnp.concatenate(do_parts, 0).astype(jnp.bfloat16)
            inner[half] = jnp.concatenate(inner_parts, 1)
        dqt[...] = jnp.zeros_like(dqt)

        def visit(sel, half, start, count, mask):
            keys = kv_ref[0, half, pl.ds(start, count), kl]
            values = kv_ref[0, half, pl.ds(start, count), vl]
            s = dot(keys, qs[sel], NT)
            p = jnp.exp(s - lse_ref[0, pl.ds(2 * h + sel, 1), :])
            if mask is not None:
                p = jnp.where(mask, p, 0.0)
            dp = dot(values, dos[sel], NT)
            ds = (p * (dp - inner[sel])).astype(jnp.bfloat16)
            dkv[half, pl.ds(start, count), kl] += dot(ds, qs[sel])
            dkv[half, pl.ds(start, count), vl] += dot(p.astype(jnp.bfloat16), dos[sel])
            dqt[sel] += dot(keys, ds, TN)

        def wide_visit(i, carry):
            visit(1, 0, i * pair, pair, None)
            return carry

        lax.fori_loop(0, n // 2, wide_visit, 0, unroll=2)

        def narrow_visit(d, carry):
            sel = (d > c).astype(jnp.int32)
            visit(sel, sel, d * block, block, jnp.logical_or(causal, d != c))
            return carry

        lax.fori_loop(0, n, narrow_visit, 0, unroll=unroll)
        visit(1, 1, c * block, block, causal)
        for half in range(2):
            grad = dqt[half].T * SCALE
            for g in range(GROUPS):
                j = h * GROUPS + g
                tile = pl.ds((j // 2) * LANES, LANES)
                dq_full[half, :, tile] += place_head(
                    grad[g * block : (g + 1) * block], kp, j % 2
                )
    for half in range(2):
        at = slice(half * block, (half + 1) * block)
        for t in range(dq_full.shape[-1] // LANES):
            value = turn(
                dq_full[half, :, t * LANES : (t + 1) * LANES], cos_ref[at], -sin_ref[at]
            ).astype(jnp.bfloat16)
            hi = min((t + 1) * LANES, width)
            dq_ref[0, half, :, t * LANES : hi] = value[:, : hi - t * LANES]
    dkv_ref[0] = dkv[...].astype(jnp.bfloat16)


def attend_back(rank, queries, pairs, grad_attn, attended, lse, cosine, sine):
    seqs, _, block, q_width = queries.shape
    width = grad_attn.shape[-1]
    n = pairs.shape[2] // block
    rows = GROUPS * block
    whole4 = lambda b: (b, 0, 0, 0)
    buffers = pl.Buffered(2 if n <= 8 else 1)
    return pl.pallas_call(
        functools.partial(attend_back_kernel, n, block),
        grid=(seqs,),
        in_specs=[
            pl.BlockSpec(memory_space=pltpu.SMEM),
            pl.BlockSpec((1, 2, block, q_width), whole4),
            pl.BlockSpec((1, 2, n * block, 2 * KV_WIDTH), whole4, pipeline_mode=buffers),
            pl.BlockSpec((1, 2, block, width), whole4),
            pl.BlockSpec((1, 2, block, width), whole4),
            pl.BlockSpec((1, 2 * KV_HEADS, rows), lambda b: (b, 0, 0)),
            pl.BlockSpec((2 * block, LANES), lambda b: (0, 0)),
            pl.BlockSpec((2 * block, LANES), lambda b: (0, 0)),
        ],
        out_specs=[
            pl.BlockSpec((1, 2, block, width), whole4),
            pl.BlockSpec((1, 2, n * block, 2 * KV_WIDTH), whole4, pipeline_mode=buffers),
        ],
        out_shape=[
            jax.ShapeDtypeStruct((seqs, 2, block, width), jnp.bfloat16),
            jax.ShapeDtypeStruct((seqs, 2, n * block, 2 * KV_WIDTH), jnp.bfloat16),
        ],
        scratch_shapes=[
            pltpu.VMEM((2, rows, LANES), jnp.bfloat16),
            pltpu.VMEM((2, rows, LANES), jnp.bfloat16),
            pltpu.VMEM((2, 1, rows), jnp.float32),
            pltpu.VMEM((2, LANES, rows), jnp.float32),
            pltpu.VMEM((2, n * block, 2 * KV_WIDTH), jnp.float32),
            pltpu.VMEM((2, block, q_width), jnp.float32),
        ],
        compiler_params=pltpu.CompilerParams(vmem_limit_bytes=VMEM_BYTES),
        cost_estimate=pl.CostEstimate(
            flops=10 * seqs * HEADS * block * block * HEAD * (2 * n + 1),
            bytes_accessed=16 * 1024 * 1024,
            transcendentals=seqs * HEADS * block * block * (2 * n + 1),
        ),
        name="attend_back",
    )(rank, queries, pairs, grad_attn, attended, lse, cosine, sine)


def pieces_of(shard, axis):
    count = lax.axis_size(axis)
    found = {0: shard}
    bit = count // 2
    while bit:
        swap = [(i, i ^ bit) for i in range(count)]
        for p in list(found):
            found[p ^ bit] = lax.ppermute(found[p], axis, swap)
        bit //= 2
    return [found[p] for p in range(count)]


def weight_pieces(shard, axis):
    if shard.shape[0] % 16 == 0:
        return pieces_of(shard, axis), lax.axis_index(axis)
    return [lax.all_gather(shard, axis, axis=0, tiled=True)], jnp.int32(0)


def fetch(pieces, target, base, sems):
    copies = []
    for p, piece in enumerate(pieces):
        height = piece.shape[0]
        at = pl.multiple_of(jnp.bitwise_xor(base, p) * height, 16)
        copy = pltpu.make_async_copy(piece, target.at[pl.ds(at, height)], sems.at[p])
        copy.start()
        copies.append(copy)
    return copies


def project_kernel(count, base_ref, x_ref, cos_ref, sin_ref, *refs):
    pieces = refs[:count]
    w_ref, normed_ref, q_ref, kv_ref, gains_ref, sems = refs[count:]
    copies = fetch(pieces, w_ref, base_ref[0], sems)
    seqs, _, block, width = x_ref.shape
    rows = seqs * 2 * block
    x = x_ref[...].reshape(rows, width).astype(jnp.float32)
    scale = lax.rsqrt(jnp.mean(x * x, axis=1, keepdims=True) + EPSILON)
    scaled = x * scale
    for copy in copies:
        copy.wait()
    last = w_ref[:, w_ref.shape[1] - LANES :].astype(jnp.float32).T
    gains = last[HEAD : HEAD + 8, :]
    gains_ref[...] = gains
    normed = (scaled * gains[0:1, :]).astype(jnp.bfloat16)
    normed_ref[...] = normed
    cosine = jnp.concatenate([cos_ref[...]] * seqs, 0)
    sine = jnp.concatenate([sin_ref[...]] * seqs, 0)
    for t in range(0, w_ref.shape[1] // LANES):
        lo = t * LANES
        u = dot(normed, w_ref[:, lo : lo + LANES])
        if lo >= 2 * KV_WIDTH:
            at = lo - 2 * KV_WIDTH
            u = turn(u, cosine, sine).astype(jnp.bfloat16) * jnp.bfloat16(SCALE)
            q_ref[:, at : at + LANES] = u
        else:
            r = turn(u, cosine, sine)
            is_key = lane_ids(u.shape) + lo < KV_WIDTH
            kv_ref[:, lo : lo + LANES] = jnp.where(is_key, r, u).astype(jnp.bfloat16)


def project(base, inputs, cosine, sine, pieces):
    seqs, _, block, width = inputs.shape
    rows = seqs * 2 * block
    columns = pieces[0].shape[1]
    q_width = columns - 2 * KV_WIDTH
    return pl.pallas_call(
        functools.partial(project_kernel, len(pieces)),
        in_specs=[
            pl.BlockSpec(memory_space=pltpu.SMEM),
            pl.BlockSpec(memory_space=pltpu.VMEM),
            pl.BlockSpec(memory_space=pltpu.VMEM),
            pl.BlockSpec(memory_space=pltpu.VMEM),
        ]
        + [pl.BlockSpec(memory_space=pl.ANY)] * len(pieces),
        out_specs=[pl.BlockSpec(memory_space=pltpu.VMEM)] * 5,
        out_shape=[
            jax.ShapeDtypeStruct((width, columns), jnp.bfloat16),
            jax.ShapeDtypeStruct((rows, width), jnp.bfloat16),
            jax.ShapeDtypeStruct((rows, q_width), jnp.bfloat16),
            jax.ShapeDtypeStruct((rows, 2 * KV_WIDTH), jnp.bfloat16),
            jax.ShapeDtypeStruct((8, width), jnp.float32),
        ],
        scratch_shapes=[pltpu.SemaphoreType.DMA((len(pieces),))],
        compiler_params=pltpu.CompilerParams(vmem_limit_bytes=VMEM_BYTES),
        cost_estimate=pl.CostEstimate(
            flops=2 * rows * width * columns, bytes_accessed=8 * 1024 * 1024, transcendentals=0
        ),
        name="project",
    )(base, inputs, cosine, sine, *pieces)


def per_device(
    inputs, norm1_gain, q_weight, k_weight, v_weight, o_weight, norm2_gain,
    gate_weight, up_weight, down_weight, cotangent,
):
    seqs, _, block, width = inputs.shape
    rows = seqs * 2 * block
    ctx_count = lax.axis_size("ctx")
    ctx_rank = lax.axis_index("ctx")
    rank = ctx_rank.astype(jnp.int32).reshape(1)
    cosine, sine = rope_tables(ctx_rank, ctx_count, block)
    pad = 2 * HEAD - 2 * HEAD // 2
    packed = jnp.concatenate(
        [
            k_weight, v_weight, q_weight, norm1_gain[:, None], norm2_gain[:, None],
            jnp.zeros((q_weight.shape[0], pad - 2), jnp.bfloat16),
        ],
        1,
    )
    pieces, base = weight_pieces(packed, "wsh")
    base = base.astype(jnp.int32).reshape(1)
    w_all, normed, queries, kv_rows, gains = project(base, inputs, cosine, sine, pieces)
    gain_one, gain_two = gains[0:1], gains[1:2]
    queries = queries.reshape(seqs, 2, block, -1)
    pairs = lax.all_gather(
        kv_rows.reshape(seqs, 2, block, 2 * KV_WIDTH), "ctx", axis=2, tiled=True
    )
    weight_o = lax.all_gather(o_weight, "wsh", axis=0, tiled=True)
    weight_gate = lax.all_gather(gate_weight, "wsh", axis=0, tiled=True)
    weight_up = lax.all_gather(up_weight, "wsh", axis=0, tiled=True)
    weight_down = lax.all_gather(down_weight, "wsh", axis=0, tiled=True)
    attended, lse = attend(rank, queries, pairs, width)
    stream = inputs.reshape(rows, width).astype(jnp.float32)
    cot_rows = cotangent.reshape(rows, width)
    attn_rows = attended.reshape(rows, width).astype(jnp.bfloat16)
    middle = stream + dot(attn_rows, weight_o)
    scale_two = lax.rsqrt(jnp.mean(middle * middle, -1, keepdims=True) + EPSILON)
    normed_two = (middle * scale_two * gain_two).astype(jnp.bfloat16)
    gate_pre = dot(normed_two, weight_gate)
    up_pre = dot(normed_two, weight_up)
    gate_sig = jax.nn.sigmoid(gate_pre)
    gate_act = gate_pre * gate_sig
    hidden = (gate_act * up_pre).astype(jnp.bfloat16)
    output = (middle + dot(hidden, weight_down)).astype(jnp.bfloat16).reshape(inputs.shape)
    grad_down = dot(hidden, cot_rows, TN)
    grad_hidden = dot(cot_rows, weight_down, NT)
    grad_gate = (grad_hidden * up_pre * gate_sig * (1.0 + gate_pre * (1.0 - gate_sig))).astype(
        jnp.bfloat16
    )
    grad_up = (grad_hidden * gate_act).astype(jnp.bfloat16)
    grad_wgate = dot(normed_two, grad_gate, TN)
    grad_wup = dot(normed_two, grad_up, TN)
    grad_normed_two = dot(grad_gate, weight_gate, NT) + dot(grad_up, weight_up, NT)
    grad_gain_two = jnp.sum(grad_normed_two * middle * scale_two, 0)
    scaled_two = grad_normed_two * gain_two
    grad_middle = cot_rows.astype(jnp.float32) + scale_two * (
        scaled_two
        - middle * scale_two * scale_two * jnp.mean(scaled_two * middle, -1, keepdims=True)
    )

    def reduce_weight(grad):
        part = lax.psum_scatter(grad.astype(jnp.bfloat16), "wsh", scatter_dimension=0, tiled=True)
        return lax.psum(part, "ctx").astype(jnp.float32)

    grad_branch = grad_middle.astype(jnp.bfloat16)
    grad_wo = dot(attn_rows, grad_branch, TN)
    grad_attn = dot(grad_branch, weight_o, NT).astype(jnp.bfloat16)
    grad_q, grad_pairs = attend_back(
        rank, queries, pairs, grad_attn.reshape(seqs, 2, block, width), attended, lse, cosine, sine
    )
    grad_kv = lax.psum_scatter(grad_pairs, "ctx", scatter_dimension=2, tiled=True)
    grad_kv = grad_kv.reshape(seqs, 2 * block, 2 * KV_WIDTH).astype(jnp.float32)
    tile_cos = jnp.concatenate(
        [jnp.tile(cosine[:, :HEAD], (1, KV_HEADS)), jnp.ones((2 * block, KV_WIDTH))], 1
    )
    tile_sin = jnp.concatenate(
        [jnp.tile(-sine[:, :HEAD], (1, KV_HEADS)), jnp.zeros((2 * block, KV_WIDTH))], 1
    )
    lane = jnp.arange(2 * KV_WIDTH)
    partner = jnp.where(
        (lane & 32) == 0, jnp.roll(grad_kv, -32, -1), jnp.roll(grad_kv, 32, -1)
    )
    grad_kv = (grad_kv * tile_cos + partner * tile_sin).astype(jnp.bfloat16).reshape(rows, -1)
    grad_q = grad_q.reshape(rows, width)
    grad_wq = dot(normed, grad_q, TN)
    grad_wkv = dot(normed, grad_kv, TN)
    weight_kv = w_all[:, : 2 * KV_WIDTH]
    weight_q = w_all[:, 2 * KV_WIDTH : 2 * KV_WIDTH + width]
    grad_normed = dot(grad_q, weight_q, NT) + dot(grad_kv, weight_kv, NT)
    scale_one = lax.rsqrt(jnp.mean(stream * stream, -1, keepdims=True) + EPSILON)
    grad_gain_one = jnp.sum(grad_normed * stream * scale_one, 0)
    scaled_one = grad_normed * gain_one
    grad_stream = grad_middle + scale_one * (
        scaled_one
        - stream * scale_one * scale_one * jnp.mean(scaled_one * stream, -1, keepdims=True)
    )
    sum_kv = reduce_weight(grad_wkv)
    return (
        output,
        grad_stream.reshape(inputs.shape),
        reduce_weight(grad_gain_one),
        reduce_weight(grad_wq),
        sum_kv[:, :KV_WIDTH],
        sum_kv[:, KV_WIDTH:],
        reduce_weight(grad_wo),
        reduce_weight(grad_gain_two),
        reduce_weight(grad_wgate),
        reduce_weight(grad_wup),
        reduce_weight(grad_down),
    )


def solution(mesh):
    weight = P("wsh", None)
    rows = P("wsh", None, "ctx", None)
    gain = P("wsh")
    return jax.shard_map(
        per_device,
        mesh=mesh,
        in_specs=(
            rows, gain, weight, weight, weight, weight, gain, weight, weight, weight, rows,
        ),
        out_specs=(
            rows, rows, gain, weight, weight, weight, weight, gain, weight, weight, weight,
        ),
        check_vma=False,
    )
```

time: 1350 us -> 919 us (0.68)
  local copies, waits for them, and re-layouts: 441 us -> 49.9 us
  matrix products: 335 us -> 81.9 us
  waiting for transfers between devices: 414 us -> 611 us
  Pallas kernels: 0 us -> 97.9 us
  other arithmetic: 54.2 us -> 20.6 us
  blocking collectives: 55.6 us -> 29.3 us
  loops' own time: 18.3 us -> 0 us
    dot_general x139 -> x16, matrix products: 335 us -> 81.9 us  [the longest x12 57.8 us: dot(): return lax.dot_general(a, b, dims, preferred_element_type=jnp.float32)]
    slice x189 -> x4, local copies, waits for them, and re-layouts: 156 us -> 2.43 us  [the longest x2 1.47 us: per_device(): jnp.roll(grad_kv, 32, -1)]
    pallas_call x0 -> x3, Pallas kernels: none -> 97.9 us  [the longest x1 51.9 us: attend_back(): pl.pallas_call(functools.partial(attend_back_kernel, n, block), grid=(seq...]
    all_gather x6 -> x5, waiting for transfers between devices: 59.8 us -> 154 us  [the longest x1 71.9 us: per_device(): lax.all_gather(kv_rows.reshape(seqs, 2, block, 2 * KV_WIDTH), 'ctx', axis...]
    dynamic_slice x47 -> x0, local copies, waits for them, and re-layouts: 68.9 us -> none  [the longest x27 42.5 us: take_half(): return lax.dynamic_index_in_dim(stacked, my_half, 0, keepdims=False)]
    unnamed x18 -> x14, waiting for transfers between devices: 3.13 us -> 51.1 us
    reduce_scatter x5 -> x6, waiting for transfers between devices: 225 us -> 263 us  [the longest x5 197 us: reduce_weight(): lax.psum_scatter(grad.astype(jnp.bfloat16), 'wsh', scatter_dimension=0, t...]
    unnamed x149 -> x67, local copies, waits for them, and re-layouts: 63.4 us -> 28.4 us
  transfers between devices with their start and end apart: 15 -> 16, of which waited for: 7 -> 14; matrix products, arithmetic and copies ran while one was open for 39% -> 12% of each run, Pallas kernels for 0% -> 4%
where the time goes in v1:
time: 919 us; the launch traced here: 910 us
  waiting for transfers between devices  611 us (66%)
  Pallas kernels  97.9 us (11%)
  matrix products  81.9 us (9%)
  local copies, waits for them, and re-layouts  49.9 us (5%)
  blocking collectives  29.3 us (3%)
  other arithmetic  20.6 us (2%)
  between operations  15.5 us (2%)
    reduce_scatter x5, waiting for transfers between devices, reduce_weight(): lax.psum_scatter(grad.astype(jnp.bfloat16), 'wsh', scatter_dimension=0, t...  197 us
    psum x1, waiting for transfers between devices, reduce_weight(): return lax.psum(part, 'ctx').astype(jnp.float32)  126 us
    all_gather x1, waiting for transfers between devices, per_device(): lax.all_gather(kv_rows.reshape(seqs, 2, block, 2 * KV_WIDTH), 'ctx', axis...  71.9 us
    reduce_scatter x1, waiting for transfers between devices, per_device(): lax.psum_scatter(grad_pairs, 'ctx', scatter_dimension=2, tiled=True)  66.5 us
    dot_general x12, matrix products, dot(): return lax.dot_general(a, b, dims, preferred_element_type=jnp.float32)  57.8 us
    pallas_call x1, Pallas kernels, attend_back(): pl.pallas_call(functools.partial(attend_back_kernel, n, block), grid=(seq...  51.9 us
    unnamed x14, waiting for transfers between devices  51.1 us
    pallas_call x1, Pallas kernels, attend(): pl.pallas_call(functools.partial(attend_kernel, n, block), grid=(seqs,),...  37.8 us
  transfers between devices with their start and end apart: 16, of which 14 were waited for; matrix products, arithmetic and copies ran while one was open for 12% of the time, Pallas kernels for 4%

profile of v1, /device:TPU:0, one launch (start us, length us, event | category | flops | bytes accessed | tf_op | source)
XLA Modules:
  0.0 909.8 jit_solution(9133517177343969487)
XLA Ops:
  16.6 16.5 %collective-permute-done.1.refs_2_ = bf16[240,1664]{1,0:T(8,128)(2,1)S(1)} collective-permute-done((bf16[240,1664]{1,0:T(8,128)(2,1)S(1)}, bf16[240,1664]{1,0:T(8,128)(2,1)S(1)}, u32[]{:S(2)}, u32[]{:S(2)}) %collective-permute-start.1) | collective-permute-done | bytes 798752 | tf_op jit(solution)/shard_map/ppermute | solution.py:334
  36.3 8.2 project.1
  52.4 3.9 copy.70
  60.7 71.9 %all-gather.6.cloned.1.call-done.kv_ref = bf16[2,2,1024,640]{3,2,1,0:T(8,128)(2,1)} async-done(((bf16[2,2,128,640]{3,2,1,0:T(8,128)(2,1)}), bf16[2,2,1024,640]{3,2,1,0:T(8,128)(2,1)}) %all-gather.6.cloned.1.call-update) | async-done | bytes 5242896 | tf_op jit(solution)/shard_map/all_gather | solution.py:441
  132.5 37.8 %attend.1 = (f32[2,2,128,960]{3,2,1,0:T(8,128)}, f32[2,10,384]{2,1,0:T(8,128)}) custom-call(s32[1]{0:T(128)} %bitcast.rank_ref, bf16[2,2,128,1024]{3,2,1,0:T(8,128)(2,1)} %bitcast.85, bf16[2,2,1024,640]{3,2,1,0:T(8,128)(2,1)} %all-gather.6.cloned.1.call-done.kv_ref), custom_call_target="tpu_custom_call" | custom-call | flops 2139095040 | bytes 8388608 | tf_op jit(solution)/shard_map/attend/pallas_call | solution.py:169
  177.8 16.6 %all-gather.10.cloned.1.call-done = bf16[960,2560]{1,0:T(8,128)(2,1)} async-done(((bf16[240,2560]{1,0:T(8,128)(2,1)}), bf16[960,2560]{1,0:T(8,128)(2,1)}) %all-gather.10.cloned.1.call-update) | async-done | bytes 4915216 | tf_op jit(solution)/shard_map/all_gather | solution.py:445
  194.3 7.1 fusion.18
  201.4 33.0 %all-gather.12.cloned.1.call-done = bf16[960,2560]{1,0:T(8,128)(2,1)} async-done(((bf16[240,2560]{1,0:T(8,128)(2,1)}), bf16[960,2560]{1,0:T(8,128)(2,1)}) %all-gather.12.cloned.1.call-update) | async-done | bytes 4915216 | tf_op jit(solution)/shard_map/all_gather | solution.py:446
  234.4 7.0 fusion.19
  241.4 33.0 %all-gather.14.cloned.1.call-done = bf16[2560,960]{0,1:T(8,128)(2,1)} async-done(((bf16[640,960]{0,1:T(8,128)(2,1)}), bf16[2560,960]{0,1:T(8,128)(2,1)}) %all-gather.14.cloned.1.call-update) | async-done | bytes 4915216 | tf_op jit(solution)/shard_map/all_gather | solution.py:447
  274.4 10.3 %multiply_convert_fusion = (bf16[512,2560]{1,0:T(8,128)(2,1)S(1)}, bf16[512,2560]{1,0:T(8,128)(2,1)S(1)}, bf16[512,2560]{1,0:T(8,128)(2,1)}) fusion(f32[512,2560]{1,0:T(8,128)} %fusion.18, f32[512,2560]{1,0:T(8,128)} %fusion.19, bf16[512,960]{0,1:T(8,128)(2,1)S(1)} %copy-done.9, bf16[2560,960]{0,1:T(8,128)(2,1)} %all-gather.14.cloned.1.call-done), kind=kOutput, calls=%fused_computation.3 | convolution fusion | flops 2536243200 | bytes 24248320 | tf_op jit(solution)/shard_map/dot_general | solution.py:29
  284.6 6.6 fusion.20
  300.6 51.9 %attend_back.1 = (bf16[2,2,128,960]{3,2,1,0:T(8,128)(2,1)}, bf16[2,2,1024,640]{3,2,1,0:T(8,128)(2,1)}) custom-call(s32[1]{0:T(128)} %bitcast.rank_ref, bf16[2,2,128,1024]{3,2,1,0:T(8,128)(2,1)} %bitcast.86, bf16[2,2,1024,640]{3,2,1,0:T(8,128)(2,1)} %all-gather.6.cloned.1.call-done.kv_ref, bf16[2,2,128,960]{3,2,1,0:T(8,128)(2,1)} %bitcast.72, ...), custom_call_target="tpu_custom_call" | custom-call | flops 5347737600 | bytes 16777216 | tf_op jit(solution)/shard_map/attend_back/pallas_call | solution.py:288
  352.6 6.1 convolution_convert_fusion
  358.7 7.9 copy.80
  366.7 4.0 convolution_convert_fusion.4
  370.8 4.5 convolution_convert_fusion.3
  375.4 6.1 convolution_convert_fusion.2
  381.6 6.2 convolution_convert_fusion.1
  388.8 66.5 %reduce-scatter.10.cloned.1.call-done = bf16[2,2,128,640]{3,2,1,0:T(8,128)(2,1)} async-done(((bf16[2,2,1024,640]{3,2,1,0:T(8,128)(2,1)}), bf16[2,2,128,640]{3,2,1,0:T(8,128)(2,1)}) %reduce-scatter.10.cloned.1.call-update) | async-done | bytes 655376 | tf_op jit(solution)/shard_map/reduce_scatter | solution.py:487
  460.5 48.5 %reduce-scatter.22.cloned.1.call-done = bf16[640,960]{1,0:T(8,128)(2,1)} async-done(((bf16[2560,960]{1,0:T(8,128)(2,1)}), bf16[640,960]{1,0:T(8,128)(2,1)}) %reduce-scatter.22.cloned.1.call-update) | async-done | bytes 1228816
  511.7 31.3 %reduce-scatter.12.cloned.1.call-done = bf16[240,960]{1,0:T(8,128)(2,1)} async-done(((bf16[960,960]{1,0:T(8,128)(2,1)}), bf16[240,960]{1,0:T(8,128)(2,1)}) %reduce-scatter.12.cloned.1.call-update) | async-done | bytes 460816 | tf_op jit(solution)/shard_map/reduce_scatter | solution.py:478
  543.0 33.3 %reduce-scatter.16.cloned.1.call-done = bf16[240,960]{1,0:T(8,128)(2,1)} async-done(((bf16[960,960]{1,0:T(8,128)(2,1)}), bf16[240,960]{1,0:T(8,128)(2,1)}) %reduce-scatter.16.cloned.1.call-update) | async-done | bytes 460816 | tf_op jit(solution)/shard_map/reduce_scatter | solution.py:478
  576.3 51.8 %reduce-scatter.18.cloned.1.call-done = bf16[240,2560]{1,0:T(8,128)(2,1)} async-done(((bf16[960,2560]{1,0:T(8,128)(2,1)}), bf16[240,2560]{1,0:T(8,128)(2,1)}) %reduce-scatter.18.cloned.1.call-update) | async-done | bytes 1228816 | tf_op jit(solution)/shard_map/reduce_scatter | solution.py:478
  628.1 51.8 %reduce-scatter.20.cloned.1.call-done = bf16[240,2560]{1,0:T(8,128)(2,1)} async-done(((bf16[960,2560]{1,0:T(8,128)(2,1)}), bf16[240,2560]{1,0:T(8,128)(2,1)}) %reduce-scatter.20.cloned.1.call-update) | async-done | bytes 1228816 | tf_op jit(solution)/shard_map/reduce_scatter | solution.py:478
  679.9 28.7 %reduce-scatter.14.cloned.1.call-done = bf16[240,640]{1,0:T(8,128)(2,1)} async-done(((bf16[960,640]{1,0:T(8,128)(2,1)}), bf16[240,640]{1,0:T(8,128)(2,1)}) %reduce-scatter.14.cloned.1.call-update) | async-done | bytes 307216 | tf_op jit(solution)/shard_map/reduce_scatter | solution.py:478
  710.7 6.9 add_convert_fusion
  724.1 4.0 multiply_reduce_fusion.1
  728.1 6.6 all-reduce.6
  734.8 22.7 %all-reduce.4 = (bf16[240]{0:T(256)(128)(2,1)S(1)}, bf16[240]{0:T(256)(128)(2,1)S(1)}) all-reduce(bf16[240]{0:T(256)(128)(2,1)S(1)} %dynamic-slice.1, bf16[240]{0:T(256)(128)(2,1)S(1)} %dynamic-slice.3), channel_id=1, replica_groups=mesh['ctx'=8,'wsh'=4] {'ctx'}, use_global_device_ids=true, to_apply=%region_7.8 | all-reduce | flops 480 | bytes 1920 | tf_op jit(solution)/shard_map/psum | solution.py:479
  758.7 4.0 multiply_add_fusion
  766.6 125.8 %all-reduce.9.cloned.1.call-done = (bf16[240,640]{1,0:T(8,128)(2,1)}, bf16[240,960]{1,0:T(8,128)(2,1)}, bf16[240,960]{1,0:T(8,128)(2,1)}, bf16[240,2560]{1,0:T(8...) async-done(((bf16[240,640]{1,0:T(8,128)(2,1)}, bf16[240,960]{1,0:T(8,128)(2,1)}, bf16[240,960]{1,0:T(8,128)(2,1)}, bf16[240,2560]{1,0:T(8,128)(2,1)}, ...) | async-done | bytes 4915216 | tf_op jit(solution)/shard_map/psum | solution.py:479
  (147 shorter events, 74.0 us)
Async XLA Ops:
  7.2 8.2 copy-start.1
  7.2 125.4 %all-gather.6.cloned.1.call-start = ((), (), s32[]{:S(2)}) async-start(), calls=%async_computation.7 | async-start | bytes 5898240 | tf_op jit(solution)/shard_map/all_gather | solution.py:441
  12.3 23.1 %copy-start.15 = (bf16[240,1664]{1,0:T(8,128)(2,1)}, bf16[240,1664]{1,0:T(8,128)(2,1)S(1)}, u32[]{:S(2)}) copy-start(bf16[240,1664]{1,0:T(8,128)(2,1)S(1)} %concatenate.49.refs_0_) | copy-start | bytes 2396164
  12.3 20.8 %collective-permute-start.1 = (bf16[240,1664]{1,0:T(8,128)(2,1)S(1)}, bf16[240,1664]{1,0:T(8,128)(2,1)S(1)}, u32[]{:S(2)}, u32[]{:S(2)}) collective-permute-start(bf16[240,1664]{1,0:T(8,128)(2,1)S(1)} %concatenate.49.refs_0_), channel_id=1, source_target_pairs={{0,2},{1,3},{2,0},{3,1},{4,6},{5,7},{6,4},{7,5},{8,10},{9,11},{10,... | collective-permute-start | bytes 2396168 | tf_op jit(solution)/shard_map/ppermute | solution.py:334
  15.3 20.1 %collective-permute-start = (bf16[240,1664]{1,0:T(8,128)(2,1)S(1)}, bf16[240,1664]{1,0:T(8,128)(2,1)}, u32[]{:S(2)}, u32[]{:S(2)}) collective-permute-start(bf16[240,1664]{1,0:T(8,128)(2,1)S(1)} %concatenate.49.refs_0_), channel_id=1, source_target_pairs={{0,1},{1,0},{2,3},{3,2},{4,5},{5,4},{6,7},{7,6},{8,9},{9,8},{10,11... | collective-permute-start | bytes 2396168 | tf_op jit(solution)/shard_map/ppermute | solution.py:334
  33.1 2.3 copy-start.20
  33.1 2.3 collective-permute-start.2
  44.5 128.5 %all-gather.8.cloned.1.call-start = ((), (), s32[]{:S(2)}) async-start(), calls=%async_computation.8 | async-start | bytes 2457600 | tf_op jit(solution)/shard_map/all_gather | solution.py:444
  45.3 149.1 %all-gather.10.cloned.1.call-start = ((), (), s32[]{:S(2)}) async-start(), calls=%async_computation.9 | async-start | bytes 6144000 | tf_op jit(solution)/shard_map/all_gather | solution.py:445
  46.0 188.4 %all-gather.12.cloned.1.call-start = ((), (), s32[]{:S(2)}) async-start(), calls=%async_computation.10 | async-start | bytes 6144000 | tf_op jit(solution)/shard_map/all_gather | solution.py:446
  46.6 227.8 %all-gather.14.cloned.1.call-start = ((), (), s32[]{:S(2)}) async-start(), calls=%async_computation.11 | async-start | bytes 6144000 | tf_op jit(solution)/shard_map/all_gather | solution.py:447
  47.2 408.1 %reduce-scatter.10.cloned.1.call-start = ((), (), s32[]{:S(2)}) async-start(), calls=%async_computation.12 | async-start | bytes 5898240 | tf_op jit(solution)/shard_map/reduce_scatter | solution.py:487
  52.4 120.7 %copy-start.2 = (f32[512,960]{0,1:T(8,128)}, f32[512,960]{0,1:T(8,128)S(1)}, u32[]{:S(2)}) copy-start(f32[512,960]{0,1:T(8,128)S(1)} %reshape.138) | copy-start | bytes 5898244
  201.4 72.9 %copy-start.9 = (bf16[512,960]{0,1:T(8,128)(2,1)S(1)}, bf16[512,960]{0,1:T(8,128)(2,1)}, u32[]{:S(2)}) copy-start(bf16[512,960]{0,1:T(8,128)(2,1)} %reshape.134) | copy-start | bytes 2949124
  284.6 6.6 copy-start.25
  284.6 6.6 copy-start.24
  284.6 6.6 copy-start.6
  284.6 6.6 copy-start.8
  294.4 1.8 copy-start.19
  352.6 156.4 %reduce-scatter.22.cloned.1.call-start = ((), (), s32[]{:S(2)}) async-start(), calls=%async_computation.18 | async-start | bytes 6553600
  366.6 176.4 %reduce-scatter.12.cloned.1.call-start = ((), (), s32[]{:S(2)}) async-start(), calls=%async_computation.13 | async-start | bytes 2457600 | tf_op jit(solution)/shard_map/reduce_scatter | solution.py:478
  370.7 205.5 %reduce-scatter.16.cloned.1.call-start = ((), (), s32[]{:S(2)}) async-start(), calls=%async_computation.15 | async-start | bytes 2457600 | tf_op jit(solution)/shard_map/reduce_scatter | solution.py:478
  375.4 252.7 %reduce-scatter.18.cloned.1.call-start = ((), (), s32[]{:S(2)}) async-start(), calls=%async_computation.16 | async-start | bytes 6144000 | tf_op jit(solution)/shard_map/reduce_scatter | solution.py:478
  381.6 298.4 %reduce-scatter.20.cloned.1.call-start = ((), (), s32[]{:S(2)}) async-start(), calls=%async_computation.17 | async-start | bytes 6144000 | tf_op jit(solution)/shard_map/reduce_scatter | solution.py:478
  387.8 320.8 %reduce-scatter.14.cloned.1.call-start = ((), (), s32[]{:S(2)}) async-start(), calls=%async_computation.14 | async-start | bytes 1536000 | tf_op jit(solution)/shard_map/reduce_scatter | solution.py:478
  460.5 431.9 %all-reduce.9.cloned.1.call-start = ((), (), s32[]{:S(2)}) async-start(), calls=%async_computation.19 | async-start | bytes 9953280 | tf_op jit(solution)/shard_map/psum | solution.py:479
  708.6 2.1 copy-start.7
  720.2 3.9 copy-start.18
  721.2 2.8 copy-start.3
  892.4 3.1 copy-start.14
  898.8 1.9 copy-start.17
  898.8 2.9 copy-start.16
  (10 other events, 12.3 us)
Sparse Core Ops, SparseCore 0:
  44.6 87.8 all-gather.5
  134.1 20.0 all-gather.7
  155.7 38.5 all-gather.9
  195.8 38.5 all-gather.11
  235.8 38.5 all-gather.13
  352.7 102.5 reduce-scatter.9
  457.8 51.1 reduce-scatter.21
  512.3 30.6 reduce-scatter.11
  545.6 30.6 reduce-scatter.15
  578.9 49.1 reduce-scatter.17
  630.7 49.1 reduce-scatter.19
  682.5 26.0 reduce-scatter.13
  713.1 179.2 all-reduce.8

commit v2 on v1

--- a/solution.py
+++ b/solution.py
@@ -81,10 +81,40 @@
     return jnp.concatenate(parts, 0)
 
 
-def attend_kernel(n, block, rank_ref, q_ref, kv_ref, o_ref, lse_ref, qs, wide, narrow, top, total, acc):
+def fetch_pairs(n, block, seq, owners_ref, pieces, kv_ref, sems):
+    if len(pieces) == 1:
+        return [pltpu.make_async_copy(pieces[0].at[seq], kv_ref, sems.at[0])]
+    side = n // 2
+    copies = []
+    for i, piece in enumerate(pieces):
+        place = i if i < side else n + side - 1 - i if i < n - 1 else side
+        rows = pl.ds(pl.multiple_of(owners_ref[place] * block, block), block)
+        target = kv_ref.at[:, rows] if i < n - 1 else kv_ref.at[i - (n - 1), rows]
+        copies.append(pltpu.make_async_copy(piece.at[seq], target, sems.at[i]))
+    return copies
+
+
+def attend_kernel(n, block, count, rank_ref, owners_ref, q_ref, *refs):
+    o_ref, lse_ref, kv_ref, qs, wide, narrow, top, total, acc, sems = refs[count:]
     c = rank_ref[0]
     rows = GROUPS * block
     pair = 2 * block
+    seq = pl.program_id(0)
+    seqs = kv_ref.shape[0]
+
+    @pl.when(seq == 0)
+    def _():
+        for b in range(seqs):
+            for copy in fetch_pairs(n, block, b, owners_ref, refs[:count], kv_ref.at[b], sems.at[b]):
+                copy.start()
+
+    for b in range(seqs):
+
+        @pl.when(seq == b)
+        def _():
+            for copy in fetch_pairs(n, block, b, owners_ref, refs[:count], kv_ref.at[b], sems.at[b]):
+                copy.wait()
+
     q_at = lax.broadcasted_iota(jnp.int32, (rows, block), 0) % block
     k_at = lax.broadcasted_iota(jnp.int32, (rows, block), 1)
     causal = k_at <= q_at
@@ -98,7 +128,7 @@
         top[...] = jnp.full_like(top, MASKED)
 
         def wide_scores(i, carry):
-            s = dot(qs[1], kv_ref[0, 0, pl.ds(i * pair, pair), kl], NT)
+            s = dot(qs[1], kv_ref[seq, 0, pl.ds(i * pair, pair), kl], NT)
             wide[i] = s
             top[1] = jnp.maximum(top[1], jnp.maximum(s[:, :block], s[:, block:]))
             return carry
@@ -107,14 +137,14 @@
 
         def narrow_scores(d, carry):
             sel = (d > c).astype(jnp.int32)
-            s = dot(qs[sel], kv_ref[0, sel, pl.ds(d * block, block), kl], NT)
+            s = dot(qs[sel], kv_ref[seq, sel, pl.ds(d * block, block), kl], NT)
             s = jnp.where(jnp.logical_or(causal, d != c), s, MASKED)
             narrow[d] = s
             top[sel] = jnp.maximum(top[sel], s)
             return carry
 
         lax.fori_loop(0, n, narrow_scores, 0, unroll=unroll)
-        s = dot(qs[1], kv_ref[0, 1, pl.ds(c * block, block), kl], NT)
+        s = dot(qs[1], kv_ref[seq, 1, pl.ds(c * block, block), kl], NT)
         s = jnp.where(causal, s, MASKED)
         narrow[n] = s
         top[1] = jnp.maximum(top[1], s)
@@ -132,7 +162,7 @@
             pb = jnp.exp(s[:, block:] - t)
             total[1] += pa + pb
             p = jnp.concatenate([pa, pb], 1).astype(jnp.bfloat16)
-            acc[1] += dot(p, kv_ref[0, 0, pl.ds(i * pair, pair), vl])
+            acc[1] += dot(p, kv_ref[seq, 0, pl.ds(i * pair, pair), vl])
             return carry
 
         lax.fori_loop(0, n // 2, wide_sums, 0, unroll=2)
@@ -141,13 +171,13 @@
             sel = (d > c).astype(jnp.int32)
             p = jnp.exp(narrow[d] - top[sel])
             total[sel] += p
-            acc[sel] += dot(p.astype(jnp.bfloat16), kv_ref[0, sel, pl.ds(d * block, block), vl])
+            acc[sel] += dot(p.astype(jnp.bfloat16), kv_ref[seq, sel, pl.ds(d * block, block), vl])
             return carry
 
         lax.fori_loop(0, n, narrow_sums, 0, unroll=unroll)
         p = jnp.exp(narrow[n] - top[1])
         total[1] += p
-        acc[1] += dot(p.astype(jnp.bfloat16), kv_ref[0, 1, pl.ds(c * block, block), vl])
+        acc[1] += dot(p.astype(jnp.bfloat16), kv_ref[seq, 1, pl.ds(c * block, block), vl])
         for half in range(2):
             whole = jnp.broadcast_to(jnp.sum(total[half], axis=1, keepdims=True), (rows, LANES))
             out = acc[half] / whole
@@ -162,49 +192,59 @@
                 o_ref[0, half, :, lo : lo + HEAD] = value[:, (j % 2) * HEAD : (j % 2 + 1) * HEAD]
 
 
-def attend(rank, queries, pairs, width):
+def attend(rank, owners, queries, pieces, width):
     seqs, _, block, q_width = queries.shape
-    n = pairs.shape[2] // block
+    n = owners.shape[0]
     rows = GROUPS * block
+    count = len(pieces)
+    here = lambda i: (i, 0, 0, 0)
     return pl.pallas_call(
-        functools.partial(attend_kernel, n, block),
+        functools.partial(attend_kernel, n, block, count),
         grid=(seqs,),
         in_specs=[
             pl.BlockSpec(memory_space=pltpu.SMEM),
-            pl.BlockSpec((1, 2, block, q_width), lambda b: (b, 0, 0, 0)),
-            pl.BlockSpec((1, 2, n * block, 2 * KV_WIDTH), lambda b: (b, 0, 0, 0)),
-        ],
+            pl.BlockSpec(memory_space=pltpu.SMEM),
+            pl.BlockSpec((1, 2, block, q_width), here),
+        ]
+        + [pl.BlockSpec(memory_space=pl.ANY)] * count,
         out_specs=[
-            pl.BlockSpec((1, 2, block, width), lambda b: (b, 0, 0, 0)),
-            pl.BlockSpec((1, 2 * KV_HEADS, rows), lambda b: (b, 0, 0)),
+            pl.BlockSpec((1, 2, block, width), here),
+            pl.BlockSpec((1, 2 * KV_HEADS, rows), lambda i: (i, 0, 0)),
         ],
         out_shape=[
             jax.ShapeDtypeStruct((seqs, 2, block, width), jnp.float32),
             jax.ShapeDtypeStruct((seqs, 2 * KV_HEADS, rows), jnp.float32),
         ],
         scratch_shapes=[
+            pltpu.VMEM((seqs, 2, n * block, 2 * KV_WIDTH), jnp.bfloat16),
             pltpu.VMEM((2, rows, LANES), jnp.bfloat16),
             pltpu.VMEM((n // 2, rows, 2 * block), jnp.float32),
             pltpu.VMEM((n + 1, rows, block), jnp.float32),
             pltpu.VMEM((2, rows, LANES), jnp.float32),
             pltpu.VMEM((2, rows, LANES), jnp.float32),
             pltpu.VMEM((2, rows, LANES), jnp.float32),
+            pltpu.SemaphoreType.DMA((seqs, count)),
         ],
         compiler_params=pltpu.CompilerParams(vmem_limit_bytes=VMEM_BYTES),
         cost_estimate=pl.CostEstimate(
-            flops=4 * seqs * HEADS * block * block * HEAD * (2 * n + 1),
-            bytes_accessed=8 * 1024 * 1024,
-            transcendentals=seqs * HEADS * block * block * (2 * n + 1),
+            flops=4 * seqs * HEADS * block * block * HEAD * (2 * n + 1) * 8,
+            bytes_accessed=4 * 1024 * 1024,
+            transcendentals=HEADS * block * block * (2 * n + 1),
         ),
         name="attend",
-    )(rank, queries, pairs)
+    )(rank, owners, queries, *pieces)
 
 
 def attend_back_kernel(
-    n, block, rank_ref, q_ref, kv_ref, do_ref, o_ref, lse_ref, cos_ref, sin_ref,
-    dq_ref, dkv_ref, qs, dos, inner, dqt, dkv, dq_full,
+    n, block, count, seq, rank_ref, owners_ref, q_ref, do_ref, o_ref, lse_ref, cos_ref, sin_ref, *refs
 ):
+    dq_ref, dkv_ref, kv_ref, qs, dos, inner, dqt, dkv, dq_full, sems = refs[count:]
     c = rank_ref[0]
+    copies = fetch_pairs(n, block, seq, owners_ref, refs[:count], kv_ref.at[0], sems)
+    for copy in copies:
+        copy.start()
+    for copy in copies:
+        copy.wait()
     rows = GROUPS * block
     pair = 2 * block
     width = do_ref.shape[-1]
@@ -275,71 +315,75 @@
             ).astype(jnp.bfloat16)
             hi = min((t + 1) * LANES, width)
             dq_ref[0, half, :, t * LANES : hi] = value[:, : hi - t * LANES]
-    dkv_ref[0] = dkv[...].astype(jnp.bfloat16)
-
-
-def attend_back(rank, queries, pairs, grad_attn, attended, lse, cosine, sine):
-    seqs, _, block, q_width = queries.shape
+    for place in range(n):
+        at = pl.multiple_of(owners_ref[place] * block, block)
+        dkv_ref[place] = dkv[:, pl.ds(at, block), :].astype(jnp.bfloat16)
+
+
+def attend_back(rank, owners, queries, pieces, seq, grad_attn, attended, lse, cosine, sine):
+    _, _, block, q_width = queries.shape
     width = grad_attn.shape[-1]
-    n = pairs.shape[2] // block
+    n = owners.shape[0]
     rows = GROUPS * block
-    whole4 = lambda b: (b, 0, 0, 0)
-    buffers = pl.Buffered(2 if n <= 8 else 1)
+    count = len(pieces)
+    there = lambda i: (seq, 0, 0, 0)
+    here = lambda i: (0, 0, 0, 0)
     return pl.pallas_call(
-        functools.partial(attend_back_kernel, n, block),
-        grid=(seqs,),
+        functools.partial(attend_back_kernel, n, block, count, seq),
+        grid=(1,),
         in_specs=[
             pl.BlockSpec(memory_space=pltpu.SMEM),
-            pl.BlockSpec((1, 2, block, q_width), whole4),
-            pl.BlockSpec((1, 2, n * block, 2 * KV_WIDTH), whole4, pipeline_mode=buffers),
-            pl.BlockSpec((1, 2, block, width), whole4),
-            pl.BlockSpec((1, 2, block, width), whole4),
-            pl.BlockSpec((1, 2 * KV_HEADS, rows), lambda b: (b, 0, 0)),
-            pl.BlockSpec((2 * block, LANES), lambda b: (0, 0)),
-            pl.BlockSpec((2 * block, LANES), lambda b: (0, 0)),
-        ],
+            pl.BlockSpec(memory_space=pltpu.SMEM),
+            pl.BlockSpec((1, 2, block, q_width), there),
+            pl.BlockSpec((1, 2, block, width), there),
+            pl.BlockSpec((1, 2, block, width), there),
+            pl.BlockSpec((1, 2 * KV_HEADS, rows), lambda i: (seq, 0, 0)),
+            pl.BlockSpec((2 * block, LANES), lambda i: (0, 0)),
+            pl.BlockSpec((2 * block, LANES), lambda i: (0, 0)),
+        ]
+        + [pl.BlockSpec(memory_space=pl.ANY)] * count,
         out_specs=[
-            pl.BlockSpec((1, 2, block, width), whole4),
-            pl.BlockSpec((1, 2, n * block, 2 * KV_WIDTH), whole4, pipeline_mode=buffers),
+            pl.BlockSpec((1, 2, block, width), here),
+            pl.BlockSpec((n, 2, block, 2 * KV_WIDTH), here, pipeline_mode=pl.Buffered(1)),
         ],
         out_shape=[
-            jax.ShapeDtypeStruct((seqs, 2, block, width), jnp.bfloat16),
-            jax.ShapeDtypeStruct((seqs, 2, n * block, 2 * KV_WIDTH), jnp.bfloat16),
+            jax.ShapeDtypeStruct((1, 2, block, width), jnp.bfloat16),
+            jax.ShapeDtypeStruct((n, 2, block, 2 * KV_WIDTH), jnp.bfloat16),
         ],
         scratch_shapes=[
+            pltpu.VMEM((1, 2, n * block, 2 * KV_WIDTH), jnp.bfloat16),
             pltpu.VMEM((2, rows, LANES), jnp.bfloat16),
             pltpu.VMEM((2, rows, LANES), jnp.bfloat16),
             pltpu.VMEM((2, 1, rows), jnp.float32),
             pltpu.VMEM((2, LANES, rows), jnp.float32),
             pltpu.VMEM((2, n * block, 2 * KV_WIDTH), jnp.float32),
             pltpu.VMEM((2, block, q_width), jnp.float32),
+            pltpu.SemaphoreType.DMA((count,)),
         ],
         compiler_params=pltpu.CompilerParams(vmem_limit_bytes=VMEM_BYTES),
         cost_estimate=pl.CostEstimate(
-            flops=10 * seqs * HEADS * block * block * HEAD * (2 * n + 1),
-            bytes_accessed=16 * 1024 * 1024,
-            transcendentals=seqs * HEADS * block * block * (2 * n + 1),
+            flops=10 * HEADS * block * block * HEAD * (2 * n + 1) * 8,
+            bytes_accessed=8 * 1024 * 1024,
+            transcendentals=HEADS * block * block * (2 * n + 1),
         ),
         name="attend_back",
-    )(rank, queries, pairs, grad_attn, attended, lse, cosine, sine)
-
-
-def pieces_of(shard, axis):
-    count = lax.axis_size(axis)
-    found = {0: shard}
-    bit = count // 2
-    while bit:
-        swap = [(i, i ^ bit) for i in range(count)]
-        for p in list(found):
-            found[p ^ bit] = lax.ppermute(found[p], axis, swap)
-        bit //= 2
-    return [found[p] for p in range(count)]
-
-
-def weight_pieces(shard, axis):
-    if shard.shape[0] % 16 == 0:
-        return pieces_of(shard, axis), lax.axis_index(axis)
-    return [lax.all_gather(shard, axis, axis=0, tiled=True)], jnp.int32(0)
+    )(rank, owners, queries, grad_attn, attended, lse, cosine, sine, *pieces)
+
+
+def follow(value, *others):
+    return lax.optimization_barrier((value,) + others)[0]
+
+
+def swap_over(value, axis, bit):
+    return lax.ppermute(value, axis, [(i, i ^ bit) for i in range(lax.axis_size(axis))])
+
+
+def whole_weights(shard, dimension=0):
+    return [lax.all_gather(shard, "wsh", axis=dimension, tiled=True)]
+
+
+def near_pieces(shard, far):
+    return [shard, swap_over(shard, "wsh", 1), far, swap_over(far, "wsh", 1)]
 
 
 def fetch(pieces, target, base, sems):
@@ -415,114 +459,545 @@
     )(base, inputs, cosine, sine, *pieces)
 
 
+def padded_rows(height, count):
+    return -(-height // 256) * 256 if count > 1 and height % 128 else height
+
+
+def send_out(source, targets, base, sems, column=0):
+    count = 1 if len(targets) == 1 else 4
+    height, width = source.shape[0] // count, source.shape[1]
+    rows = targets[0].shape[0]
+    copies = []
+    for p in range(count):
+        target = targets[2] if p % 2 else targets[p // 2]
+        row = rows if p == 3 else 0
+        at = pl.multiple_of(jnp.bitwise_xor(base, p) * height, 16)
+        copy = pltpu.make_async_copy(
+            source.at[pl.ds(at, height)],
+            target.at[pl.ds(row, height), pl.ds(column, width)],
+            sems.at[p],
+        )
+        copy.start()
+        copies.append(copy)
+    return copies
+
+
+def piece_shapes(height, width, count):
+    rows = padded_rows(height // count, count)
+    shapes = [rows] if count == 1 else [rows, rows, 2 * rows]
+    return [jax.ShapeDtypeStruct((row, width), jnp.bfloat16) for row in shapes]
+
+
+def as_column(row):
+    return jnp.broadcast_to(row, (LANES, row.shape[1])).T
+
+
+def feed_body(count, step, base_ref, x_ref, cot_ref, gains_ref, *refs):
+    refs = list(refs)
+
+    def take(k):
+        got = refs[:k]
+        del refs[:k]
+        return got
+
+    attended = take(1)[0]
+    outs = 1 if count == 1 else 3
+    o_in, gate_in, up_in, down_in = take(count), take(count), take(count), take(count)
+    out_ref, middle_grad_ref, attn_grad_ref = take(3)
+    gate_out, up_out = take(outs), take(outs)
+    down_out = take(1) if count == 1 else up_out
+    w_o, w_gate, w_up, w_down, g_o, g_gate, g_up, g_down = take(8)
+    attn, middle, n2, n2t, cott, total, back, sems, down_sems = take(9)
+    base = base_ref[0]
+    copies_o = fetch(o_in, w_o, base, sems.at[0])
+    copies_gate = fetch(gate_in, w_gate, base, sems.at[1])
+    copies_up = fetch(up_in, w_up, base, sems.at[2])
+    copies_down = []
+    for p, piece in enumerate(down_in):
+        part = piece.shape[1]
+        at = pl.multiple_of(jnp.bitwise_xor(base, p) * part, LANES)
+        copies_down.append(
+            pltpu.make_async_copy(piece, w_down.at[:, pl.ds(at, part)], sems.at[3, p])
+        )
+        copies_down[-1].start()
+    rows, width = attn.shape
+    gain = gains_ref[1:2, :]
+    attn[...] = attended[...].reshape(rows, width).astype(jnp.bfloat16)
+    for copy in copies_o:
+        copy.wait()
+    mid = x_ref[...].reshape(rows, width).astype(jnp.float32) + dot(attn[...], w_o[...])
+    middle[...] = mid
+    scale = lax.rsqrt(jnp.mean(mid * mid, axis=1, keepdims=True) + EPSILON)
+    normed = (mid * scale * gain).astype(jnp.bfloat16)
+    n2[...] = normed
+    n2t[...] = normed.T
+    cott[...] = cot_ref[...].reshape(rows, width).T
+    total[...] = jnp.zeros_like(total)
+    back[...] = jnp.zeros_like(back)
+    for copy in copies_gate + copies_up + copies_down:
+        copy.wait()
+
+    def chunk(f, carry):
+        at = pl.multiple_of(f * step, step)
+        cols = pl.ds(at, step)
+        cot = cot_ref[...].reshape(rows, width)
+        gate = dot(n2[...], w_gate[:, cols])
+        up = dot(n2[...], w_up[:, cols])
+        grad_hidden = dot(cot, w_down[:, cols])
+        sig = jax.nn.sigmoid(gate)
+        act = gate * sig
+        hidden = (act * up).astype(jnp.bfloat16)
+        grad_gate = (grad_hidden * up * (sig * (1.0 + gate * (1.0 - sig)))).astype(jnp.bfloat16)
+        grad_up = (grad_hidden * act).astype(jnp.bfloat16)
+        total[...] += dot(hidden, w_down[:, cols], NT)
+        g_down[:, cols] = dot(cott[...], hidden).astype(jnp.bfloat16)
+        g_gate[:, cols] = dot(n2t[...], grad_gate).astype(jnp.bfloat16)
+        g_up[:, cols] = dot(n2t[...], grad_up).astype(jnp.bfloat16)
+        back[...] += dot(grad_gate, w_gate[:, cols], NT) + dot(grad_up, w_up[:, cols], NT)
+        return carry
+
+    lax.fori_loop(0, w_gate.shape[1] // step, chunk, 0)
+    copies = send_out(g_gate, gate_out, base, sems.at[1])
+    copies += send_out(g_up, up_out, base, sems.at[2])
+    if count == 1:
+        copies += send_out(g_down, down_out, base, down_sems)
+    else:
+        part, height = g_down.shape[1] // count, width // count
+        for p in range(count):
+            target = up_out[2] if p % 2 else up_out[p // 2]
+            row = up_out[0].shape[0] if p == 3 else 0
+            at = pl.multiple_of(jnp.bitwise_xor(base, p) * part, LANES)
+            for k in range(count):
+                copy = pltpu.make_async_copy(
+                    g_down.at[pl.ds(k * height, height), pl.ds(at, part)],
+                    target.at[pl.ds(row, height), pl.ds(g_up.shape[1] + k * part, part)],
+                    down_sems.at[p * count + k],
+                )
+                copy.start()
+                copies.append(copy)
+    mid = middle[...]
+    scale = lax.rsqrt(jnp.mean(mid * mid, axis=1, keepdims=True) + EPSILON)
+    out_ref[...] = (mid + total[...]).astype(jnp.bfloat16).reshape(out_ref.shape)
+    grad = back[...]
+    gain_grad = jnp.sum(grad * mid * scale, axis=0, keepdims=True)
+    u = grad * gain
+    grad_middle = cot_ref[...].reshape(rows, width).astype(jnp.float32) + scale * (
+        u - mid * scale * scale * jnp.mean(u * mid, axis=1, keepdims=True)
+    )
+    middle_grad_ref[...] = grad_middle
+    branch = grad_middle.astype(jnp.bfloat16)
+    attn_grad_ref[...] = (
+        dot(branch, w_o[...], NT).astype(jnp.bfloat16).reshape(attn_grad_ref.shape)
+    )
+    g_o[:, :width] = dot(attn[...], branch, TN).astype(jnp.bfloat16)
+    column = as_column(gain_grad).astype(jnp.bfloat16)
+    g_o[:, width:] = column[:, : g_o.shape[1] - width]
+    copies += send_out(g_o, gate_out, base, sems.at[0], g_gate.shape[1])
+    for copy in copies:
+        copy.wait()
+
+
+def feed(base, inputs, cotangent, gains, attended, o_in, gate_in, up_in, down_in):
+    seqs, _, block, width = inputs.shape
+    rows = seqs * 2 * block
+    count = len(o_in)
+    units = gate_in[0].shape[1]
+    wide = width + HEAD
+    outs = 1 if count == 1 else 3
+    vmem = pl.BlockSpec(memory_space=pltpu.VMEM)
+    hbm = pl.BlockSpec(memory_space=pl.ANY)
+    bf, f32 = jnp.bfloat16, jnp.float32
+    out = pl.pallas_call(
+        functools.partial(feed_body, count, 256),
+        in_specs=[pl.BlockSpec(memory_space=pltpu.SMEM)]
+        + [vmem] * 4
+        + [hbm] * (4 * count),
+        out_specs=[vmem] * 3 + [hbm] * (3 if count == 1 else 6),
+        out_shape=[
+            jax.ShapeDtypeStruct(inputs.shape, bf),
+            jax.ShapeDtypeStruct((rows, width), f32),
+            jax.ShapeDtypeStruct(inputs.shape, bf),
+        ]
+        + piece_shapes(width, units + wide, count)
+        + (
+            piece_shapes(width, units, 1) * 2
+            if count == 1
+            else piece_shapes(width, 2 * units, count)
+        ),
+        scratch_shapes=[
+            pltpu.VMEM((width, width), bf),
+            pltpu.VMEM((width, units), bf),
+            pltpu.VMEM((width, units), bf),
+            pltpu.VMEM((width, units), bf),
+            pltpu.VMEM((width, wide), bf),
+            pltpu.VMEM((width, units), bf),
+            pltpu.VMEM((width, units), bf),
+            pltpu.VMEM((width, units), bf),
+            pltpu.VMEM((rows, width), bf),
+            pltpu.VMEM((rows, width), f32),
+            pltpu.VMEM((rows, width), bf),
+            pltpu.VMEM((width, rows), bf),
+            pltpu.VMEM((width, rows), bf),
+            pltpu.VMEM((rows, width), f32),
+            pltpu.VMEM((rows, width), f32),
+            pltpu.SemaphoreType.DMA((4, count)),
+            pltpu.SemaphoreType.DMA((count * count,)),
+        ],
+        compiler_params=pltpu.CompilerParams(vmem_limit_bytes=VMEM_BYTES + 4 * 1024 * 1024),
+        cost_estimate=pl.CostEstimate(
+            flops=2 * rows * width * (9 * units + 3 * width),
+            bytes_accessed=48 * 1024 * 1024,
+            transcendentals=rows * units,
+        ),
+        name="feed",
+    )(base, inputs, cotangent, gains, attended, *o_in, *gate_in, *up_in, *down_in)
+    k = 3
+    return out[0], out[1], out[2], out[k:]
+
+
+def query_kernel(count, seqs, base_ref, normed_ref, w_ref, *refs):
+    dq_in, part_ref, outs, g_q, sems = (
+        refs[:seqs], refs[seqs], refs[seqs + 1 : -2], refs[-2], refs[-1],
+    )
+    rows, width = normed_ref.shape
+    dq = jnp.concatenate([r[...].reshape(rows // seqs, width) for r in dq_in], 0)
+    g_q[:, :width] = dot(normed_ref[...], dq, TN).astype(jnp.bfloat16)
+    g_q[:, width:] = jnp.zeros((width, g_q.shape[1] - width), jnp.bfloat16)
+    copies = send_out(g_q, outs, base_ref[0], sems)
+    part_ref[...] = dot(dq, w_ref[:, 2 * KV_WIDTH : 2 * KV_WIDTH + width], NT)
+    for copy in copies:
+        copy.wait()
+
+
+def query_grads(count, base, normed, w_all, grad_queries):
+    rows, width = normed.shape
+    seqs = len(grad_queries)
+    vmem = pl.BlockSpec(memory_space=pltpu.VMEM)
+    out = pl.pallas_call(
+        functools.partial(query_kernel, count, seqs),
+        in_specs=[pl.BlockSpec(memory_space=pltpu.SMEM)] + [vmem] * (2 + seqs),
+        out_specs=[vmem] + [pl.BlockSpec(memory_space=pl.ANY)] * (1 if count == 1 else 3),
+        out_shape=[jax.ShapeDtypeStruct((rows, width), jnp.float32)]
+        + piece_shapes(width, width + HEAD, count),
+        scratch_shapes=[
+            pltpu.VMEM((width, width + HEAD), jnp.bfloat16),
+            pltpu.SemaphoreType.DMA((count,)),
+        ],
+        compiler_params=pltpu.CompilerParams(vmem_limit_bytes=VMEM_BYTES),
+        cost_estimate=pl.CostEstimate(
+            flops=4 * rows * width * width, bytes_accessed=10 * 1024 * 1024, transcendentals=0
+        ),
+        name="query_grads",
+    )(base, normed, w_all, *grad_queries)
+    return out[0], out[1:]
+
+
+def finish_kernel(
+    count, seqs, base_ref, x_ref, normed_ref, w_ref, part_ref, middle_grad_ref, gains_ref,
+    cos_ref, sin_ref, *refs,
+):
+    dkv_in, out_ref, outs, g_kv, sems = (
+        refs[:seqs], refs[seqs], refs[seqs + 1 : -2], refs[-2], refs[-1],
+    )
+    rows, width = normed_ref.shape
+    columns = 2 * KV_WIDTH
+    dkv = jnp.concatenate([r[...].reshape(rows // seqs, columns) for r in dkv_in], 0)
+    cosine = jnp.concatenate([cos_ref[...]] * seqs, 0)
+    sine = -jnp.concatenate([sin_ref[...]] * seqs, 0)
+    tiles = []
+    for lo in range(0, columns, LANES):
+        u = dkv[:, lo : lo + LANES]
+        if lo < KV_WIDTH:
+            u = jnp.where(lane_ids(u.shape) + lo < KV_WIDTH, turn(u, cosine, sine), u)
+        tiles.append(u.astype(jnp.bfloat16))
+    dkv = jnp.concatenate(tiles, 1)
+    x = x_ref[...].reshape(rows, width).astype(jnp.float32)
+    scale = lax.rsqrt(jnp.mean(x * x, axis=1, keepdims=True) + EPSILON)
+    grad = part_ref[...] + dot(dkv, w_ref[:, :columns], NT)
+    g_kv[:, :columns] = dot(normed_ref[...], dkv, TN).astype(jnp.bfloat16)
+    gain_grad = jnp.sum(grad * x * scale, axis=0, keepdims=True)
+    g_kv[:, columns:] = as_column(gain_grad).astype(jnp.bfloat16)
+    copies = send_out(g_kv, outs, base_ref[0], sems)
+    u = grad * gains_ref[0:1, :]
+    out_ref[...] = (
+        middle_grad_ref[...]
+        + scale * (u - x * scale * scale * jnp.mean(u * x, axis=1, keepdims=True))
+    ).reshape(out_ref.shape)
+    for copy in copies:
+        copy.wait()
+
+
+def finish(count, base, inputs, normed, w_all, part, middle_grad, gains, cosine, sine, grad_pairs):
+    rows, width = normed.shape
+    seqs = len(grad_pairs)
+    vmem = pl.BlockSpec(memory_space=pltpu.VMEM)
+    out = pl.pallas_call(
+        functools.partial(finish_kernel, count, seqs),
+        in_specs=[pl.BlockSpec(memory_space=pltpu.SMEM)] + [vmem] * (8 + seqs),
+        out_specs=[vmem] + [pl.BlockSpec(memory_space=pl.ANY)] * (1 if count == 1 else 3),
+        out_shape=[jax.ShapeDtypeStruct(inputs.shape, jnp.float32)]
+        + piece_shapes(width, 2 * KV_WIDTH + LANES, count),
+        scratch_shapes=[
+            pltpu.VMEM((width, 2 * KV_WIDTH + LANES), jnp.bfloat16),
+            pltpu.SemaphoreType.DMA((count,)),
+        ],
+        compiler_params=pltpu.CompilerParams(vmem_limit_bytes=VMEM_BYTES),
+        cost_estimate=pl.CostEstimate(
+            flops=8 * rows * width * KV_WIDTH, bytes_accessed=14 * 1024 * 1024, transcendentals=0
+        ),
+        name="finish",
+    )(base, inputs, normed, w_all, part, middle_grad, gains, cosine, sine, *grad_pairs)
+    return out[0], out[1:]
+
+
+def added(*values):
+    total = values[0].astype(jnp.float32)
+    for value in values[1:]:
+        total = total + value.astype(jnp.float32)
+    return total.astype(jnp.bfloat16)
+
+
+def core_sums(group):
+    if len(group) == 1:
+        return group
+    kept, passed, sent = group
+    rows = kept.shape[0]
+    came = swap_over(sent, "wsh", 1)
+    return [added(kept, came[:rows]), added(passed, came[rows:])]
+
+
+def far_sums(group):
+    return added(group[0], swap_over(group[1], "wsh", 2))
+
+
+def rank_bits():
+    count = lax.axis_size("ctx")
+    return [1 << i for i in range(count.bit_length() - 1)]
+
+
+def split_sums(mine):
+    rank = lax.axis_index("ctx")
+    bits = rank_bits()
+    for bit in bits:
+        half = mine.shape[0] // 2
+        upper = ((rank & bit) != 0).astype(jnp.int32)
+        sent = lax.dynamic_slice_in_dim(mine, (1 - upper) * half, half, 0)
+        kept = lax.dynamic_slice_in_dim(mine, upper * half, half, 0)
+        mine = added(kept, swap_over(sent, "ctx", bit))
+    for bit in reversed(bits):
+        upper = (rank & bit) != 0
+        other = swap_over(mine, "ctx", bit)
+        mine = jnp.concatenate([jnp.where(upper, other, mine), jnp.where(upper, mine, other)], 0)
+    return mine
+
+
+def whole_sums(mine):
+    for bit in rank_bits():
+        mine = added(mine, swap_over(mine, "ctx", bit))
+    return mine
+
+
+def plain_sums(grad, dimension=0):
+    part = lax.psum_scatter(grad, "wsh", scatter_dimension=dimension, tiled=True)
+    return lax.psum(part, "ctx")
+
+
+def ring_order(n):
+    return [0, 2, 4, 6, 7, 5, 3, 1] if n == 8 else list(range(n))
+
+
+def ring_steps(n):
+    order = ring_order(n)
+    onward = [(order[i], order[(i + 1) % n]) for i in range(n)]
+    return onward, [(b, a) for a, b in onward]
+
+
+def ring_owners(n, rank):
+    order = jnp.array(ring_order(n), jnp.int32)
+    steps = jnp.arange(n, dtype=jnp.int32)
+    place = jnp.sum(jnp.where(order == rank, steps, 0))
+    hit = ((place + steps) % n)[:, None] == steps[None, :]
+    return jnp.sum(jnp.where(hit, order[None, :], 0), -1).astype(jnp.int32)
+
+
+def ring_gather(own, n, beside):
+    onward, backward = ring_steps(n)
+    ahead, behind = [own], [own]
+    side = n // 2
+    for step in range(1, side):
+        one = lax.ppermute(behind[-1], "ctx", onward)
+        two = lax.ppermute(ahead[-1], "ctx", backward)
+        if step in beside:
+            one, two, beside[step] = lax.optimization_barrier((one, two, beside[step]))
+        else:
+            one, two = lax.optimization_barrier((one, two))
+        behind.append(one)
+        ahead.append(two)
+    one = lax.ppermute(behind[-1][:, 0], "ctx", onward)
+    two = lax.ppermute(ahead[-1][:, 1], "ctx", backward)
+    if side in beside:
+        one, two, beside[side] = lax.optimization_barrier((one, two, beside[side]))
+    return ahead + behind[1:] + [one, two]
+
+
+def ring_sums(terms, n, beside):
+    onward, backward = ring_steps(n)
+    side = n // 2
+
+    def term(k, half=None):
+        if half is None:
+            return jnp.stack([one[k] for one in terms])
+        return jnp.stack([one[k, half] for one in terms])
+
+    one = lax.ppermute(term(side, 0), "ctx", onward)
+    two = lax.ppermute(term(side, 1), "ctx", backward)
+    one, two = lax.optimization_barrier((one, two))
+    up = jnp.stack([added(term(side - 1, 0), one), term(side - 1, 1)], 1)
+    down = jnp.stack([term(n - side + 1, 0), added(term(n - side + 1, 1), two)], 1)
+    for k in range(side - 1, 0, -1):
+        up = lax.ppermute(up, "ctx", onward)
+        down = lax.ppermute(down, "ctx", backward)
+        if k in beside:
+            up, down, beside[k] = lax.optimization_barrier((up, down, beside[k]))
+        else:
+            up, down = lax.optimization_barrier((up, down))
+        if k > 1:
+            up = added(up, term(k - 1))
+            down = added(down, term(n - k + 1))
+    return term(0).astype(jnp.float32) + up.astype(jnp.float32) + down.astype(jnp.float32)
+
+
 def per_device(
     inputs, norm1_gain, q_weight, k_weight, v_weight, o_weight, norm2_gain,
     gate_weight, up_weight, down_weight, cotangent,
 ):
     seqs, _, block, width = inputs.shape
     rows = seqs * 2 * block
-    ctx_count = lax.axis_size("ctx")
+    n = lax.axis_size("ctx")
     ctx_rank = lax.axis_index("ctx")
     rank = ctx_rank.astype(jnp.int32).reshape(1)
-    cosine, sine = rope_tables(ctx_rank, ctx_count, block)
-    pad = 2 * HEAD - 2 * HEAD // 2
+    owners = ring_owners(n, ctx_rank)
+    cosine, sine = rope_tables(ctx_rank, n, block)
     packed = jnp.concatenate(
         [
             k_weight, v_weight, q_weight, norm1_gain[:, None], norm2_gain[:, None],
-            jnp.zeros((q_weight.shape[0], pad - 2), jnp.bfloat16),
+            jnp.zeros((q_weight.shape[0], HEAD - 2), jnp.bfloat16),
         ],
         1,
     )
-    pieces, base = weight_pieces(packed, "wsh")
-    base = base.astype(jnp.int32).reshape(1)
+    split = packed.shape[0] % 16 == 0 and lax.axis_size("wsh") == 4
+    ringed = n <= 8
+    if split:
+        pieces = near_pieces(packed, swap_over(packed, "wsh", 2))
+    else:
+        pieces = whole_weights(packed)
+    count = len(pieces)
+    base = lax.axis_index("wsh").astype(jnp.int32) if count > 1 else jnp.int32(0)
+    base = base.reshape(1)
     w_all, normed, queries, kv_rows, gains = project(base, inputs, cosine, sine, pieces)
-    gain_one, gain_two = gains[0:1], gains[1:2]
     queries = queries.reshape(seqs, 2, block, -1)
-    pairs = lax.all_gather(
-        kv_rows.reshape(seqs, 2, block, 2 * KV_WIDTH), "ctx", axis=2, tiled=True
+    beside = {}
+    if split:
+        far_o = swap_over(follow(o_weight, pieces[2]), "wsh", 2)
+        kv_rows, far_o = lax.optimization_barrier((kv_rows, far_o))
+        far_gate = swap_over(follow(gate_weight, far_o), "wsh", 2)
+        far_up = swap_over(follow(up_weight, far_gate), "wsh", 2)
+        far_down = swap_over(follow(down_weight.T, far_up), "wsh", 2)
+        beside = {2: far_gate, 4: far_up}
+    kv_rows = kv_rows.reshape(seqs, 2, block, 2 * KV_WIDTH)
+    if ringed:
+        pairs = ring_gather(kv_rows, n, beside)
+    else:
+        pairs = [lax.all_gather(kv_rows, "ctx", axis=2, tiled=True)]
+    attended, lse = attend(rank, owners, queries, pairs, width)
+    if split:
+        attended, far_down = lax.optimization_barrier((attended, far_down))
+        o_in = near_pieces(o_weight, far_o)
+        gate_in = near_pieces(gate_weight, beside[2])
+        up_in = near_pieces(up_weight, beside[4])
+        down_in = near_pieces(down_weight.T, far_down)
+    else:
+        o_in, gate_in, up_in = [whole_weights(w) for w in (o_weight, gate_weight, up_weight)]
+        down_in = whole_weights(down_weight.T, 1)
+    output, middle_grad, attn_grad, groups = feed(
+        base, inputs, cotangent, gains, attended, o_in, gate_in, up_in, down_in
     )
-    weight_o = lax.all_gather(o_weight, "wsh", axis=0, tiled=True)
-    weight_gate = lax.all_gather(gate_weight, "wsh", axis=0, tiled=True)
-    weight_up = lax.all_gather(up_weight, "wsh", axis=0, tiled=True)
-    weight_down = lax.all_gather(down_weight, "wsh", axis=0, tiled=True)
-    attended, lse = attend(rank, queries, pairs, width)
-    stream = inputs.reshape(rows, width).astype(jnp.float32)
-    cot_rows = cotangent.reshape(rows, width)
-    attn_rows = attended.reshape(rows, width).astype(jnp.bfloat16)
-    middle = stream + dot(attn_rows, weight_o)
-    scale_two = lax.rsqrt(jnp.mean(middle * middle, -1, keepdims=True) + EPSILON)
-    normed_two = (middle * scale_two * gain_two).astype(jnp.bfloat16)
-    gate_pre = dot(normed_two, weight_gate)
-    up_pre = dot(normed_two, weight_up)
-    gate_sig = jax.nn.sigmoid(gate_pre)
-    gate_act = gate_pre * gate_sig
-    hidden = (gate_act * up_pre).astype(jnp.bfloat16)
-    output = (middle + dot(hidden, weight_down)).astype(jnp.bfloat16).reshape(inputs.shape)
-    grad_down = dot(hidden, cot_rows, TN)
-    grad_hidden = dot(cot_rows, weight_down, NT)
-    grad_gate = (grad_hidden * up_pre * gate_sig * (1.0 + gate_pre * (1.0 - gate_sig))).astype(
-        jnp.bfloat16
+    units = gate_weight.shape[1]
+    beside = {}
+    if split:
+        kept_b, pass_b = core_sums(groups[:3])
+        kept_a, passed, sent = groups[3:]
+        came = swap_over(sent, "wsh", 1)
+        tall = kept_a.shape[0]
+        pass_up = added(passed[:, :units], came[tall:, :units])
+        pass_down = added(passed[:, units:], came[tall:, units:])
+        far_up = swap_over(pass_up, "wsh", 2)
+        far_down = swap_over(follow(pass_down, far_up), "wsh", 2)
+        far_b = swap_over(follow(pass_b, far_down), "wsh", 2)
+        beside = {3: far_down, 1: far_b}
+    grad_queries, terms = [], []
+    for b in range(seqs):
+        at = follow(rank, pass_up, pass_down, pass_b) if split and b else rank
+        grad_q, term = attend_back(
+            at, owners, queries, pairs, b, attn_grad, attended, lse, cosine, sine
+        )
+        grad_queries.append(grad_q)
+        terms.append(term)
+    if ringed:
+        if split:
+            terms[-1], far_up = lax.optimization_barrier((terms[-1], far_up))
+        summed = list(ring_sums(terms, n, beside))
+    else:
+        summed = []
+        for term in terms:
+            ordered = jnp.zeros_like(term).at[owners].set(term)
+            part = lax.psum_scatter(ordered, "ctx", scatter_dimension=0, tiled=False)
+            summed.append(part.astype(jnp.float32))
+    part, q_group = query_grads(count, base, normed, w_all, grad_queries)
+    if split:
+        mine = jnp.concatenate(
+            [
+                added(kept_a[:, :units], came[:tall, :units], far_up),
+                added(kept_a[:, units:], came[:tall, units:], beside[3]),
+            ],
+            1,
+        )
+        sum_a = split_sums(mine).astype(jnp.float32)
+        sum_q = far_sums(core_sums(q_group))
+        sum_b = split_sums(jnp.concatenate([added(kept_b, beside[1]), sum_q], 1)).astype(jnp.float32)
+        sum_gate, sum_q = sum_b, sum_b[:, units + width + HEAD :]
+        sum_up = sum_a
+        height = width // count
+        per = units // count
+        sum_down = jnp.concatenate(
+            [sum_a[:height, units + k * per : units + (k + 1) * per] for k in range(count)], 0
+        ).T
+    else:
+        sum_gate = plain_sums(groups[0]).astype(jnp.float32)
+        sum_up = plain_sums(groups[1]).astype(jnp.float32)
+        sum_down = plain_sums(groups[2], 1).astype(jnp.float32).T
+        sum_q = plain_sums(q_group[0]).astype(jnp.float32)
+    input_grad, kv_group = finish(
+        count, base, inputs, normed, w_all, part, middle_grad, gains, cosine, sine, summed
     )
-    grad_up = (grad_hidden * gate_act).astype(jnp.bfloat16)
-    grad_wgate = dot(normed_two, grad_gate, TN)
-    grad_wup = dot(normed_two, grad_up, TN)
-    grad_normed_two = dot(grad_gate, weight_gate, NT) + dot(grad_up, weight_up, NT)
-    grad_gain_two = jnp.sum(grad_normed_two * middle * scale_two, 0)
-    scaled_two = grad_normed_two * gain_two
-    grad_middle = cot_rows.astype(jnp.float32) + scale_two * (
-        scaled_two
-        - middle * scale_two * scale_two * jnp.mean(scaled_two * middle, -1, keepdims=True)
-    )
-
-    def reduce_weight(grad):
-        part = lax.psum_scatter(grad.astype(jnp.bfloat16), "wsh", scatter_dimension=0, tiled=True)
-        return lax.psum(part, "ctx").astype(jnp.float32)
-
-    grad_branch = grad_middle.astype(jnp.bfloat16)
-    grad_wo = dot(attn_rows, grad_branch, TN)
-    grad_attn = dot(grad_branch, weight_o, NT).astype(jnp.bfloat16)
-    grad_q, grad_pairs = attend_back(
-        rank, queries, pairs, grad_attn.reshape(seqs, 2, block, width), attended, lse, cosine, sine
-    )
-    grad_kv = lax.psum_scatter(grad_pairs, "ctx", scatter_dimension=2, tiled=True)
-    grad_kv = grad_kv.reshape(seqs, 2 * block, 2 * KV_WIDTH).astype(jnp.float32)
-    tile_cos = jnp.concatenate(
-        [jnp.tile(cosine[:, :HEAD], (1, KV_HEADS)), jnp.ones((2 * block, KV_WIDTH))], 1
-    )
-    tile_sin = jnp.concatenate(
-        [jnp.tile(-sine[:, :HEAD], (1, KV_HEADS)), jnp.zeros((2 * block, KV_WIDTH))], 1
-    )
-    lane = jnp.arange(2 * KV_WIDTH)
-    partner = jnp.where(
-        (lane & 32) == 0, jnp.roll(grad_kv, -32, -1), jnp.roll(grad_kv, 32, -1)
-    )
-    grad_kv = (grad_kv * tile_cos + partner * tile_sin).astype(jnp.bfloat16).reshape(rows, -1)
-    grad_q = grad_q.reshape(rows, width)
-    grad_wq = dot(normed, grad_q, TN)
-    grad_wkv = dot(normed, grad_kv, TN)
-    weight_kv = w_all[:, : 2 * KV_WIDTH]
-    weight_q = w_all[:, 2 * KV_WIDTH : 2 * KV_WIDTH + width]
-    grad_normed = dot(grad_q, weight_q, NT) + dot(grad_kv, weight_kv, NT)
-    scale_one = lax.rsqrt(jnp.mean(stream * stream, -1, keepdims=True) + EPSILON)
-    grad_gain_one = jnp.sum(grad_normed * stream * scale_one, 0)
-    scaled_one = grad_normed * gain_one
-    grad_stream = grad_middle + scale_one * (
-        scaled_one
-        - stream * scale_one * scale_one * jnp.mean(scaled_one * stream, -1, keepdims=True)
-    )
-    sum_kv = reduce_weight(grad_wkv)
+    if split:
+        sum_kv = whole_sums(far_sums(core_sums(kv_group))).astype(jnp.float32)
+    else:
+        sum_kv = plain_sums(kv_group[0]).astype(jnp.float32)
+    height = norm1_gain.shape[0]
+    columns = 2 * KV_WIDTH
     return (
         output,
-        grad_stream.reshape(inputs.shape),
-        reduce_weight(grad_gain_one),
-        reduce_weight(grad_wq),
-        sum_kv[:, :KV_WIDTH],
-        sum_kv[:, KV_WIDTH:],
-        reduce_weight(grad_wo),
-        reduce_weight(grad_gain_two),
-        reduce_weight(grad_wgate),
-        reduce_weight(grad_wup),
-        reduce_weight(grad_down),
+        input_grad,
+        sum_kv[:height, columns],
+        sum_q[:height, :width],
+        sum_kv[:height, :KV_WIDTH],
+        sum_kv[:height, KV_WIDTH:columns],
+        sum_gate[:height, units : units + width],
+        sum_gate[:height, units + width],
+        sum_gate[:height, :units],
+        sum_up[:height, :units],
+        sum_down,
     )
 
 

time: 919 us -> 541 us (0.59)
  waiting for transfers between devices: 611 us -> 236 us
  matrix products: 81.9 us -> 0 us
  Pallas kernels: 97.9 us -> 163 us
  starting transfers between devices: 3.53 us -> 57.6 us
  blocking collectives: 29.3 us -> 0 us
  other arithmetic: 20.6 us -> 42.9 us
  local copies, waits for them, and re-layouts: 49.9 us -> 33.2 us
  between operations: 15.5 us -> 1.56 us
    reduce_scatter x6 -> x0, waiting for transfers between devices: 263 us -> none  [the longest x5 197 us: reduce_weight(): lax.psum_scatter(grad.astype(jnp.bfloat16), 'wsh', scatter_dimension=0, t...]
    ppermute x3 -> x55, waiting for transfers between devices: 16.6 us -> 236 us  [the longest x39 148 us: swap_over(): lax.ppermute(value, axis, [(i, i ^ bit) for i in range(lax.axis_size(axis...]
    all_gather x5 -> x0, waiting for transfers between devices: 154 us -> none  [the longest x1 71.9 us: per_device(): lax.all_gather(kv_rows.reshape(seqs, 2, block, 2 * KV_WIDTH), 'ctx', axis...]
    psum x1 -> x0, waiting for transfers between devices: 126 us -> none  [reduce_weight(): return lax.psum(part, 'ctx').astype(jnp.float32)]
    dot_general x16 -> x0, matrix products: 81.9 us -> none  [the longest x12 57.8 us: dot(): return lax.dot_general(a, b, dims, preferred_element_type=jnp.float32)]
    pallas_call x2 -> x6, Pallas kernels: 89.7 us -> 155 us  [the longest x2 56.8 us: attend_back(): pl.pallas_call(functools.partial(attend_back_kernel, n, block, count, seq...]
    ppermute x3 -> x55, starting transfers between devices: 3.01 us -> 57.6 us  [the longest x39 40.8 us: swap_over(): lax.ppermute(value, axis, [(i, i ^ bit) for i in range(lax.axis_size(axis...]
    unnamed x14 -> x0, waiting for transfers between devices: 51.1 us -> none
  transfers between devices with their start and end apart: 16 -> 55, of which waited for: 14 -> 29; matrix products, arithmetic and copies ran while one was open for 12% -> 11% of each run, Pallas kernels for 4% -> 22%
where the time goes in v2:
time: 541 us; the launch traced here: 534 us
  waiting for transfers between devices  236 us (44%)
  Pallas kernels  163 us (30%)
  starting transfers between devices  57.6 us (11%)
  other arithmetic  42.9 us (8%)
  local copies, waits for them, and re-layouts  33.2 us (6%)
    ppermute x39, waiting for transfers between devices, swap_over(): lax.ppermute(value, axis, [(i, i ^ bit) for i in range(lax.axis_size(axis...  148 us
    pallas_call x2, Pallas kernels, attend_back(): pl.pallas_call(functools.partial(attend_back_kernel, n, block, count, seq...  56.8 us
    ppermute x3, waiting for transfers between devices, ring_sums(): down = lax.ppermute(down, 'ctx', backward)  55 us
    pallas_call x1, Pallas kernels, feed(): pl.pallas_call(functools.partial(feed_body, count, 256), in_specs=[pl.Blo...  43.7 us
    ppermute x39, starting transfers between devices, swap_over(): lax.ppermute(value, axis, [(i, i ^ bit) for i in range(lax.axis_size(axis...  40.8 us
    pallas_call x1, Pallas kernels, attend(): pl.pallas_call(functools.partial(attend_kernel, n, block, count), grid=(s...  38.6 us
    convert_element_type x20, other arithmetic, added(): return total.astype(jnp.bfloat16)  22.3 us
    ppermute x3, waiting for transfers between devices, ring_gather(): one = lax.ppermute(behind[-1], 'ctx', onward)  16.6 us
  transfers between devices with their start and end apart: 55, of which 29 were waited for; matrix products, arithmetic and copies ran while one was open for 11% of the time, Pallas kernels for 22%

profile of v2, /device:TPU:0, one launch (start us, length us, event | category | flops | bytes accessed | tf_op | source)
XLA Modules:
  0.0 534.4 jit_solution(12225007384505272878)
XLA Ops:
  5.8 3.0 collective-permute-start.1
  8.8 17.8 %collective-permute-done.1.refs_2_ = bf16[240,1664]{1,0:T(8,128)(2,1)S(1)} collective-permute-done((bf16[240,1664]{1,0:T(8,128)(2,1)S(1)}, bf16[240,1664]{1,0:T(8,128)(2,1)S(1)}, u32[]{:S(2)}, u32[]{:S(2)}) %collective-permute-start.1) | collective-permute-done | bytes 798752 | tf_op jit(solution)/shard_map/ppermute | solution.py:378
  32.0 8.3 %project.1 = (bf16[960,1664]{1,0:T(8,128)(2,1)}, bf16[512,960]{1,0:T(8,128)(2,1)}, bf16[512,1024]{1,0:T(8,128)(2,1)}, bf16[512,640]{1,0:T(8,128)(2,1)}, f32[8,960]{1,0:T(8,128)}) custom-call(s32[1]{0:T(128)} %bitcast.base_ref, bf16[2,2,128,960]{3,2,1,0:T(8,128)(2,1)} %copy.132.x_ref, f32[256,128]{1,0:T(8,128)} %pad_maximum_fusion.9.cos_ref, ...), custom_call_target="tpu_custom_call" | custom-call | flops 1635778560 | bytes 8388608 | tf_op jit(solution)/shard_map/project/pallas_call | solution.py:436
  45.6 12.8 %collective-permute-done.4 = bf16[2,2,128,640]{3,2,0,1:T(8,128)(2,1)S(1)} collective-permute-done((bf16[2,2,128,640]{3,2,0,1:T(8,128)(2,1)S(1)}, bf16[2,2,128,640]{3,2,0,1:T(8,128)(2,1)S(1)}, u32[]{:S(2)}, u32[]{:S(2)}) %collective-permute-start.4) | collective-permute-done | bytes 655392 | tf_op jit(solution)/shard_map/ppermute | solution.py:828
  61.8 10.5 %collective-permute-done.8.refs_7_ = bf16[240,2560]{1,0:T(8,128)(2,1)} collective-permute-done((bf16[240,2560]{1,0:T(8,128)(2,1)S(1)}, bf16[240,2560]{1,0:T(8,128)(2,1)}, u32[]{:S(2)}, u32[]{:S(2)}) %collective-permute-start.8) | collective-permute-done | bytes 1228832 | tf_op jit(solution)/shard_map/ppermute | solution.py:378
  72.3 2.8 collective-permute-done.6
  80.3 10.2 %collective-permute-done.10 = bf16[2,2,128,640]{3,2,0,1:T(8,128)(2,1)S(1)} collective-permute-done((bf16[2,2,128,640]{3,2,0,1:T(8,128)(2,1)S(1)}, bf16[2,2,128,640]{3,2,0,1:T(8,128)(2,1)S(1)}, u32[]{:S(2)}, u32[]{:S(2)}) %collective-permute-start.10) | collective-permute-done | bytes 655392 | tf_op jit(solution)/shard_map/ppermute | solution.py:829
  105.7 38.6 %attend.1 = (f32[2,2,128,960]{3,2,1,0:T(8,128)}, f32[2,10,384]{2,1,0:T(8,128)}) custom-call(s32[1]{0:T(128)} %bitcast.1.rank_ref, s32[8]{0:T(128)} %select_reduce_fusion.owners_ref, bf16[2,2,128,1024]{3,2,1,0:T(8,128)(2,1)} %bitcast.54, bf16[2,2,128,640]{3,2,1,0:T(8,128)(2,1)} %bitcast.48, bf16[2,2,128,640]{3,2,1,0:T(8,128)(2,1)} %copy.126.refs_1_, ...), custom_call_target="tpu_custom_call" | custom-call | flops 17112760320 | bytes 4194304 | tf_op jit(solution)/shard_map/attend/pallas_call | solution.py:201
  151.8 43.7 %feed.1 = (bf16[2,2,128,960]{3,2,1,0:T(8,128)(2,1)}, f32[512,960]{1,0:T(8,128)}, bf16[2,2,128,960]{3,2,1,0:T(8,128)(2,1)}, bf16[256,3584]{1,0:T(8,128)(2,1)}, bf...) custom-call(s32[1]{0:T(128)} %bitcast.base_ref, ...), custom_call_target="tpu_custom_call" | custom-call | flops 25480396800 | bytes 50331648 | tf_op jit(solution)/shard_map/feed/pallas_call | solution.py:610
  196.1 28.5 %attend_back.2 = (bf16[1,2,128,960]{3,2,1,0:T(8,128)(2,1)}, bf16[8,2,128,640]{3,2,1,0:T(8,128)(2,1)}) custom-call(s32[1]{0:T(128)} %bitcast.1.rank_ref, s32[8]{0:T(128)} %select_reduce_fusion.owners_ref, bf16[2,2,128,1024]{3,2,1,0:T(8,128)(2,1)} %bitcast.55, bf16[2,2,128,960]{3,2,1,0:T(8,128)(2,1)} %get-tuple-element.97.do_ref, ...), custom_call_target="tpu_custom_call" | custom-call | flops 21390950400 | bytes 8388608 | tf_op jit(solution)/shard_map/attend_back/pallas_call | solution.py:331
  226.6 3.3 add_convert_fusion.2
  229.9 2.4 add_convert_fusion.6
  233.1 28.3 %attend_back.3 = (bf16[1,2,128,960]{3,2,1,0:T(8,128)(2,1)}, bf16[8,2,128,640]{3,2,1,0:T(8,128)(2,1)}) custom-call(s32[1]{0:T(128)} %bitcast.1.rank_ref, s32[8]{0:T(128)} %select_reduce_fusion.owners_ref, bf16[2,2,128,1024]{3,2,1,0:T(8,128)(2,1)} %bitcast.56, bf16[2,2,128,960]{3,2,1,0:T(8,128)(2,1)} %get-tuple-element.97.do_ref, ...), custom_call_target="tpu_custom_call" | custom-call | flops 21390950400 | bytes 8388608 | tf_op jit(solution)/shard_map/attend_back/pallas_call | solution.py:331
  266.8 6.3 %query_grads.1 = (f32[512,960]{1,0:T(8,128)}, bf16[256,1024]{1,0:T(8,128)(2,1)}, bf16[256,1024]{1,0:T(8,128)(2,1)}, bf16[512,1024]{1,0:T(8,128)(2,1)}) custom-call(s32[1]{0:T(128)} %bitcast.base_ref, bf16[512,960]{1,0:T(8,128)(2,1)} %get-tuple-element.95.normed_ref, bf16[960,1664]{1,0:T(8,128)(2,1)} %get-tuple-element.96.w_ref, ...), custom_call_target="tpu_custom_call" | custom-call | flops 1887436800 | bytes 10485760 | tf_op jit(solution)/shard_map/query_grads/pallas_call | solution.py:676
  281.2 9.9 %collective-permute-done.29 = bf16[2,2,128,640]{3,2,1,0:T(8,128)(2,1)S(1)} collective-permute-done((bf16[2,2,128,640]{3,2,1,0:T(8,128)(2,1)S(1)}, bf16[2,2,128,640]{3,2,1,0:T(8,128)(2,1)S(1)}, u32[]{:S(2)}, u32[]{:S(2)}) %collective-permute-start.29) | collective-permute-done | bytes 655392 | tf_op jit(solution)/shard_map/ppermute | solution.py:859
  291.7 13.1 %collective-permute-done.30 = bf16[256,2560]{1,0:T(8,128)(2,1)S(1)} collective-permute-done((bf16[256,2560]{1,0:T(8,128)(2,1)S(1)}, bf16[256,2560]{1,0:T(8,128)(2,1)S(1)}, u32[]{:S(2)}, u32[]{:S(2)}) %collective-permute-start.30) | collective-permute-done | bytes 1310752 | tf_op jit(solution)/shard_map/ppermute | solution.py:378
  304.8 2.7 add_convert_fusion.4
  318.3 32.7 %collective-permute-done.32 = bf16[2,2,128,640]{3,2,1,0:T(8,128)(2,1)} collective-permute-done((bf16[2,2,128,640]{3,2,1,0:T(8,128)(2,1)}, bf16[2,2,128,640]{3,2,1,0:T(8,128)(2,1)}, u32[]{:S(2)}, u32[]{:S(2)}) %collective-permute-start.32) | collective-permute-done | bytes 655392 | tf_op jit(solution)/shard_map/ppermute | solution.py:859
  359.8 12.4 %collective-permute-done.34 = bf16[2,2,128,640]{3,2,1,0:T(8,128)(2,1)S(1)} collective-permute-done((bf16[2,2,128,640]{3,2,1,0:T(8,128)(2,1)S(1)}, bf16[2,2,128,640]{3,2,1,0:T(8,128)(2,1)S(1)}, u32[]{:S(2)}, u32[]{:S(2)}) %collective-permute-start.34) | collective-permute-done | bytes 655392 | tf_op jit(solution)/shard_map/ppermute | solution.py:859
  375.2 9.5 %collective-permute-done.50 = bf16[64,5120]{1,0:T(8,128)(2,1)S(1)} collective-permute-done((bf16[64,5120]{1,0:T(8,128)(2,1)S(1)}, bf16[64,5120]{1,0:T(8,128)(2,1)S(1)}, u32[]{:S(2)}, u32[]{:S(2)}) %collective-permute-start.50) | collective-permute-done | bytes 655392 | tf_op jit(solution)/shard_map/ppermute | solution.py:378
  386.9 5.1 collective-permute-start.43
  392.2 6.7 %collective-permute-done.51 = bf16[32,5120]{1,0:T(8,128)(2,1)S(1)} collective-permute-done((bf16[32,5120]{1,0:T(8,128)(2,1)S(1)}, bf16[32,5120]{1,0:T(8,128)(2,1)S(1)}, u32[]{:S(2)}, u32[]{:S(2)}) %collective-permute-start.51) | collective-permute-done | bytes 327712 | tf_op jit(solution)/shard_map/ppermute | solution.py:378
  400.2 9.1 %finish.1 = (f32[2,2,128,960]{3,2,1,0:T(8,128)}, bf16[256,768]{1,0:T(8,128)(2,1)}, bf16[256,768]{1,0:T(8,128)(2,1)}, bf16[512,768]{1,0:T(8,128)(2,1)}) custom-call(s32[1]{0:T(128)} %bitcast.base_ref, bf16[2,2,128,960]{3,2,1,0:T(8,128)(2,1)} %copy.132.x_ref, bf16[512,960]{1,0:T(8,128)(2,1)} %get-tuple-element.95.normed_ref, ...), custom_call_target="tpu_custom_call" | custom-call | flops 1258291200 | bytes 14680064 | tf_op jit(solution)/shard_map/finish/pallas_call | solution.py:734
  409.4 2.9 copy.148
  415.9 10.9 %collective-permute-start.44 = (bf16[64,4608]{1,0:T(8,128)(2,1)S(1)}, bf16[64,4608]{1,0:T(8,128)(2,1)S(1)}, u32[]{:S(2)}, u32[]{:S(2)}) collective-permute-start(bf16[64,4608]{1,0:T(8,128)(2,1)S(1)} %constant_dynamic-slice_fusion.3), channel_id=1, source_target_pairs={{0,8},{4,12},{8,0},{12,4},{16,24},{20,28},{24,16},{28,20},{1,9},{5... | collective-permute-start | bytes 1769480 | tf_op jit(solution)/shard_map/ppermute | solution.py:378
  427.1 3.0 collective-permute-start.38
  430.1 10.8 %collective-permute-done.44 = bf16[64,4608]{1,0:T(8,128)(2,1)S(1)} collective-permute-done((bf16[64,4608]{1,0:T(8,128)(2,1)S(1)}, bf16[64,4608]{1,0:T(8,128)(2,1)S(1)}, u32[]{:S(2)}, u32[]{:S(2)}) %collective-permute-start.44) | collective-permute-done | bytes 589856 | tf_op jit(solution)/shard_map/ppermute | solution.py:378
  441.1 19.7 %collective-permute-done.53 = bf16[64,5120]{1,0:T(8,128)(2,1)S(1)} collective-permute-done((bf16[64,5120]{1,0:T(8,128)(2,1)S(1)}, bf16[64,5120]{1,0:T(8,128)(2,1)S(1)}, u32[]{:S(2)}, u32[]{:S(2)}) %collective-permute-start.53) | collective-permute-done | bytes 655392 | tf_op jit(solution)/shard_map/ppermute | solution.py:378
  464.8 13.5 %collective-permute-done.39 = bf16[256,768]{1,0:T(8,128)(2,1)S(1)} collective-permute-done((bf16[256,768]{1,0:T(8,128)(2,1)S(1)}, bf16[256,768]{1,0:T(8,128)(2,1)S(1)}, u32[]{:S(2)}, u32[]{:S(2)}) %collective-permute-start.39) | collective-permute-done | bytes 393248 | tf_op jit(solution)/shard_map/ppermute | solution.py:378
  480.8 16.0 %collective-permute-done.40 = bf16[256,768]{1,0:T(8,128)(2,1)S(1)} collective-permute-done((bf16[256,768]{1,0:T(8,128)(2,1)S(1)}, bf16[256,768]{1,0:T(8,128)(2,1)S(1)}, u32[]{:S(2)}, u32[]{:S(2)}) %collective-permute-start.40) | collective-permute-done | bytes 393248 | tf_op jit(solution)/shard_map/ppermute | solution.py:378
  499.5 2.9 collective-permute-done.47
  509.7 20.1 %collective-permute-done.48 = bf16[128,4608]{1,0:T(8,128)(2,1)S(1)} collective-permute-done((bf16[128,4608]{1,0:T(8,128)(2,1)S(1)}, bf16[128,4608]{1,0:T(8,128)(2,1)S(1)}, u32[]{:S(2)}, u32[]{:S(2)}) %collective-permute-start.48) | collective-permute-done | bytes 1179680 | tf_op jit(solution)/shard_map/ppermute | solution.py:378
  (231 shorter events, 115.4 us)
Async XLA Ops:
  5.8 20.8 %collective-permute-start.1 = (bf16[240,1664]{1,0:T(8,128)(2,1)S(1)}, bf16[240,1664]{1,0:T(8,128)(2,1)S(1)}, u32[]{:S(2)}, u32[]{:S(2)}) collective-permute-start(bf16[240,1664]{1,0:T(8,128)(2,1)S(1)} %concatenate.46.refs_0_), channel_id=1, source_target_pairs={{0,2},{1,3},{2,0},{3,1},{4,6},{5,7},{6,4},{7,5},{8,10},{9,11},{10,... | collective-permute-start | bytes 2396168 | tf_op jit(solution)/shard_map/ppermute | solution.py:378
  8.8 23.2 %collective-permute-start = (bf16[240,1664]{1,0:T(8,128)(2,1)S(1)}, bf16[240,1664]{1,0:T(8,128)(2,1)}, u32[]{:S(2)}, u32[]{:S(2)}) collective-permute-start(bf16[240,1664]{1,0:T(8,128)(2,1)S(1)} %concatenate.46.refs_0_), channel_id=1, source_target_pairs={{0,1},{1,0},{2,3},{3,2},{4,5},{5,4},{6,7},{7,6},{8,9},{9,8},{10,11... | collective-permute-start | bytes 2396168 | tf_op jit(solution)/shard_map/ppermute | solution.py:378
  43.9 28.4 %collective-permute-start.8 = (bf16[240,2560]{1,0:T(8,128)(2,1)S(1)}, bf16[240,2560]{1,0:T(8,128)(2,1)}, u32[]{:S(2)}, u32[]{:S(2)}) collective-permute-start(bf16[240,2560]{1,0:T(8,128)(2,1)S(1)} %copy-done.17), channel_id=1, source_target_pairs={{0,2},{1,3},{2,0},{3,1},{4,6},{5,7},{6,4},{7,5},{8,10},{9,11},{10,... | collective-permute-start | bytes 3686408 | tf_op jit(solution)/shard_map/ppermute | solution.py:378
  78.4 25.9 %collective-permute-start.13 = (bf16[240,2560]{1,0:T(8,128)(2,1)S(1)}, bf16[240,2560]{1,0:T(8,128)(2,1)}, u32[]{:S(2)}, u32[]{:S(2)}) collective-permute-start(bf16[240,2560]{1,0:T(8,128)(2,1)S(1)} %copy-done.18), channel_id=1, source_target_pairs={{0,2},{1,3},{2,0},{3,1},{4,6},{5,7},{6,4},{7,5},{8,10},{9,11},{10,... | collective-permute-start | bytes 3686408 | tf_op jit(solution)/shard_map/ppermute | solution.py:378
  79.8 65.2 %collective-permute-start.17 = (bf16[240,2560]{1,0:T(8,128)(2,1)S(1)}, bf16[240,2560]{1,0:T(8,128)(2,1)S(1)}, u32[]{:S(2)}, u32[]{:S(2)}) collective-permute-start(bf16[240,2560]{1,0:T(8,128)(2,1)S(1)} %copy-done.17), channel_id=1, source_target_pairs={{0,1},{1,0},{2,3},{3,2},{4,5},{5,4},{6,7},{7,6},{8,9},{9,8},{10,11... | collective-permute-start | bytes 3686408 | tf_op jit(solution)/shard_map/ppermute | solution.py:378
  79.8 68.7 %collective-permute-start.19 = (bf16[240,2560]{1,0:T(8,128)(2,1)S(1)}, bf16[240,2560]{1,0:T(8,128)(2,1)}, u32[]{:S(2)}, u32[]{:S(2)}) collective-permute-start(bf16[240,2560]{1,0:T(8,128)(2,1)S(1)} %copy-done.18), channel_id=1, source_target_pairs={{0,1},{1,0},{2,3},{3,2},{4,5},{5,4},{6,7},{7,6},{8,9},{9,8},{10,11... | collective-permute-start | bytes 3686408 | tf_op jit(solution)/shard_map/ppermute | solution.py:378
  101.1 43.3 %collective-permute-start.15 = (bf16[240,960]{1,0:T(8,128)(2,1)}, bf16[240,960]{1,0:T(8,128)(2,1)S(1)}, u32[]{:S(2)}, u32[]{:S(2)}) collective-permute-start(bf16[240,960]{1,0:T(8,128)(2,1)} %refs_1_.1), channel_id=1, source_target_pairs={{0,1},{1,0},{2,3},{3,2},{4,5},{5,4},{6,7},{7,6},{8,9},{9,8},{10,11... | collective-permute-start | bytes 1382408 | tf_op jit(solution)/shard_map/ppermute | solution.py:378
  101.9 43.0 %collective-permute-start.21 = (bf16[960,640]{1,0:T(8,128)(2,1)S(1)}, bf16[960,640]{1,0:T(8,128)(2,1)S(1)}, u32[]{:S(2)}, u32[]{:S(2)}) collective-permute-start(bf16[960,640]{1,0:T(8,128)(2,1)S(1)} %bitcast.52), channel_id=1, source_target_pairs={{0,1},{1,0},{2,3},{3,2},{4,5},{5,4},{6,7},{7,6},{8,9},{9,8},{10,11... | collective-permute-start | bytes 3686408 | tf_op jit(solution)/shard_map/ppermute | solution.py:378
  104.4 39.9 %collective-permute-start.14 = (bf16[960,640]{1,0:T(8,128)(2,1)S(1)}, bf16[960,640]{1,0:T(8,128)(2,1)}, u32[]{:S(2)}, u32[]{:S(2)}) collective-permute-start(bf16[960,640]{1,0:T(8,128)(2,1)S(1)} %bitcast.53), channel_id=1, source_target_pairs={{0,2},{1,3},{2,0},{3,1},{4,6},{5,7},{6,4},{7,5},{8,10},{9,11},{10,... | collective-permute-start | bytes 3686408 | tf_op jit(solution)/shard_map/ppermute | solution.py:378
  195.6 34.4 %collective-permute-start.23 = (bf16[512,5120]{1,0:T(8,128)(2,1)}, bf16[512,5120]{1,0:T(8,128)(2,1)}, u32[]{:S(2)}, u32[]{:S(2)}) collective-permute-start(bf16[512,5120]{1,0:T(8,128)(2,1)} %get-tuple-element.101), channel_id=1, source_target_pairs={{0,1},{1,0},{2,3},{3,2},{4,5},{5,4},{6,7},{7,6},{8,9},{9,8},{10,11... | collective-permute-start | bytes 15728648 | tf_op jit(solution)/shard_map/ppermute | solution.py:378
  195.8 30.4 %collective-permute-start.24 = (bf16[512,3584]{1,0:T(8,128)(2,1)}, bf16[512,3584]{1,0:T(8,128)(2,1)}, u32[]{:S(2)}, u32[]{:S(2)}) collective-permute-start(bf16[512,3584]{1,0:T(8,128)(2,1)} %get-tuple-element.103), channel_id=1, source_target_pairs={{0,1},{1,0},{2,3},{3,2},{4,5},{5,4},{6,7},{7,6},{8,9},{9,8},{10,11... | collective-permute-start | bytes 11010056 | tf_op jit(solution)/shard_map/ppermute | solution.py:378
  232.3 30.9 %collective-permute-start.25 = (bf16[256,2560]{1,0:T(8,128)(2,1)S(1)}, bf16[256,2560]{1,0:T(8,128)(2,1)S(1)}, u32[]{:S(2)}, u32[]{:S(2)}) collective-permute-start(bf16[256,2560]{1,0:T(8,128)(2,1)S(1)} %get-tuple-element.180), channel_id=1, source_target_pairs={{0,2},{1,3},{2,0},{3,1},{4,6},{5,7},{6,4},{7,5},{8,10},{9,11},{10,... | collective-permute-start | bytes 3932168 | tf_op jit(solution)/shard_map/ppermute | solution.py:378
  273.2 31.6 %collective-permute-start.30 = (bf16[256,2560]{1,0:T(8,128)(2,1)S(1)}, bf16[256,2560]{1,0:T(8,128)(2,1)S(1)}, u32[]{:S(2)}, u32[]{:S(2)}) collective-permute-start(bf16[256,2560]{1,0:T(8,128)(2,1)S(1)} %get-tuple-element.113), channel_id=1, source_target_pairs={{0,2},{1,3},{2,0},{3,1},{4,6},{5,7},{6,4},{7,5},{8,10},{9,11},{10,... | collective-permute-start | bytes 3932168 | tf_op jit(solution)/shard_map/ppermute | solution.py:378
  274.3 16.9 %collective-permute-start.29 = (bf16[2,2,128,640]{3,2,1,0:T(8,128)(2,1)S(1)}, bf16[2,2,128,640]{3,2,1,0:T(8,128)(2,1)S(1)}, u32[]{:S(2)}, u32[]{:S(2)}) collective-permute-start(bf16[2,2,128,640]{3,2,1,0:T(8,128)(2,1)S(1)} %pad_maximum_fusion.4), channel_id=1, source_target_pairs={{8,0},{16,8},{24,16},{28,24},{20,28},{12,20},{4,12},{0,4},{9,1},{1... | collective-permute-start | bytes 1966088 | tf_op jit(solution)/shard_map/ppermute | solution.py:859
  278.9 36.8 %collective-permute-start.42 = (bf16[256,1024]{1,0:T(8,128)(2,1)}, bf16[256,1024]{1,0:T(8,128)(2,1)}, u32[]{:S(2)}, u32[]{:S(2)}) collective-permute-start(bf16[256,1024]{1,0:T(8,128)(2,1)} %add_convert_fusion.16), channel_id=1, source_target_pairs={{0,2},{1,3},{2,0},{3,1},{4,6},{5,7},{6,4},{7,5},{8,10},{9,11},{10,... | collective-permute-start | bytes 1572872 | tf_op jit(solution)/shard_map/ppermute | solution.py:378
  308.7 49.1 %collective-permute-start.49 = (bf16[128,5120]{1,0:T(8,128)(2,1)}, bf16[128,5120]{1,0:T(8,128)(2,1)}, u32[]{:S(2)}, u32[]{:S(2)}) collective-permute-start(bf16[128,5120]{1,0:T(8,128)(2,1)} %fusion), channel_id=1, source_target_pairs={{0,4},{4,0},{8,12},{12,8},{16,20},{20,16},{24,28},{28,24},{1,5},{5... | collective-permute-start | bytes 3932168 | tf_op jit(solution)/shard_map/ppermute | solution.py:378
  310.2 40.8 %collective-permute-start.32 = (bf16[2,2,128,640]{3,2,1,0:T(8,128)(2,1)}, bf16[2,2,128,640]{3,2,1,0:T(8,128)(2,1)}, u32[]{:S(2)}, u32[]{:S(2)}) collective-permute-start(bf16[2,2,128,640]{3,2,1,0:T(8,128)(2,1)} %add_convert_fusion.12), channel_id=1, source_target_pairs={{8,0},{16,8},{24,16},{28,24},{20,28},{12,20},{4,12},{0,4},{9,1},{1... | collective-permute-start | bytes 1966088 | tf_op jit(solution)/shard_map/ppermute | solution.py:859
  312.8 40.2 %collective-permute-start.31 = (bf16[2,2,128,640]{3,2,1,0:T(8,128)(2,1)}, bf16[2,2,128,640]{3,2,1,0:T(8,128)(2,1)}, u32[]{:S(2)}, u32[]{:S(2)}) collective-permute-start(bf16[2,2,128,640]{3,2,1,0:T(8,128)(2,1)} %add_convert_fusion.13), channel_id=1, source_target_pairs={{0,8},{8,16},{16,24},{24,28},{28,20},{20,12},{12,4},{4,0},{1,9},{9... | collective-permute-start | bytes 1966088 | tf_op jit(solution)/shard_map/ppermute | solution.py:858
  317.5 55.5 %collective-permute-start.35 = (bf16[256,3584]{1,0:T(8,128)(2,1)S(1)}, bf16[256,3584]{1,0:T(8,128)(2,1)S(1)}, u32[]{:S(2)}, u32[]{:S(2)}) collective-permute-start(bf16[256,3584]{1,0:T(8,128)(2,1)S(1)} %copy-done.5), channel_id=1, source_target_pairs={{0,2},{1,3},{2,0},{3,1},{4,6},{5,7},{6,4},{7,5},{8,10},{9,11},{10,... | collective-permute-start | bytes 5505032 | tf_op jit(solution)/shard_map/ppermute | solution.py:378
  354.4 17.7 %collective-permute-start.34 = (bf16[2,2,128,640]{3,2,1,0:T(8,128)(2,1)S(1)}, bf16[2,2,128,640]{3,2,1,0:T(8,128)(2,1)S(1)}, u32[]{:S(2)}, u32[]{:S(2)}) collective-permute-start(bf16[2,2,128,640]{3,2,1,0:T(8,128)(2,1)S(1)} %add_convert_fusion.10), channel_id=1, source_target_pairs={{8,0},{16,8},{24,16},{28,24},{20,28},{12,20},{4,12},{0,4},{9,1},{1... | collective-permute-start | bytes 1966088 | tf_op jit(solution)/shard_map/ppermute | solution.py:859
  359.7 25.0 %collective-permute-start.50 = (bf16[64,5120]{1,0:T(8,128)(2,1)S(1)}, bf16[64,5120]{1,0:T(8,128)(2,1)S(1)}, u32[]{:S(2)}, u32[]{:S(2)}) collective-permute-start(bf16[64,5120]{1,0:T(8,128)(2,1)S(1)} %constant_dynamic-slice_fusion.1), channel_id=1, source_target_pairs={{0,8},{4,12},{8,0},{12,4},{16,24},{20,28},{24,16},{28,20},{1,9},{5... | collective-permute-start | bytes 1966088 | tf_op jit(solution)/shard_map/ppermute | solution.py:378
  386.9 27.3 %collective-permute-start.43 = (bf16[128,4608]{1,0:T(8,128)(2,1)}, bf16[128,4608]{1,0:T(8,128)(2,1)}, u32[]{:S(2)}, u32[]{:S(2)}) collective-permute-start(bf16[128,4608]{1,0:T(8,128)(2,1)} %fusion.3), channel_id=1, source_target_pairs={{0,4},{4,0},{8,12},{12,8},{16,20},{20,16},{24,28},{28,24},{1,5},{5... | collective-permute-start | bytes 3538952 | tf_op jit(solution)/shard_map/ppermute | solution.py:378
  415.9 25.0 %collective-permute-start.44 = (bf16[64,4608]{1,0:T(8,128)(2,1)S(1)}, bf16[64,4608]{1,0:T(8,128)(2,1)S(1)}, u32[]{:S(2)}, u32[]{:S(2)}) collective-permute-start(bf16[64,4608]{1,0:T(8,128)(2,1)S(1)} %constant_dynamic-slice_fusion.3), channel_id=1, source_target_pairs={{0,8},{4,12},{8,0},{12,4},{16,24},{20,28},{24,16},{28,20},{1,9},{5... | collective-permute-start | bytes 1769480 | tf_op jit(solution)/shard_map/ppermute | solution.py:378
  426.8 34.0 %collective-permute-start.53 = (bf16[64,5120]{1,0:T(8,128)(2,1)S(1)}, bf16[64,5120]{1,0:T(8,128)(2,1)S(1)}, u32[]{:S(2)}, u32[]{:S(2)}) collective-permute-start(bf16[64,5120]{1,0:T(8,128)(2,1)S(1)} %pad_maximum_fusion.5), channel_id=1, source_target_pairs={{0,8},{4,12},{8,0},{12,4},{16,24},{20,28},{24,16},{28,20},{1,9},{5... | collective-permute-start | bytes 1966088 | tf_op jit(solution)/shard_map/ppermute | solution.py:378
  427.1 34.0 %collective-permute-start.38 = (bf16[256,768]{1,0:T(8,128)(2,1)S(1)}, bf16[256,768]{1,0:T(8,128)(2,1)S(1)}, u32[]{:S(2)}, u32[]{:S(2)}) collective-permute-start(bf16[256,768]{1,0:T(8,128)(2,1)S(1)} %add_convert_fusion.21), channel_id=1, source_target_pairs={{0,4},{4,0},{8,12},{12,8},{16,20},{20,16},{24,28},{28,24},{1,5},{5... | collective-permute-start | bytes 1179656 | tf_op jit(solution)/shard_map/ppermute | solution.py:378
  441.1 20.2 %collective-permute-start.45 = (bf16[32,4608]{1,0:T(8,128)(2,1)S(1)}, bf16[32,4608]{1,0:T(8,128)(2,1)S(1)}, u32[]{:S(2)}, u32[]{:S(2)}) collective-permute-start(bf16[32,4608]{1,0:T(8,128)(2,1)S(1)} %constant_dynamic-slice_fusion.2), channel_id=1, source_target_pairs={{0,16},{4,20},{8,24},{12,28},{16,0},{20,4},{24,8},{28,12},{1,17},{... | collective-permute-start | bytes 884744 | tf_op jit(solution)/shard_map/ppermute | solution.py:378
  461.2 17.1 %collective-permute-start.39 = (bf16[256,768]{1,0:T(8,128)(2,1)S(1)}, bf16[256,768]{1,0:T(8,128)(2,1)S(1)}, u32[]{:S(2)}, u32[]{:S(2)}) collective-permute-start(bf16[256,768]{1,0:T(8,128)(2,1)S(1)} %add_convert_fusion.20), channel_id=1, source_target_pairs={{0,8},{4,12},{8,0},{12,4},{16,24},{20,28},{24,16},{28,20},{1,9},{5... | collective-permute-start | bytes 1179656 | tf_op jit(solution)/shard_map/ppermute | solution.py:378
  461.4 17.1 %collective-permute-start.46 = (bf16[32,4608]{1,0:T(8,128)(2,1)S(1)}, bf16[32,4608]{1,0:T(8,128)(2,1)S(1)}, u32[]{:S(2)}, u32[]{:S(2)}) collective-permute-start(bf16[32,4608]{1,0:T(8,128)(2,1)S(1)} %add_convert_fusion.27), channel_id=1, source_target_pairs={{0,16},{4,20},{8,24},{12,28},{16,0},{20,4},{24,8},{28,12},{1,17},{... | collective-permute-start | bytes 884744 | tf_op jit(solution)/shard_map/ppermute | solution.py:378
  464.8 39.0 %collective-permute-start.54 = (bf16[128,5120]{1,0:T(8,128)(2,1)}, bf16[128,5120]{1,0:T(8,128)(2,1)}, u32[]{:S(2)}, u32[]{:S(2)}) collective-permute-start(bf16[128,5120]{1,0:T(8,128)(2,1)} %pad_maximum_fusion), channel_id=1, source_target_pairs={{0,4},{4,0},{8,12},{12,8},{16,20},{20,16},{24,28},{28,24},{1,5},{5... | collective-permute-start | bytes 3932168 | tf_op jit(solution)/shard_map/ppermute | solution.py:378
  478.4 18.4 %collective-permute-start.40 = (bf16[256,768]{1,0:T(8,128)(2,1)S(1)}, bf16[256,768]{1,0:T(8,128)(2,1)S(1)}, u32[]{:S(2)}, u32[]{:S(2)}) collective-permute-start(bf16[256,768]{1,0:T(8,128)(2,1)S(1)} %add_convert_fusion.19), channel_id=1, source_target_pairs={{0,16},{4,20},{8,24},{12,28},{16,0},{20,4},{24,8},{28,12},{1,17},{... | collective-permute-start | bytes 1179656 | tf_op jit(solution)/shard_map/ppermute | solution.py:378
  479.4 23.0 %collective-permute-start.47 = (bf16[64,4608]{1,0:T(8,128)(2,1)}, bf16[64,4608]{1,0:T(8,128)(2,1)}, u32[]{:S(2)}, u32[]{:S(2)}) collective-permute-start(bf16[64,4608]{1,0:T(8,128)(2,1)} %pad_maximum_fusion.6), channel_id=1, source_target_pairs={{0,8},{4,12},{8,0},{12,4},{16,24},{20,28},{24,16},{28,20},{1,9},{5... | collective-permute-start | bytes 1769480 | tf_op jit(solution)/shard_map/ppermute | solution.py:378
  503.7 26.1 %collective-permute-start.48 = (bf16[128,4608]{1,0:T(8,128)(2,1)S(1)}, bf16[128,4608]{1,0:T(8,128)(2,1)S(1)}, u32[]{:S(2)}, u32[]{:S(2)}) collective-permute-start(bf16[128,4608]{1,0:T(8,128)(2,1)S(1)} %pad_maximum_fusion.2), channel_id=1, source_target_pairs={{0,4},{4,0},{8,12},{12,8},{16,20},{20,16},{24,28},{28,24},{1,5},{5... | collective-permute-start | bytes 3538952 | tf_op jit(solution)/shard_map/ppermute | solution.py:378
  (51 other events, 620.8 us)

commit v3 on v2

--- a/solution.py
+++ b/solution.py
@@ -934,7 +934,7 @@
         far_up = swap_over(pass_up, "wsh", 2)
         far_down = swap_over(follow(pass_down, far_up), "wsh", 2)
         far_b = swap_over(follow(pass_b, far_down), "wsh", 2)
-        beside = {3: far_down, 1: far_b}
+        beside = {2: far_down}
     grad_queries, terms = [], []
     for b in range(seqs):
         at = follow(rank, pass_up, pass_down, pass_b) if split and b else rank
@@ -958,14 +958,13 @@
         mine = jnp.concatenate(
             [
                 added(kept_a[:, :units], came[:tall, :units], far_up),
-                added(kept_a[:, units:], came[:tall, units:], beside[3]),
+                added(kept_a[:, units:], came[:tall, units:], beside[2]),
             ],
             1,
         )
         sum_a = split_sums(mine).astype(jnp.float32)
-        sum_q = far_sums(core_sums(q_group))
-        sum_b = split_sums(jnp.concatenate([added(kept_b, beside[1]), sum_q], 1)).astype(jnp.float32)
-        sum_gate, sum_q = sum_b, sum_b[:, units + width + HEAD :]
+        mine_q = far_sums(core_sums(q_group))
+        sum_gate = split_sums(added(kept_b, far_b)).astype(jnp.float32)
         sum_up = sum_a
         height = width // count
         per = units // count
@@ -981,7 +980,9 @@
         count, base, inputs, normed, w_all, part, middle_grad, gains, cosine, sine, summed
     )
     if split:
-        sum_kv = whole_sums(far_sums(core_sums(kv_group))).astype(jnp.float32)
+        mine_kv = far_sums(core_sums(kv_group))
+        sum_kv = split_sums(jnp.concatenate([mine_kv, mine_q], 1)).astype(jnp.float32)
+        sum_q = sum_kv[:, mine_kv.shape[1] :]
     else:
         sum_kv = plain_sums(kv_group[0]).astype(jnp.float32)
     height = norm1_gain.shape[0]

time: 541 us -> 520 us (0.961)
  waiting for transfers between devices: 236 us -> 216 us
  starting transfers between devices: 57.6 us -> 51.1 us
  other arithmetic: 42.9 us -> 49.1 us
    ppermute x3, waiting for transfers between devices: 55 us -> 5.2 us  [ring_sums(): down = lax.ppermute(down, 'ctx', backward)]
    ppermute x39 -> x42, waiting for transfers between devices: 148 us -> 168 us  [swap_over(): lax.ppermute(value, axis, [(i, i ^ bit) for i in range(lax.axis_size(axis...]
    ppermute x1, waiting for transfers between devices: 0.01 us -> 6.69 us  [ring_sums(): two = lax.ppermute(term(side, 1), 'ctx', backward)]
    ppermute x39 -> x42, starting transfers between devices: 40.8 us -> 34.6 us  [swap_over(): lax.ppermute(value, axis, [(i, i ^ bit) for i in range(lax.axis_size(axis...]
    convert_element_type x20 -> x21, other arithmetic: 22.3 us -> 28 us  [added(): return total.astype(jnp.bfloat16)]
    unnamed x64 -> x62, local copies, waits for them, and re-layouts: 14.9 us -> 15.1 us
  transfers between devices with their start and end apart: 55 -> 58, of which waited for: 29 -> 33; matrix products, arithmetic and copies ran while one was open for 11% -> 13% of each run, Pallas kernels for 22% -> 23%
where the time goes in v3:
time: 520 us; the launch traced here: 514 us
  waiting for transfers between devices  216 us (42%)
  Pallas kernels  163 us (31%)
  starting transfers between devices  51.1 us (10%)
  other arithmetic  49.1 us (9%)
  local copies, waits for them, and re-layouts  33 us (6%)
    ppermute x42, waiting for transfers between devices, swap_over(): lax.ppermute(value, axis, [(i, i ^ bit) for i in range(lax.axis_size(axis...  168 us
    pallas_call x2, Pallas kernels, attend_back(): pl.pallas_call(functools.partial(attend_back_kernel, n, block, count, seq...  56.8 us
    pallas_call x1, Pallas kernels, feed(): pl.pallas_call(functools.partial(feed_body, count, 256), in_specs=[pl.Blo...  43.8 us
    pallas_call x1, Pallas kernels, attend(): pl.pallas_call(functools.partial(attend_kernel, n, block, count), grid=(s...  38.7 us
    ppermute x42, starting transfers between devices, swap_over(): lax.ppermute(value, axis, [(i, i ^ bit) for i in range(lax.axis_size(axis...  34.6 us
    convert_element_type x21, other arithmetic, added(): return total.astype(jnp.bfloat16)  28 us
    ppermute x3, waiting for transfers between devices, ring_gather(): one = lax.ppermute(behind[-1], 'ctx', onward)  16.6 us
    unnamed x62, local copies, waits for them, and re-layouts  15.1 us
  transfers between devices with their start and end apart: 58, of which 33 were waited for; matrix products, arithmetic and copies ran while one was open for 13% of the time, Pallas kernels for 23%

profile of v3, /device:TPU:0, one launch (start us, length us, event | category | flops | bytes accessed | tf_op | source)
XLA Modules:
  0.0 514.0 jit_solution(16130134515438648444)
XLA Ops:
  5.8 3.0 collective-permute-start.1
  8.8 17.8 %collective-permute-done.1.refs_2_ = bf16[240,1664]{1,0:T(8,128)(2,1)S(1)} collective-permute-done((bf16[240,1664]{1,0:T(8,128)(2,1)S(1)}, bf16[240,1664]{1,0:T(8,128)(2,1)S(1)}, u32[]{:S(2)}, u32[]{:S(2)}) %collective-permute-start.1) | collective-permute-done | bytes 798752 | tf_op jit(solution)/shard_map/ppermute | solution.py:378
  32.0 8.3 %project.1 = (bf16[960,1664]{1,0:T(8,128)(2,1)}, bf16[512,960]{1,0:T(8,128)(2,1)}, bf16[512,1024]{1,0:T(8,128)(2,1)}, bf16[512,640]{1,0:T(8,128)(2,1)}, f32[8,960]{1,0:T(8,128)}) custom-call(s32[1]{0:T(128)} %bitcast.base_ref, bf16[2,2,128,960]{3,2,1,0:T(8,128)(2,1)} %copy.132.x_ref, f32[256,128]{1,0:T(8,128)} %pad_maximum_fusion.11.cos_ref, ...), custom_call_target="tpu_custom_call" | custom-call | flops 1635778560 | bytes 8388608 | tf_op jit(solution)/shard_map/project/pallas_call | solution.py:436
  45.4 12.9 %collective-permute-done.4 = bf16[2,2,128,640]{3,2,0,1:T(8,128)(2,1)S(1)} collective-permute-done((bf16[2,2,128,640]{3,2,0,1:T(8,128)(2,1)S(1)}, bf16[2,2,128,640]{3,2,0,1:T(8,128)(2,1)S(1)}, u32[]{:S(2)}, u32[]{:S(2)}) %collective-permute-start.4) | collective-permute-done | bytes 655392 | tf_op jit(solution)/shard_map/ppermute | solution.py:828
  61.7 10.5 %collective-permute-done.8.refs_7_ = bf16[240,2560]{1,0:T(8,128)(2,1)} collective-permute-done((bf16[240,2560]{1,0:T(8,128)(2,1)S(1)}, bf16[240,2560]{1,0:T(8,128)(2,1)}, u32[]{:S(2)}, u32[]{:S(2)}) %collective-permute-start.8) | collective-permute-done | bytes 1228832 | tf_op jit(solution)/shard_map/ppermute | solution.py:378
  80.1 10.3 %collective-permute-done.10 = bf16[2,2,128,640]{3,2,0,1:T(8,128)(2,1)S(1)} collective-permute-done((bf16[2,2,128,640]{3,2,0,1:T(8,128)(2,1)S(1)}, bf16[2,2,128,640]{3,2,0,1:T(8,128)(2,1)S(1)}, u32[]{:S(2)}, u32[]{:S(2)}) %collective-permute-start.10) | collective-permute-done | bytes 655392 | tf_op jit(solution)/shard_map/ppermute | solution.py:829
  101.6 3.1 collective-permute-done.13.refs_11_
  105.8 38.7 %attend.1 = (f32[2,2,128,960]{3,2,1,0:T(8,128)}, f32[2,10,384]{2,1,0:T(8,128)}) custom-call(s32[1]{0:T(128)} %bitcast.1.rank_ref, s32[8]{0:T(128)} %select_reduce_fusion.owners_ref, bf16[2,2,128,1024]{3,2,1,0:T(8,128)(2,1)} %bitcast.54, bf16[2,2,128,640]{3,2,1,0:T(8,128)(2,1)} %bitcast.48, bf16[2,2,128,640]{3,2,1,0:T(8,128)(2,1)} %copy.126.refs_1_, ...), custom_call_target="tpu_custom_call" | custom-call | flops 17112760320 | bytes 4194304 | tf_op jit(solution)/shard_map/attend/pallas_call | solution.py:201
  152.1 43.8 %feed.1 = (bf16[2,2,128,960]{3,2,1,0:T(8,128)(2,1)}, f32[512,960]{1,0:T(8,128)}, bf16[2,2,128,960]{3,2,1,0:T(8,128)(2,1)}, bf16[256,3584]{1,0:T(8,128)(2,1)}, bf...) custom-call(s32[1]{0:T(128)} %bitcast.base_ref, ...), custom_call_target="tpu_custom_call" | custom-call | flops 25480396800 | bytes 50331648 | tf_op jit(solution)/shard_map/feed/pallas_call | solution.py:610
  196.4 28.6 %attend_back.2 = (bf16[1,2,128,960]{3,2,1,0:T(8,128)(2,1)}, bf16[8,2,128,640]{3,2,1,0:T(8,128)(2,1)}) custom-call(s32[1]{0:T(128)} %bitcast.1.rank_ref, s32[8]{0:T(128)} %select_reduce_fusion.owners_ref, bf16[2,2,128,1024]{3,2,1,0:T(8,128)(2,1)} %bitcast.55, bf16[2,2,128,960]{3,2,1,0:T(8,128)(2,1)} %get-tuple-element.96.do_ref, ...), custom_call_target="tpu_custom_call" | custom-call | flops 21390950400 | bytes 8388608 | tf_op jit(solution)/shard_map/attend_back/pallas_call | solution.py:331
  227.0 3.3 add_convert_fusion.2
  234.0 28.2 %attend_back.3 = (bf16[1,2,128,960]{3,2,1,0:T(8,128)(2,1)}, bf16[8,2,128,640]{3,2,1,0:T(8,128)(2,1)}) custom-call(s32[1]{0:T(128)} %bitcast.1.rank_ref, s32[8]{0:T(128)} %select_reduce_fusion.owners_ref, bf16[2,2,128,1024]{3,2,1,0:T(8,128)(2,1)} %bitcast.56, bf16[2,2,128,960]{3,2,1,0:T(8,128)(2,1)} %get-tuple-element.96.do_ref, ...), custom_call_target="tpu_custom_call" | custom-call | flops 21390950400 | bytes 8388608 | tf_op jit(solution)/shard_map/attend_back/pallas_call | solution.py:331
  268.1 6.7 %collective-permute-done.27 = bf16[2,128,640]{2,1,0:T(8,128)(2,1)S(1)} collective-permute-done((bf16[2,128,640]{2,1,0:T(8,128)(2,1)S(1)}, bf16[2,128,640]{2,1,0:T(8,128)(2,1)S(1)}, u32[]{:S(2)}, u32[]{:S(2)}) %collective-permute-start.27) | collective-permute-done | bytes 327712 | tf_op jit(solution)/shard_map/ppermute | solution.py:853
  278.4 6.5 %query_grads.1 = (f32[512,960]{1,0:T(8,128)}, bf16[256,1024]{1,0:T(8,128)(2,1)}, bf16[256,1024]{1,0:T(8,128)(2,1)}, bf16[512,1024]{1,0:T(8,128)(2,1)}) custom-call(s32[1]{0:T(128)} %bitcast.base_ref, bf16[512,960]{1,0:T(8,128)(2,1)} %get-tuple-element.94.normed_ref, bf16[960,1664]{1,0:T(8,128)(2,1)} %get-tuple-element.95.w_ref, ...), custom_call_target="tpu_custom_call" | custom-call | flops 1887436800 | bytes 10485760 | tf_op jit(solution)/shard_map/query_grads/pallas_call | solution.py:676
  286.7 3.3 collective-permute-done.29
  300.6 16.2 %collective-permute-done.32 = bf16[256,2560]{1,0:T(8,128)(2,1)S(1)} collective-permute-done((bf16[256,2560]{1,0:T(8,128)(2,1)}, bf16[256,2560]{1,0:T(8,128)(2,1)S(1)}, u32[]{:S(2)}, u32[]{:S(2)}) %collective-permute-start.32) | collective-permute-done | bytes 1310752 | tf_op jit(solution)/shard_map/ppermute | solution.py:378
  323.5 3.1 add_convert_fusion.4
  335.9 4.6 collective-permute-done.33
  343.1 9.1 %finish.1 = (f32[2,2,128,960]{3,2,1,0:T(8,128)}, bf16[256,768]{1,0:T(8,128)(2,1)}, bf16[256,768]{1,0:T(8,128)(2,1)}, bf16[512,768]{1,0:T(8,128)(2,1)}) custom-call(s32[1]{0:T(128)} %bitcast.base_ref, bf16[2,2,128,960]{3,2,1,0:T(8,128)(2,1)} %copy.132.x_ref, bf16[512,960]{1,0:T(8,128)(2,1)} %get-tuple-element.94.normed_ref, ...), custom_call_target="tpu_custom_call" | custom-call | flops 1258291200 | bytes 14680064 | tf_op jit(solution)/shard_map/finish/pallas_call | solution.py:734
  352.3 2.9 copy.148
  355.1 11.3 %collective-permute-done.52 = bf16[128,5120]{1,0:T(8,128)(2,1)} collective-permute-done((bf16[128,5120]{1,0:T(8,128)(2,1)}, bf16[128,5120]{1,0:T(8,128)(2,1)}, u32[]{:S(2)}, u32[]{:S(2)}) %collective-permute-start.52) | collective-permute-done | bytes 1310752 | tf_op jit(solution)/shard_map/ppermute | solution.py:378
  370.5 5.7 %collective-permute-done.45 = bf16[256,3584]{1,0:T(8,128)(2,1)} collective-permute-done((bf16[256,3584]{1,0:T(8,128)(2,1)}, bf16[256,3584]{1,0:T(8,128)(2,1)}, u32[]{:S(2)}, u32[]{:S(2)}) %collective-permute-start.45) | collective-permute-done | bytes 1835040 | tf_op jit(solution)/shard_map/ppermute | solution.py:378
  387.8 9.9 %collective-permute-done.54 = bf16[32,5120]{1,0:T(8,128)(2,1)S(1)} collective-permute-done((bf16[32,5120]{1,0:T(8,128)(2,1)S(1)}, bf16[32,5120]{1,0:T(8,128)(2,1)S(1)}, u32[]{:S(2)}, u32[]{:S(2)}) %collective-permute-start.54) | collective-permute-done | bytes 327712 | tf_op jit(solution)/shard_map/ppermute | solution.py:378
  397.9 8.1 %collective-permute-done.39 = bf16[128,1792]{1,0:T(8,128)(2,1)S(1)} collective-permute-done((bf16[128,1792]{1,0:T(8,128)(2,1)S(1)}, bf16[128,1792]{1,0:T(8,128)(2,1)S(1)}, u32[]{:S(2)}, u32[]{:S(2)}) %collective-permute-start.39) | collective-permute-done | bytes 458784 | tf_op jit(solution)/shard_map/ppermute | solution.py:378
  408.5 12.1 %collective-permute-done.40 = bf16[64,1792]{1,0:T(8,128)(2,1)S(1)} collective-permute-done((bf16[64,1792]{1,0:T(8,128)(2,1)S(1)}, bf16[64,1792]{1,0:T(8,128)(2,1)S(1)}, u32[]{:S(2)}, u32[]{:S(2)}) %collective-permute-start.40) | collective-permute-done | bytes 229408 | tf_op jit(solution)/shard_map/ppermute | solution.py:378
  421.2 7.2 %collective-permute-done.41 = bf16[32,1792]{1,0:T(8,128)(2,1)S(1)} collective-permute-done((bf16[32,1792]{1,0:T(8,128)(2,1)S(1)}, bf16[32,1792]{1,0:T(8,128)(2,1)S(1)}, u32[]{:S(2)}, u32[]{:S(2)}) %collective-permute-start.41) | collective-permute-done | bytes 114720 | tf_op jit(solution)/shard_map/ppermute | solution.py:378
  431.1 5.1 collective-permute-done.42
  438.9 14.2 %collective-permute-done.43 = bf16[64,1792]{1,0:T(8,128)(2,1)S(1)} collective-permute-done((bf16[64,1792]{1,0:T(8,128)(2,1)S(1)}, bf16[64,1792]{1,0:T(8,128)(2,1)S(1)}, u32[]{:S(2)}, u32[]{:S(2)}) %collective-permute-start.43) | collective-permute-done | bytes 229408 | tf_op jit(solution)/shard_map/ppermute | solution.py:378
  458.3 6.6 %collective-permute-done.49 = bf16[32,3584]{1,0:T(8,128)(2,1)S(1)} collective-permute-done((bf16[32,3584]{1,0:T(8,128)(2,1)S(1)}, bf16[32,3584]{1,0:T(8,128)(2,1)S(1)}, u32[]{:S(2)}, u32[]{:S(2)}) %collective-permute-start.49) | collective-permute-done | bytes 229408 | tf_op jit(solution)/shard_map/ppermute | solution.py:378
  470.3 6.7 %collective-permute-done.50 = bf16[64,3584]{1,0:T(8,128)(2,1)} collective-permute-done((bf16[64,3584]{1,0:T(8,128)(2,1)}, bf16[64,3584]{1,0:T(8,128)(2,1)}, u32[]{:S(2)}, u32[]{:S(2)}) %collective-permute-start.50) | collective-permute-done | bytes 458784 | tf_op jit(solution)/shard_map/ppermute | solution.py:378
  478.3 16.2 %collective-permute-done.57 = bf16[128,5120]{1,0:T(8,128)(2,1)} collective-permute-done((bf16[128,5120]{1,0:T(8,128)(2,1)}, bf16[128,5120]{1,0:T(8,128)(2,1)}, u32[]{:S(2)}, u32[]{:S(2)}) %collective-permute-start.57) | collective-permute-done | bytes 1310752 | tf_op jit(solution)/shard_map/ppermute | solution.py:378
  500.4 9.5 %collective-permute-done.51 = bf16[128,3584]{1,0:T(8,128)(2,1)S(1)} collective-permute-done((bf16[128,3584]{1,0:T(8,128)(2,1)S(1)}, bf16[128,3584]{1,0:T(8,128)(2,1)S(1)}, u32[]{:S(2)}, u32[]{:S(2)}) %collective-permute-start.51) | collective-permute-done | bytes 917536 | tf_op jit(solution)/shard_map/ppermute | solution.py:378
  (245 shorter events, 139.0 us)
Async XLA Ops:
  5.8 20.8 %collective-permute-start.1 = (bf16[240,1664]{1,0:T(8,128)(2,1)S(1)}, bf16[240,1664]{1,0:T(8,128)(2,1)S(1)}, u32[]{:S(2)}, u32[]{:S(2)}) collective-permute-start(bf16[240,1664]{1,0:T(8,128)(2,1)S(1)} %concatenate.55.refs_0_), channel_id=1, source_target_pairs={{0,2},{1,3},{2,0},{3,1},{4,6},{5,7},{6,4},{7,5},{8,10},{9,11},{10,... | collective-permute-start | bytes 2396168 | tf_op jit(solution)/shard_map/ppermute | solution.py:378
  8.8 23.2 %collective-permute-start = (bf16[240,1664]{1,0:T(8,128)(2,1)S(1)}, bf16[240,1664]{1,0:T(8,128)(2,1)}, u32[]{:S(2)}, u32[]{:S(2)}) collective-permute-start(bf16[240,1664]{1,0:T(8,128)(2,1)S(1)} %concatenate.55.refs_0_), channel_id=1, source_target_pairs={{0,1},{1,0},{2,3},{3,2},{4,5},{5,4},{6,7},{7,6},{8,9},{9,8},{10,11... | collective-permute-start | bytes 2396168 | tf_op jit(solution)/shard_map/ppermute | solution.py:378
  41.6 16.8 %collective-permute-start.4 = (bf16[2,2,128,640]{3,2,0,1:T(8,128)(2,1)S(1)}, bf16[2,2,128,640]{3,2,0,1:T(8,128)(2,1)S(1)}, u32[]{:S(2)}, u32[]{:S(2)}) collective-permute-start(bf16[2,2,128,640]{3,2,0,1:T(8,128)(2,1)S(1)} %copy.124), channel_id=1, source_target_pairs={{0,8},{8,16},{16,24},{24,28},{28,20},{20,12},{12,4},{4,0},{1,9},{9... | collective-permute-start | bytes 1966088 | tf_op jit(solution)/shard_map/ppermute | solution.py:828
  43.5 16.2 %collective-permute-start.5 = (bf16[2,2,128,640]{3,2,0,1:T(8,128)(2,1)S(1)}, bf16[2,2,128,640]{3,2,0,1:T(8,128)(2,1)S(1)}, u32[]{:S(2)}, u32[]{:S(2)}) collective-permute-start(bf16[2,2,128,640]{3,2,0,1:T(8,128)(2,1)S(1)} %copy.124), channel_id=1, source_target_pairs={{8,0},{16,8},{24,16},{28,24},{20,28},{12,20},{4,12},{0,4},{9,1},{1... | collective-permute-start | bytes 1966088 | tf_op jit(solution)/shard_map/ppermute | solution.py:829
  43.7 28.5 %collective-permute-start.8 = (bf16[240,2560]{1,0:T(8,128)(2,1)S(1)}, bf16[240,2560]{1,0:T(8,128)(2,1)}, u32[]{:S(2)}, u32[]{:S(2)}) collective-permute-start(bf16[240,2560]{1,0:T(8,128)(2,1)S(1)} %copy-done.16), channel_id=1, source_target_pairs={{0,2},{1,3},{2,0},{3,1},{4,6},{5,7},{6,4},{7,5},{8,10},{9,11},{10,... | collective-permute-start | bytes 3686408 | tf_op jit(solution)/shard_map/ppermute | solution.py:378
  78.3 26.3 %collective-permute-start.13 = (bf16[240,2560]{1,0:T(8,128)(2,1)}, bf16[240,2560]{1,0:T(8,128)(2,1)}, u32[]{:S(2)}, u32[]{:S(2)}) collective-permute-start(bf16[240,2560]{1,0:T(8,128)(2,1)} %refs_9_.1), channel_id=1, source_target_pairs={{0,2},{1,3},{2,0},{3,1},{4,6},{5,7},{6,4},{7,5},{8,10},{9,11},{10,... | collective-permute-start | bytes 3686408 | tf_op jit(solution)/shard_map/ppermute | solution.py:378
  79.6 65.6 %collective-permute-start.17 = (bf16[240,2560]{1,0:T(8,128)(2,1)S(1)}, bf16[240,2560]{1,0:T(8,128)(2,1)S(1)}, u32[]{:S(2)}, u32[]{:S(2)}) collective-permute-start(bf16[240,2560]{1,0:T(8,128)(2,1)S(1)} %copy-done.16), channel_id=1, source_target_pairs={{0,1},{1,0},{2,3},{3,2},{4,5},{5,4},{6,7},{7,6},{8,9},{9,8},{10,11... | collective-permute-start | bytes 3686408 | tf_op jit(solution)/shard_map/ppermute | solution.py:378
  79.6 69.1 %collective-permute-start.19 = (bf16[240,2560]{1,0:T(8,128)(2,1)}, bf16[240,2560]{1,0:T(8,128)(2,1)}, u32[]{:S(2)}, u32[]{:S(2)}) collective-permute-start(bf16[240,2560]{1,0:T(8,128)(2,1)} %refs_9_.1), channel_id=1, source_target_pairs={{0,1},{1,0},{2,3},{3,2},{4,5},{5,4},{6,7},{7,6},{8,9},{9,8},{10,11... | collective-permute-start | bytes 3686408 | tf_op jit(solution)/shard_map/ppermute | solution.py:378
  101.0 43.6 %collective-permute-start.15 = (bf16[240,960]{1,0:T(8,128)(2,1)S(1)}, bf16[240,960]{1,0:T(8,128)(2,1)S(1)}, u32[]{:S(2)}, u32[]{:S(2)}) collective-permute-start(bf16[240,960]{1,0:T(8,128)(2,1)S(1)} %copy-done.21), channel_id=1, source_target_pairs={{0,1},{1,0},{2,3},{3,2},{4,5},{5,4},{6,7},{7,6},{8,9},{9,8},{10,11... | collective-permute-start | bytes 1382408 | tf_op jit(solution)/shard_map/ppermute | solution.py:378
  101.0 44.1 %collective-permute-start.21 = (bf16[960,640]{1,0:T(8,128)(2,1)S(1)}, bf16[960,640]{1,0:T(8,128)(2,1)S(1)}, u32[]{:S(2)}, u32[]{:S(2)}) collective-permute-start(bf16[960,640]{1,0:T(8,128)(2,1)S(1)} %bitcast.52), channel_id=1, source_target_pairs={{0,1},{1,0},{2,3},{3,2},{4,5},{5,4},{6,7},{7,6},{8,9},{9,8},{10,11... | collective-permute-start | bytes 3686408 | tf_op jit(solution)/shard_map/ppermute | solution.py:378
  104.7 39.8 %collective-permute-start.14 = (bf16[960,640]{1,0:T(8,128)(2,1)S(1)}, bf16[960,640]{1,0:T(8,128)(2,1)}, u32[]{:S(2)}, u32[]{:S(2)}) collective-permute-start(bf16[960,640]{1,0:T(8,128)(2,1)S(1)} %bitcast.53), channel_id=1, source_target_pairs={{0,2},{1,3},{2,0},{3,1},{4,6},{5,7},{6,4},{7,5},{8,10},{9,11},{10,... | collective-permute-start | bytes 3686408 | tf_op jit(solution)/shard_map/ppermute | solution.py:378
  195.9 34.5 %collective-permute-start.23 = (bf16[512,5120]{1,0:T(8,128)(2,1)}, bf16[512,5120]{1,0:T(8,128)(2,1)S(1)}, u32[]{:S(2)}, u32[]{:S(2)}) collective-permute-start(bf16[512,5120]{1,0:T(8,128)(2,1)} %get-tuple-element.100), channel_id=1, source_target_pairs={{0,1},{1,0},{2,3},{3,2},{4,5},{5,4},{6,7},{7,6},{8,9},{9,8},{10,11... | collective-permute-start | bytes 15728648 | tf_op jit(solution)/shard_map/ppermute | solution.py:378
  196.0 30.5 %collective-permute-start.24 = (bf16[512,3584]{1,0:T(8,128)(2,1)}, bf16[512,3584]{1,0:T(8,128)(2,1)}, u32[]{:S(2)}, u32[]{:S(2)}) collective-permute-start(bf16[512,3584]{1,0:T(8,128)(2,1)} %get-tuple-element.102), channel_id=1, source_target_pairs={{0,1},{1,0},{2,3},{3,2},{4,5},{5,4},{6,7},{7,6},{8,9},{9,8},{10,11... | collective-permute-start | bytes 11010056 | tf_op jit(solution)/shard_map/ppermute | solution.py:378
  233.1 30.8 %collective-permute-start.25 = (bf16[256,2560]{1,0:T(8,128)(2,1)S(1)}, bf16[256,2560]{1,0:T(8,128)(2,1)S(1)}, u32[]{:S(2)}, u32[]{:S(2)}) collective-permute-start(bf16[256,2560]{1,0:T(8,128)(2,1)S(1)} %get-tuple-element.178), channel_id=1, source_target_pairs={{0,2},{1,3},{2,0},{3,1},{4,6},{5,7},{6,4},{7,5},{8,10},{9,11},{10,... | collective-permute-start | bytes 3932168 | tf_op jit(solution)/shard_map/ppermute | solution.py:378
  284.9 31.9 %collective-permute-start.32 = (bf16[256,2560]{1,0:T(8,128)(2,1)}, bf16[256,2560]{1,0:T(8,128)(2,1)S(1)}, u32[]{:S(2)}, u32[]{:S(2)}) collective-permute-start(bf16[256,2560]{1,0:T(8,128)(2,1)} %get-tuple-element.114), channel_id=1, source_target_pairs={{0,2},{1,3},{2,0},{3,1},{4,6},{5,7},{6,4},{7,5},{8,10},{9,11},{10,... | collective-permute-start | bytes 3932168 | tf_op jit(solution)/shard_map/ppermute | solution.py:378
  294.0 22.9 %collective-permute-start.31 = (bf16[2,2,128,640]{3,2,1,0:T(8,128)(2,1)}, bf16[2,2,128,640]{3,2,1,0:T(8,128)(2,1)}, u32[]{:S(2)}, u32[]{:S(2)}) collective-permute-start(bf16[2,2,128,640]{3,2,1,0:T(8,128)(2,1)} %add_convert_fusion.12), channel_id=1, source_target_pairs={{8,0},{16,8},{24,16},{28,24},{20,28},{12,20},{4,12},{0,4},{9,1},{1... | collective-permute-start | bytes 1966088 | tf_op jit(solution)/shard_map/ppermute | solution.py:859
  297.7 19.2 %collective-permute-start.30 = (bf16[2,2,128,640]{3,2,1,0:T(8,128)(2,1)}, bf16[2,2,128,640]{3,2,1,0:T(8,128)(2,1)}, u32[]{:S(2)}, u32[]{:S(2)}) collective-permute-start(bf16[2,2,128,640]{3,2,1,0:T(8,128)(2,1)} %add_convert_fusion.13), channel_id=1, source_target_pairs={{0,8},{8,16},{16,24},{24,28},{28,20},{20,12},{12,4},{4,0},{1,9},{9... | collective-permute-start | bytes 1966088 | tf_op jit(solution)/shard_map/ppermute | solution.py:858
  299.5 31.7 %collective-permute-start.38 = (bf16[256,1024]{1,0:T(8,128)(2,1)S(1)}, bf16[256,1024]{1,0:T(8,128)(2,1)}, u32[]{:S(2)}, u32[]{:S(2)}) collective-permute-start(bf16[256,1024]{1,0:T(8,128)(2,1)S(1)} %add_convert_fusion.15), channel_id=1, source_target_pairs={{0,2},{1,3},{2,0},{3,1},{4,6},{5,7},{6,4},{7,5},{8,10},{9,11},{10,... | collective-permute-start | bytes 1572872 | tf_op jit(solution)/shard_map/ppermute | solution.py:378
  319.4 16.4 %collective-permute-start.34 = (bf16[2,2,128,640]{3,2,1,0:T(8,128)(2,1)}, bf16[2,2,128,640]{3,2,1,0:T(8,128)(2,1)}, u32[]{:S(2)}, u32[]{:S(2)}) collective-permute-start(bf16[2,2,128,640]{3,2,1,0:T(8,128)(2,1)} %add_convert_fusion.10), channel_id=1, source_target_pairs={{8,0},{16,8},{24,16},{28,24},{20,28},{12,20},{4,12},{0,4},{9,1},{1... | collective-permute-start | bytes 1966088 | tf_op jit(solution)/shard_map/ppermute | solution.py:859
  322.4 18.0 %collective-permute-start.33 = (bf16[2,2,128,640]{3,2,1,0:T(8,128)(2,1)}, bf16[2,2,128,640]{3,2,1,0:T(8,128)(2,1)}, u32[]{:S(2)}, u32[]{:S(2)}) collective-permute-start(bf16[2,2,128,640]{3,2,1,0:T(8,128)(2,1)} %add_convert_fusion.11), channel_id=1, source_target_pairs={{0,8},{8,16},{16,24},{24,28},{28,20},{20,12},{12,4},{4,0},{1,9},{9... | collective-permute-start | bytes 1966088 | tf_op jit(solution)/shard_map/ppermute | solution.py:858
  327.8 38.6 %collective-permute-start.52 = (bf16[128,5120]{1,0:T(8,128)(2,1)}, bf16[128,5120]{1,0:T(8,128)(2,1)}, u32[]{:S(2)}, u32[]{:S(2)}) collective-permute-start(bf16[128,5120]{1,0:T(8,128)(2,1)} %fusion), channel_id=1, source_target_pairs={{0,4},{4,0},{8,12},{12,8},{16,20},{20,16},{24,28},{28,24},{1,5},{5... | collective-permute-start | bytes 3932168 | tf_op jit(solution)/shard_map/ppermute | solution.py:378
  332.9 43.3 %collective-permute-start.45 = (bf16[256,3584]{1,0:T(8,128)(2,1)}, bf16[256,3584]{1,0:T(8,128)(2,1)}, u32[]{:S(2)}, u32[]{:S(2)}) collective-permute-start(bf16[256,3584]{1,0:T(8,128)(2,1)} %add_convert_fusion.2), channel_id=1, source_target_pairs={{0,2},{1,3},{2,0},{3,1},{4,6},{5,7},{6,4},{7,5},{8,10},{9,11},{10,... | collective-permute-start | bytes 5505032 | tf_op jit(solution)/shard_map/ppermute | solution.py:378
  352.2 16.0 %collective-permute-start.35 = (bf16[512,768]{1,0:T(8,128)(2,1)}, bf16[512,768]{1,0:T(8,128)(2,1)}, u32[]{:S(2)}, u32[]{:S(2)}) collective-permute-start(bf16[512,768]{1,0:T(8,128)(2,1)} %get-tuple-element.121), channel_id=1, source_target_pairs={{0,1},{1,0},{2,3},{3,2},{4,5},{5,4},{6,7},{7,6},{8,9},{9,8},{10,11... | collective-permute-start | bytes 2359304 | tf_op jit(solution)/shard_map/ppermute | solution.py:378
  379.0 28.8 %collective-permute-start.46 = (bf16[128,3584]{1,0:T(8,128)(2,1)S(1)}, bf16[128,3584]{1,0:T(8,128)(2,1)S(1)}, u32[]{:S(2)}, u32[]{:S(2)}) collective-permute-start(bf16[128,3584]{1,0:T(8,128)(2,1)S(1)} %constant_dynamic-slice_fusion.4), channel_id=1, source_target_pairs={{0,4},{4,0},{8,12},{12,8},{16,20},{20,16},{24,28},{28,24},{1,5},{5... | collective-permute-start | bytes 2752520 | tf_op jit(solution)/shard_map/ppermute | solution.py:378
  385.3 20.7 %collective-permute-start.39 = (bf16[128,1792]{1,0:T(8,128)(2,1)S(1)}, bf16[128,1792]{1,0:T(8,128)(2,1)S(1)}, u32[]{:S(2)}, u32[]{:S(2)}) collective-permute-start(bf16[128,1792]{1,0:T(8,128)(2,1)S(1)} %fusion.3), channel_id=1, source_target_pairs={{0,4},{4,0},{8,12},{12,8},{16,20},{20,16},{24,28},{28,24},{1,5},{5... | collective-permute-start | bytes 1376264 | tf_op jit(solution)/shard_map/ppermute | solution.py:378
  397.8 23.3 %collective-permute-start.55 = (bf16[32,5120]{1,0:T(8,128)(2,1)S(1)}, bf16[32,5120]{1,0:T(8,128)(2,1)S(1)}, u32[]{:S(2)}, u32[]{:S(2)}) collective-permute-start(bf16[32,5120]{1,0:T(8,128)(2,1)S(1)} %add_convert_fusion.22), channel_id=1, source_target_pairs={{0,16},{4,20},{8,24},{12,28},{16,0},{20,4},{24,8},{28,12},{1,17},{... | collective-permute-start | bytes 983048 | tf_op jit(solution)/shard_map/ppermute | solution.py:378
  408.0 28.3 %collective-permute-start.47 = (bf16[64,3584]{1,0:T(8,128)(2,1)S(1)}, bf16[64,3584]{1,0:T(8,128)(2,1)S(1)}, u32[]{:S(2)}, u32[]{:S(2)}) collective-permute-start(bf16[64,3584]{1,0:T(8,128)(2,1)S(1)} %constant_dynamic-slice_fusion.3), channel_id=1, source_target_pairs={{0,8},{4,12},{8,0},{12,4},{16,24},{20,28},{24,16},{28,20},{1,9},{5... | collective-permute-start | bytes 1376264 | tf_op jit(solution)/shard_map/ppermute | solution.py:378
  428.6 27.6 %collective-permute-start.56 = (bf16[64,5120]{1,0:T(8,128)(2,1)S(1)}, bf16[64,5120]{1,0:T(8,128)(2,1)S(1)}, u32[]{:S(2)}, u32[]{:S(2)}) collective-permute-start(bf16[64,5120]{1,0:T(8,128)(2,1)S(1)} %pad_maximum_fusion.5), channel_id=1, source_target_pairs={{0,8},{4,12},{8,0},{12,4},{16,24},{20,28},{24,16},{28,20},{1,9},{5... | collective-permute-start | bytes 1966088 | tf_op jit(solution)/shard_map/ppermute | solution.py:378
  436.3 16.8 %collective-permute-start.43 = (bf16[64,1792]{1,0:T(8,128)(2,1)S(1)}, bf16[64,1792]{1,0:T(8,128)(2,1)S(1)}, u32[]{:S(2)}, u32[]{:S(2)}) collective-permute-start(bf16[64,1792]{1,0:T(8,128)(2,1)S(1)} %pad_maximum_fusion.10), channel_id=1, source_target_pairs={{0,8},{4,12},{8,0},{12,4},{16,24},{20,28},{24,16},{28,20},{1,9},{5... | collective-permute-start | bytes 688136 | tf_op jit(solution)/shard_map/ppermute | solution.py:378
  436.5 16.8 %collective-permute-start.48 = (bf16[32,3584]{1,0:T(8,128)(2,1)S(1)}, bf16[32,3584]{1,0:T(8,128)(2,1)S(1)}, u32[]{:S(2)}, u32[]{:S(2)}) collective-permute-start(bf16[32,3584]{1,0:T(8,128)(2,1)S(1)} %constant_dynamic-slice_fusion.2), channel_id=1, source_target_pairs={{0,16},{4,20},{8,24},{12,28},{16,0},{20,4},{24,8},{28,12},{1,17},{... | collective-permute-start | bytes 688136 | tf_op jit(solution)/shard_map/ppermute | solution.py:378
  457.5 36.9 %collective-permute-start.57 = (bf16[128,5120]{1,0:T(8,128)(2,1)}, bf16[128,5120]{1,0:T(8,128)(2,1)}, u32[]{:S(2)}, u32[]{:S(2)}) collective-permute-start(bf16[128,5120]{1,0:T(8,128)(2,1)} %pad_maximum_fusion), channel_id=1, source_target_pairs={{0,4},{4,0},{8,12},{12,8},{16,20},{20,16},{24,28},{28,24},{1,5},{5... | collective-permute-start | bytes 3932168 | tf_op jit(solution)/shard_map/ppermute | solution.py:378
  478.2 31.8 %collective-permute-start.51 = (bf16[128,3584]{1,0:T(8,128)(2,1)S(1)}, bf16[128,3584]{1,0:T(8,128)(2,1)S(1)}, u32[]{:S(2)}, u32[]{:S(2)}) collective-permute-start(bf16[128,3584]{1,0:T(8,128)(2,1)S(1)} %pad_maximum_fusion.2), channel_id=1, source_target_pairs={{0,4},{4,0},{8,12},{12,8},{16,20},{20,16},{24,28},{28,24},{1,5},{5... | collective-permute-start | bytes 2752520 | tf_op jit(solution)/shard_map/ppermute | solution.py:378
  (53 other events, 582.7 us)
